TPU v7x, 32 devices: a whole 2x2x4 slice. The times are simulated.
32 devices in a mesh: ctx: 16 (over z, y, core), head: 2 (over x).
Axes of the slice: x: 2, y: 2, z: 4, core: 2. Of those that a mesh axis runs over, the one named last changes fastest.
Arguments:
- query: bfloat16 [2048, 8192], P('ctx', 'head'), may hold values from -11 to 11
- key_in: bfloat16 [2048, 1024], P('ctx', 'head'), may hold values from -11 to 11
- value: bfloat16 [2048, 1024], P('ctx', 'head'), may hold values from -6 to 6
- grad_y: bfloat16 [2048, 8192], P('ctx', 'head'), may hold values from -6 to 6
- w_out: bfloat16 [8192, 8192], P('head', 'ctx'), may hold values from -0.0625 to 0.0625
- parent: int32 [16], replicated, may hold values from 1 to 15, as said below
Outputs:
- grad_query: bfloat16 [2048, 8192], P('ctx', 'head')
- grad_key: bfloat16 [2048, 1024], P('ctx', 'head')
- grad_value: bfloat16 [2048, 1024], P('ctx', 'head')
Inputs may be any that keep to these rules, and one draw needn't show every extreme that they name: The shared prefix is blocks 16 - 4 to 15: parent[15] = 15 and parent[b] = b + 1 for the other prefix blocks; the earlier blocks form particles of 4 consecutive blocks, in which each block's parent is the block after it, except a particle's last block, whose parent is a block of the shared prefix.
All inputs are finite; a program needn't handle non-finite values.
Results may differ from a plain program's by a relative error of at most 0.014.
Values may be sent and summed in bfloat16 or wider, within the bound.
No kernel may reach another device: no remote copies, remote signals or barrier semaphores. Data moves between devices by JAX's collectives and lax.ppermute only.
A program may use at most 192 MiB of HBM per device.

v0:
```python
import jax
import jax.numpy as jnp
from jax import lax
from jax.sharding import PartitionSpec as P

HPG = 8
DH = 128
BLOCK = 128


def shifted(value, axis, steps):
    count = lax.axis_size(axis)
    pairs = [(source, (source + steps) % count) for source in range(count)]
    return lax.ppermute(value, axis, pairs)


def ancestors(parent):
    count = parent.shape[0]
    index = jnp.arange(count, dtype=jnp.int32)
    start = (index[:, None] == index[None, :]).astype(jnp.int32)

    def advance(step, state):
        current, marks = state
        current = jnp.sum(jnp.where(current[:, None] == index[None, :], parent[None, :], 0), axis=1)
        marks = jnp.maximum(marks, (current[:, None] == index[None, :]).astype(jnp.int32))
        return (current, marks)

    return lax.fori_loop(0, count, advance, (index, start))[1]


def per_device(query, key_in, value, grad_y, w_out, parent):
    tokens_here = query.shape[0]
    groups = key_in.shape[1] // DH
    scale = DH ** (-0.5)
    cycle_size = lax.axis_size("ctx")
    place = lax.axis_index("ctx")
    full_rows = lax.all_gather(grad_y, "head", axis=1, tiled=True)
    grad_attn = lax.dot_general(
        full_rows,
        lax.all_gather(w_out, "ctx", axis=1, tiled=True),
        (((1,), (1,)), ((), ())),
        preferred_element_type=jnp.float32,
    ).astype(jnp.bfloat16)
    visible = ancestors(parent)
    block_count = parent.shape[0]
    blocks_here = tokens_here // BLOCK
    local_visible = lax.dynamic_slice_in_dim(visible, place * blocks_here, blocks_here, 0).astype(
        jnp.float32
    )
    query_pos = place * tokens_here + jnp.arange(tokens_here, dtype=jnp.int32)
    query_block = query_pos // BLOCK
    owned = place * blocks_here + jnp.arange(blocks_here, dtype=jnp.int32)
    query_select = (query_block[:, None] == owned[None, :]).astype(jnp.float32)
    query_visible = jnp.dot(query_select, local_visible)
    block_index = jnp.arange(block_count, dtype=jnp.int32)

    def make_mask(start, count):
        key_pos = start + jnp.arange(count, dtype=jnp.int32)
        key_block = key_pos // BLOCK
        key_select = (key_block[:, None] == block_index[None, :]).astype(jnp.float32)
        allowed = jnp.dot(query_visible, key_select.T) > 0.5
        return allowed & (
            (query_block[:, None] != key_block[None, :]) | (key_pos[None, :] <= query_pos[:, None])
        )

    query_heads = query.reshape(tokens_here, groups, HPG, DH).transpose(1, 2, 0, 3)
    grad_heads = grad_attn.reshape(tokens_here, groups, HPG, DH).transpose(1, 2, 0, 3)

    def split_heads(matrix):
        return matrix.reshape(matrix.shape[0], groups, DH).transpose(1, 0, 2)

    def join_heads(tensor):
        return tensor.transpose(1, 0, 2).reshape(tensor.shape[1], groups * DH)

    stat_shape = (groups, HPG, tokens_here)
    key_piece = lax.all_gather(key_in, "ctx", axis=0, tiled=True)
    value_piece = lax.all_gather(value, "ctx", axis=0, tiled=True)
    mask = make_mask(jnp.int32(0), key_piece.shape[0])
    statistics_top = jnp.full(stat_shape, -1e30, jnp.float32)
    scores = (
        jnp.einsum(
            "ghqd,gkd->ghqk",
            query_heads,
            split_heads(key_piece),
            preferred_element_type=jnp.float32,
        )
        * scale
    )
    masked = jnp.where(mask, scores, -1e30)
    new_top = jnp.maximum(statistics_top, jnp.max(masked, axis=3))
    weights = jnp.where(mask, jnp.exp(scores - new_top[..., None]), 0.0)
    dprob = jnp.einsum(
        "ghqd,gkd->ghqk", grad_heads, split_heads(value_piece), preferred_element_type=jnp.float32
    )
    statistics_norm = jnp.sum(weights, axis=3)
    weighted = jnp.sum(weights * dprob, axis=3)
    top, norm, weighted = (new_top, statistics_norm, weighted)
    delta = weighted / norm

    def contribution(key_piece, value_piece, mask):
        key_heads = split_heads(key_piece)
        value_heads = split_heads(value_piece)
        scores = (
            jnp.einsum("ghqd,gkd->ghqk", query_heads, key_heads, preferred_element_type=jnp.float32)
            * scale
        )
        prob = jnp.where(mask, jnp.exp(scores - top[..., None]), 0.0) / norm[..., None]
        dprob = jnp.einsum(
            "ghqd,gkd->ghqk", grad_heads, value_heads, preferred_element_type=jnp.float32
        )
        value_part = jnp.einsum(
            "ghqk,ghqd->gkd",
            prob.astype(jnp.bfloat16),
            grad_heads,
            preferred_element_type=jnp.float32,
        )
        dscore = (prob * (dprob - delta[..., None])).astype(jnp.bfloat16)
        query_part = (
            jnp.einsum("ghqk,gkd->ghqd", dscore, key_heads, preferred_element_type=jnp.float32)
            * scale
        )
        key_part = (
            jnp.einsum("ghqk,ghqd->gkd", dscore, query_heads, preferred_element_type=jnp.float32)
            * scale
        )
        return (query_part, join_heads(key_part), join_heads(value_part))

    def visit(key_piece, value_piece, start):
        mask = make_mask(start, key_piece.shape[0])
        return contribution(key_piece, value_piece, mask)

    grad_query = jnp.zeros((groups, HPG, tokens_here, DH), jnp.float32)

    def turn_one(step, state):
        grad_q, key_piece, value_piece, key_sum, value_sum = state
        owner = (place - step) % cycle_size
        query_part, key_part, value_part = visit(key_piece, value_piece, owner * tokens_here)
        grad_q = grad_q + query_part
        key_sum = key_sum + key_part
        value_sum = value_sum + value_part
        key_piece, value_piece = shifted((key_piece, value_piece), "ctx", 1)
        key_sum, value_sum = shifted((key_sum, value_sum), "ctx", 1)
        return (grad_q, key_piece, value_piece, key_sum, value_sum)

    zero_rows = jnp.zeros((tokens_here, groups * DH), jnp.float32)
    state = (grad_query, key_in, value, zero_rows, zero_rows)
    grad_query, unused_key, unused_value, grad_key, grad_value = lax.fori_loop(
        0, cycle_size, turn_one, state
    )
    grad_query = (
        grad_query.transpose(2, 0, 1, 3)
        .reshape(tokens_here, groups * HPG * DH)
        .astype(jnp.bfloat16)
    )
    return (grad_query, grad_key.astype(jnp.bfloat16), grad_value.astype(jnp.bfloat16))


def solution(mesh):
    placed = (
        P("ctx", "head"),
        P("ctx", "head"),
        P("ctx", "head"),
        P("ctx", "head"),
        P("head", "ctx"),
        P(),
    )
    return jax.shard_map(
        per_device,
        mesh=mesh,
        in_specs=placed,
        out_specs=(P("ctx", "head"), P("ctx", "head"), P("ctx", "head")),
        check_vma=False,
    )
```

profile of v0, /device:TPU:9, one launch (start us, length us, event | category | flops | bytes accessed | tf_op | source)
XLA Modules:
  0.0 817.8 jit_solution(5240799203652082542)
XLA Ops:
  15.3 4.3 while.40
  21.5 31.5 %all-gather.11.cloned.1.call-done = bf16[2048,512]{0,1:T(8,128)(2,1)} async-done(((bf16[128,512]{0,1:T(8,128)(2,1)}), bf16[2048,512]{0,1:T(8,128)(2,1)}) %all-gather.11.cloned.1.call-update) | async-done | bytes 2097168 | tf_op jit(solution)/shard_map/all_gather | solution.py:77
  53.0 4.0 copy.32
  56.9 38.9 %all-gather.5.cloned.1.call-done = bf16[2048,512]{0,1:T(8,128)(2,1)} async-done(((bf16[128,512]{0,1:T(8,128)(2,1)}), bf16[2048,512]{0,1:T(8,128)(2,1)}) %all-gather.5.cloned.1.call-update) | async-done | bytes 2097168 | tf_op jit(solution)/shard_map/all_gather | solution.py:76
  95.8 3.0 copy.28
  98.9 15.3 %select_reduce_fusion.1 = (f32[4,8,128]{2,1,0:T(8,128)S(1)}, f32[4,8,128,2048]{3,2,1,0:T(8,128)}) fusion(pred[128,2048]{1,0:T(8,128)(4,1)S(1)} %fusion.23, bf16[4,8,128,128]{2,3,1,0:T(8,128)(2,1)S(1)} %bitcast.136, bf16[2048,4,128]{2,0,1:T(8,128)(2,1)S(1)} %copy.28), kind=kOutput, calls=%fused_computation.43 | convolution fusion | flops 2172645376 | bytes 36978688 | tf_op jit(solution)/shard_map/ghqd,gkd->ghqk/dot_general | solution.py:81
  114.2 15.8 %fusion.22 = f32[4,8,128]{2,1,0:T(8,128)} fusion(f32[4,8,128,2048]{3,2,1,0:T(8,128)} %get-tuple-element.619, f32[4,8,128]{2,1,0:T(8,128)S(1)} %broadcast_maximum_fusion, pred[128,2048]{1,0:T(8,128)(4,1)S(1)} %fusion.23), kind=kLoop, calls=%fused_computation.44 | loop fusion | flops 33550336 | bytes 33849344 | tf_op jit(solution)/shard_map/reduce_sum | solution.py:95
  130.0 327.7 %all-gather.9.cloned.1.call-done = bf16[4096,8192]{1,0:T(8,128)(2,1)} async-done(((bf16[4096,512]{1,0:T(8,128)(2,1)}), bf16[4096,8192]{1,0:T(8,128)(2,1)}) %all-gather.9.cloned.1.call-update) | async-done | bytes 67108880 | tf_op jit(solution)/shard_map/all_gather | solution.py:40
  457.7 28.3 %convolution_convert_fusion = bf16[128,4096]{1,0:T(8,128)(2,1)S(1)} fusion(bf16[128,8192]{1,0:T(8,128)(2,1)} %all-gather.7.cloned.1.call-done, bf16[4096,8192]{1,0:T(8,128)(2,1)} %all-gather.9.cloned.1.call-done), kind=kOutput, calls=%fused_computation.45 | convolution fusion | flops 8590458880 | bytes 70254592 | tf_op jit(solution)/shard_map/dot_general | solution.py:38
  486.7 16.8 %multiply_reduce_fusion = f32[4,8,128]{2,1,0:T(8,128)S(1)} fusion(f32[4,8,128,2048]{3,2,1,0:T(8,128)} %get-tuple-element.619, bf16[4,8,128,128]{2,3,1,0:T(8,128)(2,1)S(1)} %bitcast.134, f32[4,8,128]{2,1,0:T(8,128)S(1)} %broadcast_maximum_fusion, pred[128,2048]{1,0:T(8,128)(4,1)S(1)} %fusion.23, bf16[2048,4,128]{2,0,1:T(8,128)(2,1)} %copy.32), kind=kOutput, calls=%fused_computation.41 | convolution fusion | flops 2189422592 | bytes 36995072 | tf_op jit(solution)/shard_map/ghqd,gkd->ghqk/dot_general | solution.py:92
  505.6 298.3 %while.41 = (s32[]{:T(128)}, f32[4,8,128,128]{3,2,1,0:T(8,128)}, bf16[128,512]{1,0:T(8,128)(2,1)}, bf16[128,512]{1,0:T(8,128)(2,1)S(1)}, f32[128,512]{0,1:T(8,12...) while((s32[]{:T(128)}, f32[4,8,128,128]{3,2,1,0:T(8,128)}, ...), condition=%wide.region_7.8_spmd.clone.clone.clone, body=%wide.region_6.7_spmd.clone.clone.clone.sunk | while | flops 677666816 | bytes 24106028 | solution.py:147
  536.1 3.3 select_add_fusion.2
  554.6 3.3 select_add_fusion.2
  572.4 3.3 select_add_fusion.2
  590.4 3.3 select_add_fusion.2
  604.5 3.4 collective-permute-start.2
  610.0 3.3 select_add_fusion.2
  629.0 3.3 select_add_fusion.2
  647.9 3.3 select_add_fusion.2
  662.1 2.7 collective-permute-start.2
  666.9 3.3 select_add_fusion.2
  685.9 3.3 select_add_fusion.2
  700.0 2.7 collective-permute-start.2
  704.8 3.3 select_add_fusion.2
  719.0 2.7 collective-permute-start.2
  723.8 3.3 select_add_fusion.2
  737.9 2.7 collective-permute-start.2
  742.8 3.3 select_add_fusion.2
  756.9 2.7 collective-permute-start.2
  761.7 3.3 select_add_fusion.2
  780.7 3.3 select_add_fusion.2
  799.6 3.3 select_add_fusion.2
  (401 shorter events, 254.8 us)
Async XLA Ops:
  7.2 45.8 %all-gather.11.cloned.1.call-start = ((), (), s32[]{:S(2)}) async-start(), calls=%async_computation.3 | async-start | bytes 2228224 | tf_op jit(solution)/shard_map/all_gather | solution.py:77
  10.5 85.4 %all-gather.5.cloned.1.call-start = ((), (), s32[]{:S(2)}) async-start(), calls=%async_computation | async-start | bytes 2228224 | tf_op jit(solution)/shard_map/all_gather | solution.py:76
  12.2 117.8 %all-gather.7.cloned.1.call-start = ((), (), s32[]{:S(2)}) async-start(), calls=%async_computation.1 | async-start | bytes 3145728 | tf_op jit(solution)/shard_map/all_gather | solution.py:37
  12.9 444.8 %all-gather.9.cloned.1.call-start = ((), (), s32[]{:S(2)}) async-start(), calls=%async_computation.2 | async-start | bytes 71303168 | tf_op jit(solution)/shard_map/all_gather | solution.py:40
  505.7 14.4 %collective-permute-start.1 = (bf16[128,512]{1,0:T(8,128)(2,1)S(1)}, bf16[128,512]{1,0:T(8,128)(2,1)S(1)}, u32[]{:S(2)}, u32[]{:S(2)}) collective-permute-start(bf16[128,512]{1,0:T(8,128)(2,1)S(1)} %copy.91), channel_id=1, source_target_pairs={{0,2},{2,4},{4,6},{6,8},{8,10},{10,12},{12,14},{14,16},{16,18},{18... | collective-permute-start | bytes 393224 | tf_op jit(solution)/shard_map/while/body/eval_jaxpr/ppermute | solution.py:14
  522.4 17.0 %collective-permute-start.1 = (bf16[128,512]{1,0:T(8,128)(2,1)S(1)}, bf16[128,512]{1,0:T(8,128)(2,1)S(1)}, u32[]{:S(2)}, u32[]{:S(2)}) collective-permute-start(bf16[128,512]{1,0:T(8,128)(2,1)S(1)} %copy.91), channel_id=1, source_target_pairs={{0,2},{2,4},{4,6},{6,8},{8,10},{10,12},{12,14},{14,16},{16,18},{18... | collective-permute-start | bytes 393224 | tf_op jit(solution)/shard_map/while/body/eval_jaxpr/ppermute | solution.py:14
  540.4 17.6 %collective-permute-start.1 = (bf16[128,512]{1,0:T(8,128)(2,1)S(1)}, bf16[128,512]{1,0:T(8,128)(2,1)S(1)}, u32[]{:S(2)}, u32[]{:S(2)}) collective-permute-start(bf16[128,512]{1,0:T(8,128)(2,1)S(1)} %copy.91), channel_id=1, source_target_pairs={{0,2},{2,4},{4,6},{6,8},{8,10},{10,12},{12,14},{14,16},{16,18},{18... | collective-permute-start | bytes 393224 | tf_op jit(solution)/shard_map/while/body/eval_jaxpr/ppermute | solution.py:14
  543.8 14.1 %collective-permute-start = (bf16[128,512]{1,0:T(8,128)(2,1)S(1)}, bf16[128,512]{1,0:T(8,128)(2,1)}, u32[]{:S(2)}, u32[]{:S(2)}) collective-permute-start(bf16[128,512]{1,0:T(8,128)(2,1)S(1)} %copy.90), channel_id=1, source_target_pairs={{0,2},{2,4},{4,6},{6,8},{8,10},{10,12},{12,14},{14,16},{16,18},{18... | collective-permute-start | bytes 393224 | tf_op jit(solution)/shard_map/while/body/eval_jaxpr/ppermute | solution.py:14
  558.9 16.8 %collective-permute-start.1 = (bf16[128,512]{1,0:T(8,128)(2,1)S(1)}, bf16[128,512]{1,0:T(8,128)(2,1)S(1)}, u32[]{:S(2)}, u32[]{:S(2)}) collective-permute-start(bf16[128,512]{1,0:T(8,128)(2,1)S(1)} %copy.91), channel_id=1, source_target_pairs={{0,2},{2,4},{4,6},{6,8},{8,10},{10,12},{12,14},{14,16},{16,18},{18... | collective-permute-start | bytes 393224 | tf_op jit(solution)/shard_map/while/body/eval_jaxpr/ppermute | solution.py:14
  576.7 17.0 %collective-permute-start.1 = (bf16[128,512]{1,0:T(8,128)(2,1)S(1)}, bf16[128,512]{1,0:T(8,128)(2,1)S(1)}, u32[]{:S(2)}, u32[]{:S(2)}) collective-permute-start(bf16[128,512]{1,0:T(8,128)(2,1)S(1)} %copy.91), channel_id=1, source_target_pairs={{0,2},{2,4},{4,6},{6,8},{8,10},{10,12},{12,14},{14,16},{16,18},{18... | collective-permute-start | bytes 393224 | tf_op jit(solution)/shard_map/while/body/eval_jaxpr/ppermute | solution.py:14
  594.5 18.9 %collective-permute-start.1 = (bf16[128,512]{1,0:T(8,128)(2,1)S(1)}, bf16[128,512]{1,0:T(8,128)(2,1)S(1)}, u32[]{:S(2)}, u32[]{:S(2)}) collective-permute-start(bf16[128,512]{1,0:T(8,128)(2,1)S(1)} %copy.91), channel_id=1, source_target_pairs={{0,2},{2,4},{4,6},{6,8},{8,10},{10,12},{12,14},{14,16},{16,18},{18... | collective-permute-start | bytes 393224 | tf_op jit(solution)/shard_map/while/body/eval_jaxpr/ppermute | solution.py:14
  597.9 15.5 %collective-permute-start = (bf16[128,512]{1,0:T(8,128)(2,1)S(1)}, bf16[128,512]{1,0:T(8,128)(2,1)}, u32[]{:S(2)}, u32[]{:S(2)}) collective-permute-start(bf16[128,512]{1,0:T(8,128)(2,1)S(1)} %copy.90), channel_id=1, source_target_pairs={{0,2},{2,4},{4,6},{6,8},{8,10},{10,12},{12,14},{14,16},{16,18},{18... | collective-permute-start | bytes 393224 | tf_op jit(solution)/shard_map/while/body/eval_jaxpr/ppermute | solution.py:14
  614.3 18.0 %collective-permute-start.1 = (bf16[128,512]{1,0:T(8,128)(2,1)S(1)}, bf16[128,512]{1,0:T(8,128)(2,1)S(1)}, u32[]{:S(2)}, u32[]{:S(2)}) collective-permute-start(bf16[128,512]{1,0:T(8,128)(2,1)S(1)} %copy.91), channel_id=1, source_target_pairs={{0,2},{2,4},{4,6},{6,8},{8,10},{10,12},{12,14},{14,16},{16,18},{18... | collective-permute-start | bytes 393224 | tf_op jit(solution)/shard_map/while/body/eval_jaxpr/ppermute | solution.py:14
  617.8 14.5 %collective-permute-start = (bf16[128,512]{1,0:T(8,128)(2,1)S(1)}, bf16[128,512]{1,0:T(8,128)(2,1)}, u32[]{:S(2)}, u32[]{:S(2)}) collective-permute-start(bf16[128,512]{1,0:T(8,128)(2,1)S(1)} %copy.90), channel_id=1, source_target_pairs={{0,2},{2,4},{4,6},{6,8},{8,10},{10,12},{12,14},{14,16},{16,18},{18... | collective-permute-start | bytes 393224 | tf_op jit(solution)/shard_map/while/body/eval_jaxpr/ppermute | solution.py:14
  633.3 18.0 %collective-permute-start.1 = (bf16[128,512]{1,0:T(8,128)(2,1)S(1)}, bf16[128,512]{1,0:T(8,128)(2,1)S(1)}, u32[]{:S(2)}, u32[]{:S(2)}) collective-permute-start(bf16[128,512]{1,0:T(8,128)(2,1)S(1)} %copy.91), channel_id=1, source_target_pairs={{0,2},{2,4},{4,6},{6,8},{8,10},{10,12},{12,14},{14,16},{16,18},{18... | collective-permute-start | bytes 393224 | tf_op jit(solution)/shard_map/while/body/eval_jaxpr/ppermute | solution.py:14
  636.7 14.5 %collective-permute-start = (bf16[128,512]{1,0:T(8,128)(2,1)S(1)}, bf16[128,512]{1,0:T(8,128)(2,1)}, u32[]{:S(2)}, u32[]{:S(2)}) collective-permute-start(bf16[128,512]{1,0:T(8,128)(2,1)S(1)} %copy.90), channel_id=1, source_target_pairs={{0,2},{2,4},{4,6},{6,8},{8,10},{10,12},{12,14},{14,16},{16,18},{18... | collective-permute-start | bytes 393224 | tf_op jit(solution)/shard_map/while/body/eval_jaxpr/ppermute | solution.py:14
  652.3 18.0 %collective-permute-start.1 = (bf16[128,512]{1,0:T(8,128)(2,1)S(1)}, bf16[128,512]{1,0:T(8,128)(2,1)S(1)}, u32[]{:S(2)}, u32[]{:S(2)}) collective-permute-start(bf16[128,512]{1,0:T(8,128)(2,1)S(1)} %copy.91), channel_id=1, source_target_pairs={{0,2},{2,4},{4,6},{6,8},{8,10},{10,12},{12,14},{14,16},{16,18},{18... | collective-permute-start | bytes 393224 | tf_op jit(solution)/shard_map/while/body/eval_jaxpr/ppermute | solution.py:14
  655.7 14.5 %collective-permute-start = (bf16[128,512]{1,0:T(8,128)(2,1)S(1)}, bf16[128,512]{1,0:T(8,128)(2,1)}, u32[]{:S(2)}, u32[]{:S(2)}) collective-permute-start(bf16[128,512]{1,0:T(8,128)(2,1)S(1)} %copy.90), channel_id=1, source_target_pairs={{0,2},{2,4},{4,6},{6,8},{8,10},{10,12},{12,14},{14,16},{16,18},{18... | collective-permute-start | bytes 393224 | tf_op jit(solution)/shard_map/while/body/eval_jaxpr/ppermute | solution.py:14
  671.2 18.0 %collective-permute-start.1 = (bf16[128,512]{1,0:T(8,128)(2,1)S(1)}, bf16[128,512]{1,0:T(8,128)(2,1)S(1)}, u32[]{:S(2)}, u32[]{:S(2)}) collective-permute-start(bf16[128,512]{1,0:T(8,128)(2,1)S(1)} %copy.91), channel_id=1, source_target_pairs={{0,2},{2,4},{4,6},{6,8},{8,10},{10,12},{12,14},{14,16},{16,18},{18... | collective-permute-start | bytes 393224 | tf_op jit(solution)/shard_map/while/body/eval_jaxpr/ppermute | solution.py:14
  674.7 14.5 %collective-permute-start = (bf16[128,512]{1,0:T(8,128)(2,1)S(1)}, bf16[128,512]{1,0:T(8,128)(2,1)}, u32[]{:S(2)}, u32[]{:S(2)}) collective-permute-start(bf16[128,512]{1,0:T(8,128)(2,1)S(1)} %copy.90), channel_id=1, source_target_pairs={{0,2},{2,4},{4,6},{6,8},{8,10},{10,12},{12,14},{14,16},{16,18},{18... | collective-permute-start | bytes 393224 | tf_op jit(solution)/shard_map/while/body/eval_jaxpr/ppermute | solution.py:14
  690.2 18.0 %collective-permute-start.1 = (bf16[128,512]{1,0:T(8,128)(2,1)S(1)}, bf16[128,512]{1,0:T(8,128)(2,1)S(1)}, u32[]{:S(2)}, u32[]{:S(2)}) collective-permute-start(bf16[128,512]{1,0:T(8,128)(2,1)S(1)} %copy.91), channel_id=1, source_target_pairs={{0,2},{2,4},{4,6},{6,8},{8,10},{10,12},{12,14},{14,16},{16,18},{18... | collective-permute-start | bytes 393224 | tf_op jit(solution)/shard_map/while/body/eval_jaxpr/ppermute | solution.py:14
  693.6 14.5 %collective-permute-start = (bf16[128,512]{1,0:T(8,128)(2,1)S(1)}, bf16[128,512]{1,0:T(8,128)(2,1)}, u32[]{:S(2)}, u32[]{:S(2)}) collective-permute-start(bf16[128,512]{1,0:T(8,128)(2,1)S(1)} %copy.90), channel_id=1, source_target_pairs={{0,2},{2,4},{4,6},{6,8},{8,10},{10,12},{12,14},{14,16},{16,18},{18... | collective-permute-start | bytes 393224 | tf_op jit(solution)/shard_map/while/body/eval_jaxpr/ppermute | solution.py:14
  709.1 18.0 %collective-permute-start.1 = (bf16[128,512]{1,0:T(8,128)(2,1)S(1)}, bf16[128,512]{1,0:T(8,128)(2,1)S(1)}, u32[]{:S(2)}, u32[]{:S(2)}) collective-permute-start(bf16[128,512]{1,0:T(8,128)(2,1)S(1)} %copy.91), channel_id=1, source_target_pairs={{0,2},{2,4},{4,6},{6,8},{8,10},{10,12},{12,14},{14,16},{16,18},{18... | collective-permute-start | bytes 393224 | tf_op jit(solution)/shard_map/while/body/eval_jaxpr/ppermute | solution.py:14
  712.6 14.5 %collective-permute-start = (bf16[128,512]{1,0:T(8,128)(2,1)S(1)}, bf16[128,512]{1,0:T(8,128)(2,1)}, u32[]{:S(2)}, u32[]{:S(2)}) collective-permute-start(bf16[128,512]{1,0:T(8,128)(2,1)S(1)} %copy.90), channel_id=1, source_target_pairs={{0,2},{2,4},{4,6},{6,8},{8,10},{10,12},{12,14},{14,16},{16,18},{18... | collective-permute-start | bytes 393224 | tf_op jit(solution)/shard_map/while/body/eval_jaxpr/ppermute | solution.py:14
  728.1 18.0 %collective-permute-start.1 = (bf16[128,512]{1,0:T(8,128)(2,1)S(1)}, bf16[128,512]{1,0:T(8,128)(2,1)S(1)}, u32[]{:S(2)}, u32[]{:S(2)}) collective-permute-start(bf16[128,512]{1,0:T(8,128)(2,1)S(1)} %copy.91), channel_id=1, source_target_pairs={{0,2},{2,4},{4,6},{6,8},{8,10},{10,12},{12,14},{14,16},{16,18},{18... | collective-permute-start | bytes 393224 | tf_op jit(solution)/shard_map/while/body/eval_jaxpr/ppermute | solution.py:14
  731.5 14.5 %collective-permute-start = (bf16[128,512]{1,0:T(8,128)(2,1)S(1)}, bf16[128,512]{1,0:T(8,128)(2,1)}, u32[]{:S(2)}, u32[]{:S(2)}) collective-permute-start(bf16[128,512]{1,0:T(8,128)(2,1)S(1)} %copy.90), channel_id=1, source_target_pairs={{0,2},{2,4},{4,6},{6,8},{8,10},{10,12},{12,14},{14,16},{16,18},{18... | collective-permute-start | bytes 393224 | tf_op jit(solution)/shard_map/while/body/eval_jaxpr/ppermute | solution.py:14
  747.1 18.0 %collective-permute-start.1 = (bf16[128,512]{1,0:T(8,128)(2,1)S(1)}, bf16[128,512]{1,0:T(8,128)(2,1)S(1)}, u32[]{:S(2)}, u32[]{:S(2)}) collective-permute-start(bf16[128,512]{1,0:T(8,128)(2,1)S(1)} %copy.91), channel_id=1, source_target_pairs={{0,2},{2,4},{4,6},{6,8},{8,10},{10,12},{12,14},{14,16},{16,18},{18... | collective-permute-start | bytes 393224 | tf_op jit(solution)/shard_map/while/body/eval_jaxpr/ppermute | solution.py:14
  750.5 14.5 %collective-permute-start = (bf16[128,512]{1,0:T(8,128)(2,1)S(1)}, bf16[128,512]{1,0:T(8,128)(2,1)}, u32[]{:S(2)}, u32[]{:S(2)}) collective-permute-start(bf16[128,512]{1,0:T(8,128)(2,1)S(1)} %copy.90), channel_id=1, source_target_pairs={{0,2},{2,4},{4,6},{6,8},{8,10},{10,12},{12,14},{14,16},{16,18},{18... | collective-permute-start | bytes 393224 | tf_op jit(solution)/shard_map/while/body/eval_jaxpr/ppermute | solution.py:14
  766.0 18.0 %collective-permute-start.1 = (bf16[128,512]{1,0:T(8,128)(2,1)S(1)}, bf16[128,512]{1,0:T(8,128)(2,1)S(1)}, u32[]{:S(2)}, u32[]{:S(2)}) collective-permute-start(bf16[128,512]{1,0:T(8,128)(2,1)S(1)} %copy.91), channel_id=1, source_target_pairs={{0,2},{2,4},{4,6},{6,8},{8,10},{10,12},{12,14},{14,16},{16,18},{18... | collective-permute-start | bytes 393224 | tf_op jit(solution)/shard_map/while/body/eval_jaxpr/ppermute | solution.py:14
  769.5 14.5 %collective-permute-start = (bf16[128,512]{1,0:T(8,128)(2,1)S(1)}, bf16[128,512]{1,0:T(8,128)(2,1)}, u32[]{:S(2)}, u32[]{:S(2)}) collective-permute-start(bf16[128,512]{1,0:T(8,128)(2,1)S(1)} %copy.90), channel_id=1, source_target_pairs={{0,2},{2,4},{4,6},{6,8},{8,10},{10,12},{12,14},{14,16},{16,18},{18... | collective-permute-start | bytes 393224 | tf_op jit(solution)/shard_map/while/body/eval_jaxpr/ppermute | solution.py:14
  785.0 18.0 %collective-permute-start.1 = (bf16[128,512]{1,0:T(8,128)(2,1)S(1)}, bf16[128,512]{1,0:T(8,128)(2,1)S(1)}, u32[]{:S(2)}, u32[]{:S(2)}) collective-permute-start(bf16[128,512]{1,0:T(8,128)(2,1)S(1)} %copy.91), channel_id=1, source_target_pairs={{0,2},{2,4},{4,6},{6,8},{8,10},{10,12},{12,14},{14,16},{16,18},{18... | collective-permute-start | bytes 393224 | tf_op jit(solution)/shard_map/while/body/eval_jaxpr/ppermute | solution.py:14
  788.4 14.5 %collective-permute-start = (bf16[128,512]{1,0:T(8,128)(2,1)S(1)}, bf16[128,512]{1,0:T(8,128)(2,1)}, u32[]{:S(2)}, u32[]{:S(2)}) collective-permute-start(bf16[128,512]{1,0:T(8,128)(2,1)S(1)} %copy.90), channel_id=1, source_target_pairs={{0,2},{2,4},{4,6},{6,8},{8,10},{10,12},{12,14},{14,16},{16,18},{18... | collective-permute-start | bytes 393224 | tf_op jit(solution)/shard_map/while/body/eval_jaxpr/ppermute | solution.py:14
  (39 other events, 623.8 us)
Sparse Core Ops, SparseCore 0:
  10.7 42.1 all-gather.10
  55.7 40.1 all-gather.4
  97.4 32.2 all-gather.6
  131.1 326.5 all-gather.8
where the time goes:
time: 828 us; the launch traced here: 818 us
  waiting for transfers between devices  416 us (50%)
  matrix products  192 us (23%)
  starting transfers between devices  79.7 us (10%)
  other arithmetic  77.4 us (9%)
  local copies, waits for them, and re-layouts  37.3 us (5%)
  between operations  13.9 us (2%)
    all_gather x1, waiting for transfers between devices, per_device(): lax.all_gather(w_out, 'ctx', axis=1, tiled=True)  328 us
    ppermute x64, starting transfers between devices, shifted(): return lax.ppermute(value, axis, pairs)  79.5 us
    dot_general x16, matrix products, contribution(): jnp.einsum('ghqk,gkd->ghqd', dscore, key_heads, preferred_element_type=jn...  51.6 us
    all_gather x1, waiting for transfers between devices, per_device(): key_piece = lax.all_gather(key_in, 'ctx', axis=0, tiled=True)  38.9 us
    dot_general x16, matrix products, contribution(): jnp.einsum('ghqd,gkd->ghqk', query_heads, key_heads, preferred_element_ty...  34.9 us
    all_gather x1, waiting for transfers between devices, per_device(): value_piece = lax.all_gather(value, 'ctx', axis=0, tiled=True)  31.5 us
    dot_general x1, matrix products, per_device(): lax.dot_general(full_rows, lax.all_gather(w_out, 'ctx', axis=1, tiled=Tru...  28.3 us
    add x16, other arithmetic, turn_one(): value_sum = value_sum + value_part  26.8 us
  transfers between devices with their start and end apart: 68, of which 19 were waited for; matrix products, arithmetic and copies ran while one was open for 30% of the time, Pallas kernels for 0%

commit v1 on v0

v1 whole, which is shorter than its diff:
```python
import functools

import jax
import jax.numpy as jnp
from jax import lax
from jax.experimental import pallas as pl
from jax.experimental.pallas import tpu as pltpu
from jax.sharding import PartitionSpec as P

DH = 128
BLOCK = 128
QUAD = 4
SCALE = DH ** (-0.5)
LOG2E = 1.4426950408889634
NT = (((1,), (1,)), ((), ()))


def project_kernel(place_ref, x_ref, *refs):
    w_refs, out_ref = refs[:-1], refs[-1]
    mine = place_ref[0]
    width = w_refs[0].shape[1]
    total = None
    for step, w_ref in enumerate(w_refs):
        columns = pl.ds(pl.multiple_of((mine ^ step) * width, width), width)
        term = lax.dot_general(x_ref[:, columns], w_ref[...], NT, preferred_element_type=jnp.float32)
        total = term if total is None else total + term
    out_ref[...] = total.astype(out_ref.dtype)


def project(place, x, pieces, dtype):
    rows, depth = x.shape
    columns, width = pieces[0].shape
    tile = min(256, columns)
    return pl.pallas_call(
        project_kernel,
        grid_spec=pltpu.PrefetchScalarGridSpec(
            num_scalar_prefetch=1,
            grid=(columns // tile,),
            in_specs=[pl.BlockSpec((rows, depth), lambda n, s: (0, 0))]
            + [pl.BlockSpec((tile, width), lambda n, s: (n, 0))] * len(pieces),
            out_specs=pl.BlockSpec((rows, tile), lambda n, s: (0, n)),
        ),
        out_shape=jax.ShapeDtypeStruct((rows, columns), dtype),
        compiler_params=pltpu.CompilerParams(vmem_limit_bytes=40 * 2**20),
        cost_estimate=pl.CostEstimate(
            flops=2 * rows * depth * columns,
            bytes_accessed=2 * (rows * depth + depth * columns + rows * columns),
            transcendentals=0,
        ),
    )(place, x, *pieces)


def attend_kernel(head_bits, place_ref, q_ref, k_ref, v_ref, kp_ref, vp_ref, *refs):
    part_refs, (gq_ref, dk_ref, dv_ref) = refs[:-9], refs[-9:-6]
    keys, values, keys_t, queries, grads, triangle = refs[-6:]
    mine, head_place, root = place_ref[0], place_ref[1], place_ref[2]
    own = QUAD * BLOCK
    half = own // 2
    pieces = 1 << head_bits
    piece = BLOCK // pieces

    @pl.when(pl.program_id(0) == 0)
    def first():
        for b in range(QUAD):
            rows = pl.ds(b * BLOCK, BLOCK)
            late = pl.ds(own + b * BLOCK, BLOCK)
            keys[rows, :] = k_ref[b ^ mine]
            values[rows, :] = v_ref[b ^ mine]
            keys[late, :] = kp_ref[b ^ mine]
            values[late, :] = vp_ref[b ^ mine]
        keys_t[...] = keys[...].astype(jnp.float32).T.astype(jnp.bfloat16)
        row = lax.broadcasted_iota(jnp.int32, (half, half), 0)
        col = lax.broadcasted_iota(jnp.int32, (half, half), 1)
        seen = (row // BLOCK > col // BLOCK) | ((row // BLOCK == col // BLOCK) & (row <= col))
        triangle[...] = jnp.where(seen, 0.0, -1e30)
        dk_ref[...] = jnp.zeros_like(dk_ref)
        dv_ref[...] = jnp.zeros_like(dv_ref)

    for b in range(QUAD):
        queries[pl.ds(b * BLOCK, BLOCK), :] = q_ref[b ^ mine]
        for i in range(pieces):
            at = (
                ((b >> 1) ^ (mine >> 1))
                | ((i ^ head_place) << 1)
                | (((b & 1) ^ (mine & 1)) << (1 + head_bits))
            )
            total = part_refs[0][at].astype(jnp.float32)
            for ref in part_refs[1:]:
                total = total + ref[at].astype(jnp.float32)
            grads[pl.ds(b * BLOCK + i * piece, piece), :] = total.astype(jnp.bfloat16)

    for pair in range(2):
        start = pair * half
        count = 2 * own - start
        q = queries[pl.ds(start, half), :]
        g = grads[pl.ds(start, half), :]
        rows = pl.ds(start, count)
        scores = lax.dot_general(keys[rows, :], q, NT, preferred_element_type=jnp.float32)
        late = lax.broadcasted_iota(jnp.int32, (own, half), 0) >= root * BLOCK
        parts = [scores[:half] + triangle[...]]
        if pair == 0:
            parts.append(scores[half : 2 * half])
        parts.append(jnp.where(late, scores[count - own :], -1e30))
        scores = jnp.concatenate(parts, axis=0)
        top = jnp.max(scores, axis=0, keepdims=True)
        weights = jnp.exp2((scores - top) * (SCALE * LOG2E))
        prob = weights * (1.0 / jnp.sum(weights, axis=0, keepdims=True))
        dprob = lax.dot_general(values[rows, :], g, NT, preferred_element_type=jnp.float32)
        delta = jnp.sum(prob * dprob, axis=0, keepdims=True)
        dscore = (prob * (dprob - delta)).astype(jnp.bfloat16)
        dv_ref[rows, :] += jnp.dot(prob.astype(jnp.bfloat16), g, preferred_element_type=jnp.float32)
        dk_ref[rows, :] += jnp.dot(dscore, q, preferred_element_type=jnp.float32) * SCALE
        gq = jnp.dot(keys_t[:, start:], dscore, preferred_element_type=jnp.float32) * SCALE
        gq = gq.T.astype(jnp.bfloat16)
        for b in range(QUAD // 2):
            gq_ref[(pair * (QUAD // 2) + b) ^ mine] = gq[b * BLOCK : (b + 1) * BLOCK]


def attend(place, qkv, prefix, partials, heads, head_bits):
    own = QUAD * BLOCK
    block = (QUAD, BLOCK, DH)

    def column(at):
        return pl.BlockSpec(block, lambda n, s: (0, 0, at))

    slots, piece, _ = partials[0].shape
    return pl.pallas_call(
        functools.partial(attend_kernel, head_bits),
        grid_spec=pltpu.PrefetchScalarGridSpec(
            num_scalar_prefetch=1,
            grid=(heads,),
            in_specs=[
                pl.BlockSpec(block, lambda n, s: (0, 0, n)),
                column(heads),
                column(heads + 1),
                column(0),
                column(1),
            ]
            + [pl.BlockSpec((slots, piece, DH), lambda n, s: (0, 0, n))] * len(partials),
            out_specs=[
                pl.BlockSpec(block, lambda n, s: (0, 0, n)),
                pl.BlockSpec((2 * own, DH), lambda n, s: (0, 0)),
                pl.BlockSpec((2 * own, DH), lambda n, s: (0, 0)),
            ],
            scratch_shapes=[
                pltpu.VMEM((2 * own, DH), jnp.bfloat16),
                pltpu.VMEM((2 * own, DH), jnp.bfloat16),
                pltpu.VMEM((DH, 2 * own), jnp.bfloat16),
                pltpu.VMEM((own, DH), jnp.bfloat16),
                pltpu.VMEM((own, DH), jnp.bfloat16),
                pltpu.VMEM((own // 2, own // 2), jnp.float32),
            ],
        ),
        out_shape=[
            jax.ShapeDtypeStruct((QUAD, BLOCK, heads * DH), jnp.bfloat16),
            jax.ShapeDtypeStruct((2 * own, DH), jnp.float32),
            jax.ShapeDtypeStruct((2 * own, DH), jnp.float32),
        ],
        compiler_params=pltpu.CompilerParams(vmem_limit_bytes=40 * 2**20),
        cost_estimate=pl.CostEstimate(
            flops=10 * own * 2 * own * DH * heads,
            bytes_accessed=16 * own * heads * DH,
            transcendentals=2 * own * own * heads,
        ),
    )(place, qkv, qkv, qkv, prefix, prefix, *partials)


def per_device(query, key_in, value, grad_y, w_out, parent):
    places, sides = lax.axis_size("ctx"), lax.axis_size("head")
    layers = places // QUAD
    head_bits = sides.bit_length() - 1
    place, side = lax.axis_index("ctx"), lax.axis_index("head")
    layer, mine = place // QUAD, place % QUAD
    tokens = query.shape[0]
    groups = key_in.shape[1] // DH
    heads = query.shape[1] // DH // QUAD
    depth = QUAD * w_out.shape[1]
    rows = w_out.shape[0] // QUAD

    def swap(x, bits):
        return lax.ppermute(x, "ctx", [(c, c ^ bits) for c in range(places)])

    def flip(x, bits):
        return lax.ppermute(x, "head", [(s, s ^ bits) for s in range(sides)])

    def rotate(x, steps):
        shift = steps * QUAD
        return lax.ppermute(x, "ctx", [(c, (c + shift) % places) for c in range(places)])

    def hop(x, sources, steps):
        pairs = [(s * QUAD + i, (s + steps) * QUAD + i) for s in sources for i in range(QUAD)]
        return lax.ppermute(x, "ctx", pairs)

    def columns(x, at, width):
        return lax.dynamic_slice_in_dim(x, at * width, width, 1)

    share = tokens // sides
    if sides == 2:
        held = lax.dynamic_slice_in_dim(grad_y, side * share, share, 0)
        other = flip(lax.dynamic_slice_in_dim(grad_y, (1 - side) * share, share, 0), 1)
        span = grad_y.shape[1] // depth

        def features(at):
            return jnp.where(
                at // span == side, columns(held, at % span, depth), columns(other, at % span, depth)
            )
    else:
        every = lax.all_to_all(grad_y, "head", 0, 1, tiled=True)

        def features(at):
            return columns(every, at, depth)

    pieces = []
    for step in range(QUAD):
        piece = lax.dynamic_slice_in_dim(w_out, (mine ^ step) * rows, rows, 0)
        pieces.append(swap(piece, step) if step else piece)

    arrived = []
    for step in range(QUAD):
        to = mine ^ step
        piece = jnp.concatenate(
            [
                columns(query, to, heads * DH),
                columns(key_in, to * groups // QUAD, DH),
                columns(value, to * groups // QUAD, DH),
            ],
            axis=1,
        )
        arrived.append(swap(piece, step) if step else piece)
    qkv = jnp.stack(arrived)

    prefix = qkv[:, :, heads * DH :]
    levels = layers.bit_length() - 1
    for level in reversed(range(levels)):
        span_of = 1 << level
        sources = [s for s in range(layers) if (layers - 1 - s) % (2 * span_of) == 0]
        landed = hop(prefix, sources, -span_of)
        prefix = jnp.where((layers - 1 - layer) % (2 * span_of) == span_of, landed, prefix)

    def gather(x):
        x = jnp.concatenate([x, swap(x, 2)], axis=0)
        for bit in range(head_bits):
            x = jnp.concatenate([x, flip(x, 1 << bit)], axis=0)
        return jnp.concatenate([x, swap(x, 1)], axis=0)

    scalars = mine.reshape(1).astype(jnp.int32)
    partials = []
    for steps in [0] + sorted(range(1, layers), key=lambda r: abs(2 * r - layers)):
        piece = features((layer - steps) % layers)
        if steps:
            piece = rotate(piece, -steps)
        everything = gather(piece)
        part = project(scalars, everything, pieces, jnp.bfloat16 if steps else jnp.float32)
        if steps:
            part = rotate(part, steps)
        partials.append(part.reshape(QUAD * sides, share, heads * DH))

    root = jnp.where(
        layer == layers - 1, QUAD, parent[layer * QUAD + QUAD - 1] - (parent.shape[0] - QUAD)
    )
    scalars = jnp.stack([mine, side, root]).astype(jnp.int32)
    grad_query, grad_key, grad_value = attend(scalars, qkv, prefix, partials, heads, head_bits)

    out_query = jnp.zeros(query.shape, query.dtype)
    for step in range(QUAD):
        piece = swap(grad_query[step], step) if step else grad_query[0]
        out_query = lax.dynamic_update_slice_in_dim(
            out_query, piece, (mine ^ step) * heads * DH, 1
        )

    own = QUAD * BLOCK
    both = jnp.concatenate([grad_key, grad_value], axis=1)
    far = both[own:]
    for level in range(levels):
        span_of = 1 << level
        sources = [s for s in range(layers) if (layers - 1 - s) % (2 * span_of) == span_of]
        far = far + hop(far.astype(jnp.bfloat16), sources, span_of).astype(jnp.float32)
    both = both[:own] + jnp.where(layer == layers - 1, far, 0.0)
    narrow = both.astype(jnp.bfloat16)
    held_groups = max(1, groups // QUAD)
    total_key = jnp.zeros(key_in.shape, jnp.float32)
    total_value = jnp.zeros(value.shape, jnp.float32)
    for step in range(QUAD):
        at = mine ^ step
        if step:
            piece = swap(lax.dynamic_slice_in_dim(narrow, at * BLOCK, BLOCK, 0), step)
        else:
            piece = lax.dynamic_slice_in_dim(both, at * BLOCK, BLOCK, 0)
        piece = piece.astype(jnp.float32)
        spot = (at * groups // QUAD) * DH

        def add(total, part):
            here = lax.dynamic_slice_in_dim(total, spot, held_groups * DH, 1)
            return lax.dynamic_update_slice_in_dim(total, here + part, spot, 1)

        total_key = add(total_key, piece[:, :DH])
        total_value = add(total_value, piece[:, DH:])
    return out_query, total_key.astype(jnp.bfloat16), total_value.astype(jnp.bfloat16)


def solution(mesh):
    placed = (
        P("ctx", "head"),
        P("ctx", "head"),
        P("ctx", "head"),
        P("ctx", "head"),
        P("head", "ctx"),
        P(),
    )
    return jax.shard_map(
        per_device,
        mesh=mesh,
        in_specs=placed,
        out_specs=(P("ctx", "head"), P("ctx", "head"), P("ctx", "head")),
        check_vma=False,
    )
```

time: 828 us -> 283 us (0.34); the launches traced: 818 us -> 282 us
  waiting for transfers between devices: 416 us -> 162 us
  matrix products: 192 us -> 0 us
  other arithmetic: 77.4 us -> 16.3 us
  Pallas kernels: 0 us -> 36.7 us
  local copies, waits for them, and re-layouts: 37.3 us -> 5.96 us
  starting transfers between devices: 79.7 us -> 59.4 us
  between operations: 13.9 us -> 1.97 us
    all_gather x4 -> x0, waiting for transfers between devices: 398 us -> none  [the longest x1 328 us: per_device(): lax.all_gather(w_out, 'ctx', axis=1, tiled=True)]
    dot_general x100 -> x0, matrix products: 192 us -> none  [the longest x16 51.6 us: contribution(): jnp.einsum('ghqk,gkd->ghqd', dscore, key_heads, preferred_element_type=jn...]
    ppermute x64 -> x35, waiting for transfers between devices: 16.6 us -> 162 us  [the longest x20 50 us: swap(): return lax.ppermute(x, 'ctx', [(c, c ^ bits) for c in range(places)])]
    add x32 -> x0, other arithmetic: 53.5 us -> none  [the longest x16 26.8 us: turn_one(): value_sum = value_sum + value_part]
    pallas_call x0 -> x5, Pallas kernels: none -> 36.7 us  [the longest x1 22.2 us: attend(): pl.pallas_call(functools.partial(attend_kernel, head_bits), grid_spec=plt...]
    ppermute x64 -> x35, starting transfers between devices: 79.5 us -> 59.4 us  [the longest x20 35.4 us: swap(): return lax.ppermute(x, 'ctx', [(c, c ^ bits) for c in range(places)])]
    reduce_sum x17 -> x0, other arithmetic: 18.8 us -> none  [the longest x1 15.8 us: per_device(): statistics_norm = jnp.sum(weights, axis=3)]
    while x50 -> x0, local copies, waits for them, and re-layouts: 18.1 us -> none
  transfers between devices with their start and end apart: 68 -> 35, of which waited for: 19 -> 17; matrix products, arithmetic and copies ran while one was open for 30% -> 6% of each run, Pallas kernels for 0% -> 5%
where the time goes in v1:
time: 283 us; the launch traced here: 282 us
  waiting for transfers between devices  162 us (57%)
  starting transfers between devices  59.4 us (21%)
  Pallas kernels  36.7 us (13%)
  other arithmetic  16.3 us (6%)
  local copies, waits for them, and re-layouts  5.96 us (2%)
    ppermute x20, waiting for transfers between devices, swap(): return lax.ppermute(x, 'ctx', [(c, c ^ bits) for c in range(places)])  50 us
    ppermute x6, waiting for transfers between devices, rotate(): lax.ppermute(x, 'ctx', [(c, (c + shift) % places) for c in range(places)])  46 us
    ppermute x4, waiting for transfers between devices, hop(): return lax.ppermute(x, 'ctx', pairs)  43.9 us
    ppermute x20, starting transfers between devices, swap(): return lax.ppermute(x, 'ctx', [(c, c ^ bits) for c in range(places)])  35.4 us
    pallas_call x1, Pallas kernels, attend(): pl.pallas_call(functools.partial(attend_kernel, head_bits), grid_spec=plt...  22.2 us
    ppermute x5, waiting for transfers between devices, flip(): return lax.ppermute(x, 'head', [(s, s ^ bits) for s in range(sides)])  21.8 us
    pallas_call x4, Pallas kernels, project(): pl.pallas_call(project_kernel, grid_spec=pltpu.PrefetchScalarGridSpec(num...  14.6 us
    ppermute x4, starting transfers between devices, hop(): return lax.ppermute(x, 'ctx', pairs)  10.6 us
  transfers between devices with their start and end apart: 35, of which 17 were waited for; matrix products, arithmetic and copies ran while one was open for 6% of the time, Pallas kernels for 5%

profile of v1, /device:TPU:9, one launch (start us, length us, event | category | flops | bytes accessed | tf_op | source)
XLA Modules:
  0.0 281.9 jit_solution(97042447597793018)
XLA Ops:
  4.4 10.3 %collective-permute-done.5 = bf16[64,4096]{1,0:T(8,128)(2,1)S(1)} collective-permute-done((bf16[64,4096]{1,0:T(8,128)(2,1)S(1)}, bf16[64,4096]{1,0:T(8,128)(2,1)S(1)}, u32[]{:S(2)}, u32[]{:S(2)}) %collective-permute-start.5) | collective-permute-done | bytes 524320 | tf_op jit(solution)/shard_map/ppermute | solution.py:184
  16.8 1.9 collective-permute-start
  18.9 2.3 collective-permute-start.12
  24.6 7.2 %collective-permute-done.17 = bf16[64,2048]{1,0:T(8,128)(2,1)S(1)} collective-permute-done((bf16[64,2048]{1,0:T(8,128)(2,1)S(1)}, bf16[64,2048]{1,0:T(8,128)(2,1)S(1)}, u32[]{:S(2)}, u32[]{:S(2)}) %collective-permute-start.17) | collective-permute-done | bytes 262176 | tf_op jit(solution)/shard_map/ppermute | solution.py:188
  33.4 4.9 %collective-permute-done.12 = bf16[64,2048]{1,0:T(8,128)(2,1)S(1)} collective-permute-done((bf16[64,2048]{1,0:T(8,128)(2,1)S(1)}, bf16[64,2048]{1,0:T(8,128)(2,1)S(1)}, u32[]{:S(2)}, u32[]{:S(2)}) %collective-permute-start.12) | collective-permute-done | bytes 262176 | tf_op jit(solution)/shard_map/ppermute | solution.py:188
  42.6 4.0 %collective-permute-done.13 = bf16[64,2048]{1,0:T(8,128)(2,1)S(1)} collective-permute-done((bf16[64,2048]{1,0:T(8,128)(2,1)S(1)}, bf16[64,2048]{1,0:T(8,128)(2,1)S(1)}, u32[]{:S(2)}, u32[]{:S(2)}) %collective-permute-start.13) | collective-permute-done | bytes 262176 | tf_op jit(solution)/shard_map/ppermute | solution.py:181
  50.7 8.7 %collective-permute-start.25 = (bf16[256,2048]{1,0:T(8,128)(2,1)}, bf16[256,2048]{1,0:T(8,128)(2,1)}, u32[]{:S(2)}, u32[]{:S(2)}) collective-permute-start(bf16[256,2048]{1,0:T(8,128)(2,1)} %pad_maximum_fusion.8), channel_id=1, source_target_pairs={{0,2},{2,0},{4,6},{6,4},{8,10},{10,8},{12,14},{14,12},{16,18},{18,... | collective-permute-start | bytes 3145736 | tf_op jit(solution)/shard_map/ppermute | solution.py:181
  61.1 10.9 %collective-permute-done.19 = bf16[128,2048]{1,0:T(8,128)(2,1)S(1)} collective-permute-done((bf16[128,2048]{1,0:T(8,128)(2,1)S(1)}, bf16[128,2048]{1,0:T(8,128)(2,1)S(1)}, u32[]{:S(2)}, u32[]{:S(2)}) %collective-permute-start.19) | collective-permute-done | bytes 524320 | tf_op jit(solution)/shard_map/ppermute | solution.py:184
  71.9 9.6 %collective-permute-start.2 = (bf16[128,1280]{1,0:T(8,128)(2,1)}, bf16[128,1280]{1,0:T(8,128)(2,1)}, u32[]{:S(2)}, u32[]{:S(2)}) collective-permute-start(bf16[128,1280]{1,0:T(8,128)(2,1)} %pad_maximum_fusion.15), channel_id=1, source_target_pairs={{0,6},{2,4},{4,2},{6,0},{8,14},{10,12},{12,10},{14,8},{16,22},{18,... | collective-permute-start | bytes 983048 | tf_op jit(solution)/shard_map/ppermute | solution.py:181
  81.6 1.8 constant_dynamic-slice_fusion.3
  84.0 6.2 %collective-permute-done.2 = bf16[128,1280]{1,0:T(8,128)(2,1)} collective-permute-done((bf16[128,1280]{1,0:T(8,128)(2,1)}, bf16[128,1280]{1,0:T(8,128)(2,1)}, u32[]{:S(2)}, u32[]{:S(2)}) %collective-permute-start.2) | collective-permute-done | bytes 327712 | tf_op jit(solution)/shard_map/ppermute | solution.py:181
  90.3 1.6 collective-permute-start.11
  92.7 1.5 pad_maximum_fusion.4.q_ref.k_ref.v_ref
  95.0 2.1 pad_maximum_fusion.5
  98.6 14.1 %collective-permute-done.10.refs_2_ = bf16[1024,512]{1,0:T(8,128)(2,1)S(1)} collective-permute-done((bf16[1024,512]{1,0:T(8,128)(2,1)}, bf16[1024,512]{1,0:T(8,128)(2,1)S(1)}, u32[]{:S(2)}, u32[]{:S(2)}) %collective-permute-start.10) | collective-permute-done | bytes 1048608 | tf_op jit(solution)/shard_map/ppermute | solution.py:181
  114.0 21.1 %collective-permute-done.11.refs_3_ = bf16[1024,512]{1,0:T(8,128)(2,1)S(1)} collective-permute-done((bf16[1024,512]{1,0:T(8,128)(2,1)S(1)}, bf16[1024,512]{1,0:T(8,128)(2,1)S(1)}, u32[]{:S(2)}, u32[]{:S(2)}) %collective-permute-start.11) | collective-permute-done | bytes 1048608 | tf_op jit(solution)/shard_map/ppermute | solution.py:181
  135.7 3.8 %shard_map.88 = bf16[512,1024]{1,0:T(8,128)(2,1)} custom-call(s32[1]{0:T(128)} %bitcast.place_ref, bf16[512,2048]{1,0:T(8,128)(2,1)S(1)} %pad_maximum_fusion.3.x_ref, bf16[1024,512]{1,0:T(8,128)(2,1)S(1)} %get-tuple-element.13.refs_0_, bf16[1024,512]{1,0:T(8,128)(2,1)S(1)} %collective-permute-done.9.refs_1_, ...), custom_call_target="tpu_custom_call" | custom-call | flops 2147483648 | bytes 7340032 | tf_op jit(solution)/shard_map/pallas_call | solution.py:34
  140.3 3.8 %shard_map.87 = bf16[512,1024]{1,0:T(8,128)(2,1)} custom-call(s32[1]{0:T(128)} %bitcast.place_ref, bf16[512,2048]{1,0:T(8,128)(2,1)S(1)} %pad_maximum_fusion.2.x_ref, bf16[1024,512]{1,0:T(8,128)(2,1)S(1)} %get-tuple-element.13.refs_0_, bf16[1024,512]{1,0:T(8,128)(2,1)S(1)} %collective-permute-done.9.refs_1_, ...), custom_call_target="tpu_custom_call" | custom-call | flops 2147483648 | bytes 7340032 | tf_op jit(solution)/shard_map/pallas_call | solution.py:34
  145.9 3.8 %shard_map.86 = bf16[512,1024]{1,0:T(8,128)(2,1)} custom-call(s32[1]{0:T(128)} %bitcast.place_ref, bf16[512,2048]{1,0:T(8,128)(2,1)S(1)} %pad_maximum_fusion.1.x_ref, bf16[1024,512]{1,0:T(8,128)(2,1)S(1)} %get-tuple-element.13.refs_0_, bf16[1024,512]{1,0:T(8,128)(2,1)S(1)} %collective-permute-done.9.refs_1_, ...), custom_call_target="tpu_custom_call" | custom-call | flops 2147483648 | bytes 7340032 | tf_op jit(solution)/shard_map/pallas_call | solution.py:34
  149.7 2.0 collective-permute-start.16
  152.4 3.3 %collective-permute-start.4 = (bf16[4,128,256]{2,1,0:T(8,128)(2,1)}, bf16[4,128,256]{2,1,0:T(8,128)(2,1)}, u32[]{:S(2)}, u32[]{:S(2)}) collective-permute-start(bf16[4,128,256]{2,1,0:T(8,128)(2,1)} %broadcast_select_fusion), channel_id=1, source_target_pairs={{8,0},{10,2},{12,4},{14,6},{24,16},{26,18},{28,20},{30,22},{9,1},{... | collective-permute-start | bytes 786440 | tf_op jit(solution)/shard_map/ppermute | solution.py:192
  157.1 35.1 %collective-permute-done.4 = bf16[4,128,256]{2,1,0:T(8,128)(2,1)} collective-permute-done((bf16[4,128,256]{2,1,0:T(8,128)(2,1)}, bf16[4,128,256]{2,1,0:T(8,128)(2,1)}, u32[]{:S(2)}, u32[]{:S(2)}) %collective-permute-start.4) | collective-permute-done | bytes 262176 | tf_op jit(solution)/shard_map/ppermute | solution.py:192
  193.2 1.9 pad_maximum_fusion.x_ref
  195.3 3.1 %shard_map.85 = f32[512,1024]{1,0:T(8,128)S(1)} custom-call(s32[1]{0:T(128)} %bitcast.place_ref, bf16[512,2048]{1,0:T(8,128)(2,1)S(1)} %pad_maximum_fusion.x_ref, bf16[1024,512]{1,0:T(8,128)(2,1)S(1)} %get-tuple-element.13.refs_0_, bf16[1024,512]{1,0:T(8,128)(2,1)S(1)} %copy-done.3, bf16[1024,512]{1,0:T(8,128)(2,1)S(1)} %collective-permute-done.10.refs_2_, ...), custom_call_target="tpu_custom_call" | custom-call | flops 2147483648 | bytes 7340032 | tf_op jit(solution)/shard_map/pallas_call | solution.py:34
  198.5 33.3 %collective-permute-done.16 = bf16[512,1024]{1,0:T(8,128)(2,1)} collective-permute-done((bf16[512,1024]{1,0:T(8,128)(2,1)}, bf16[512,1024]{1,0:T(8,128)(2,1)}, u32[]{:S(2)}, u32[]{:S(2)}) %collective-permute-start.16) | collective-permute-done | bytes 1048608 | tf_op jit(solution)/shard_map/ppermute | solution.py:188
  231.8 22.2 %shard_map.89 = (bf16[4,128,1024]{2,1,0:T(8,128)(2,1)S(1)}, f32[1024,128]{1,0:T(8,128)S(1)}, f32[1024,128]{1,0:T(8,128)S(1)}) custom-call(s32[3]{0:T(128)S(1)} %pad_add_fusion.place_ref, bf16[4,128,1280]{2,1,0:T(8,128)(2,1)S(1)} %pad_maximum_fusion.4.q_ref.k_ref.v_ref, bf16[4,128,1280]{2,1,0:T(8,128)(2,1)S(1)} %pad_maximum_fusion.4.q_ref.k_ref.v_ref, ...), custom_call_target="tpu_custom_call" | custom-call | flops 5368709120 | bytes 8388608 | tf_op jit(solution)/shard_map/pallas_call | solution.py:127
  257.9 5.8 %collective-permute-done.30 = bf16[512,256]{1,0:T(8,128)(2,1)S(1)} collective-permute-done((bf16[512,256]{1,0:T(8,128)(2,1)S(1)}, bf16[512,256]{1,0:T(8,128)(2,1)S(1)}, u32[]{:S(2)}, u32[]{:S(2)}) %collective-permute-start.30) | collective-permute-done | bytes 262176 | tf_op jit(solution)/shard_map/ppermute | solution.py:192
  263.8 4.8 %collective-permute-start.31 = (bf16[512,256]{1,0:T(8,128)(2,1)S(1)}, bf16[512,256]{1,0:T(8,128)(2,1)S(1)}, u32[]{:S(2)}, u32[]{:S(2)}) collective-permute-start(bf16[512,256]{1,0:T(8,128)(2,1)S(1)} %fusion), channel_id=1, source_target_pairs={{8,24},{10,26},{12,28},{14,30},{9,25},{11,27},{13,29},{15,31}} | collective-permute-start | bytes 786440 | tf_op jit(solution)/shard_map/ppermute | solution.py:192
  269.9 2.9 %collective-permute-done.31 = bf16[512,256]{1,0:T(8,128)(2,1)S(1)} collective-permute-done((bf16[512,256]{1,0:T(8,128)(2,1)S(1)}, bf16[512,256]{1,0:T(8,128)(2,1)S(1)}, u32[]{:S(2)}, u32[]{:S(2)}) %collective-permute-start.31) | collective-permute-done | bytes 262176 | tf_op jit(solution)/shard_map/ppermute | solution.py:192
  273.0 2.3 collective-permute-start.32
  277.2 1.8 collective-permute-done.33
  279.0 1.5 collective-permute-done.34
  (164 shorter events, 40.3 us)
Async XLA Ops:
  1.8 12.9 %collective-permute-start.5 = (bf16[64,4096]{1,0:T(8,128)(2,1)S(1)}, bf16[64,4096]{1,0:T(8,128)(2,1)S(1)}, u32[]{:S(2)}, u32[]{:S(2)}) collective-permute-start(bf16[64,4096]{1,0:T(8,128)(2,1)S(1)} %constant_dynamic-slice_fusion.7), channel_id=1, source_target_pairs={{0,1},{1,0},{2,3},{3,2},{4,5},{5,4},{6,7},{7,6},{8,9},{9,8},{10,11... | collective-permute-start | bytes 1572872 | tf_op jit(solution)/shard_map/ppermute | solution.py:184
  15.4 6.3 %collective-permute-start.22 = (bf16[64,2048]{1,0:T(8,128)(2,1)S(1)}, bf16[64,2048]{1,0:T(8,128)(2,1)S(1)}, u32[]{:S(2)}, u32[]{:S(2)}) collective-permute-start(bf16[64,2048]{1,0:T(8,128)(2,1)S(1)} %get-tuple-element.15), channel_id=1, source_target_pairs={{0,8},{2,10},{4,12},{6,14},{8,16},{10,18},{12,20},{14,22},{16,24},... | collective-permute-start | bytes 786440 | tf_op jit(solution)/shard_map/ppermute | solution.py:188
  16.8 43.3 %collective-permute-start = (bf16[128,1280]{1,0:T(8,128)(2,1)S(1)}, bf16[128,1280]{1,0:T(8,128)(2,1)S(1)}, u32[]{:S(2)}, u32[]{:S(2)}) collective-permute-start(bf16[128,1280]{1,0:T(8,128)(2,1)S(1)} %pad_maximum_fusion.13), channel_id=1, source_target_pairs={{0,2},{2,0},{4,6},{6,4},{8,10},{10,8},{12,14},{14,12},{16,18},{18,... | collective-permute-start | bytes 983048 | tf_op jit(solution)/shard_map/ppermute | solution.py:181
  18.7 13.2 %collective-permute-start.17 = (bf16[64,2048]{1,0:T(8,128)(2,1)S(1)}, bf16[64,2048]{1,0:T(8,128)(2,1)S(1)}, u32[]{:S(2)}, u32[]{:S(2)}) collective-permute-start(bf16[64,2048]{1,0:T(8,128)(2,1)S(1)} %get-tuple-element.16), channel_id=1, source_target_pairs={{0,24},{2,26},{4,28},{6,30},{8,0},{10,2},{12,4},{14,6},{16,8},{18,... | collective-permute-start | bytes 786440 | tf_op jit(solution)/shard_map/ppermute | solution.py:188
  18.9 19.4 %collective-permute-start.12 = (bf16[64,2048]{1,0:T(8,128)(2,1)S(1)}, bf16[64,2048]{1,0:T(8,128)(2,1)S(1)}, u32[]{:S(2)}, u32[]{:S(2)}) collective-permute-start(bf16[64,2048]{1,0:T(8,128)(2,1)S(1)} %get-tuple-element.17), channel_id=1, source_target_pairs={{0,16},{2,18},{4,20},{6,22},{8,24},{10,26},{12,28},{14,30},{16,0},... | collective-permute-start | bytes 786440 | tf_op jit(solution)/shard_map/ppermute | solution.py:188
  21.7 17.9 %collective-permute-start.23 = (bf16[64,2048]{1,0:T(8,128)(2,1)S(1)}, bf16[64,2048]{1,0:T(8,128)(2,1)S(1)}, u32[]{:S(2)}, u32[]{:S(2)}) collective-permute-start(bf16[64,2048]{1,0:T(8,128)(2,1)S(1)} %collective-permute-done.22), channel_id=1, source_target_pairs={{0,4},{2,6},{4,0},{6,2},{8,12},{10,14},{12,8},{14,10},{16,20},{18,... | collective-permute-start | bytes 786440 | tf_op jit(solution)/shard_map/ppermute | solution.py:181
  23.7 17.2 %collective-permute-start.6 = (bf16[64,2048]{1,0:T(8,128)(2,1)S(1)}, bf16[64,2048]{1,0:T(8,128)(2,1)S(1)}, u32[]{:S(2)}, u32[]{:S(2)}) collective-permute-start(bf16[64,2048]{1,0:T(8,128)(2,1)S(1)} %get-tuple-element.18), channel_id=1, source_target_pairs={{0,4},{2,6},{4,0},{6,2},{8,12},{10,14},{12,8},{14,10},{16,20},{18,... | collective-permute-start | bytes 786440 | tf_op jit(solution)/shard_map/ppermute | solution.py:181
  31.9 9.4 %collective-permute-start.18 = (bf16[64,2048]{1,0:T(8,128)(2,1)S(1)}, bf16[64,2048]{1,0:T(8,128)(2,1)S(1)}, u32[]{:S(2)}, u32[]{:S(2)}) collective-permute-start(bf16[64,2048]{1,0:T(8,128)(2,1)S(1)} %collective-permute-done.17), channel_id=1, source_target_pairs={{0,4},{2,6},{4,0},{6,2},{8,12},{10,14},{12,8},{14,10},{16,20},{18,... | collective-permute-start | bytes 786440 | tf_op jit(solution)/shard_map/ppermute | solution.py:181
  38.2 8.4 %collective-permute-start.13 = (bf16[64,2048]{1,0:T(8,128)(2,1)S(1)}, bf16[64,2048]{1,0:T(8,128)(2,1)S(1)}, u32[]{:S(2)}, u32[]{:S(2)}) collective-permute-start(bf16[64,2048]{1,0:T(8,128)(2,1)S(1)} %collective-permute-done.12), channel_id=1, source_target_pairs={{0,4},{2,6},{4,0},{6,2},{8,12},{10,14},{12,8},{14,10},{16,20},{18,... | collective-permute-start | bytes 786440 | tf_op jit(solution)/shard_map/ppermute | solution.py:181
  39.6 9.9 %collective-permute-start.24 = (bf16[128,2048]{1,0:T(8,128)(2,1)S(1)}, bf16[128,2048]{1,0:T(8,128)(2,1)S(1)}, u32[]{:S(2)}, u32[]{:S(2)}) collective-permute-start(bf16[128,2048]{1,0:T(8,128)(2,1)S(1)} %pad_maximum_fusion.12), channel_id=1, source_target_pairs={{0,1},{1,0},{2,3},{3,2},{4,5},{5,4},{6,7},{7,6},{8,9},{9,8},{10,11... | collective-permute-start | bytes 1572872 | tf_op jit(solution)/shard_map/ppermute | solution.py:184
  40.9 50.9 %collective-permute-start.7 = (bf16[128,2048]{1,0:T(8,128)(2,1)S(1)}, bf16[128,2048]{1,0:T(8,128)(2,1)}, u32[]{:S(2)}, u32[]{:S(2)}) collective-permute-start(bf16[128,2048]{1,0:T(8,128)(2,1)S(1)} %pad_maximum_fusion.9), channel_id=1, source_target_pairs={{0,1},{1,0},{2,3},{3,2},{4,5},{5,4},{6,7},{7,6},{8,9},{9,8},{10,11... | collective-permute-start | bytes 1572872 | tf_op jit(solution)/shard_map/ppermute | solution.py:184
  41.3 30.6 %collective-permute-start.19 = (bf16[128,2048]{1,0:T(8,128)(2,1)S(1)}, bf16[128,2048]{1,0:T(8,128)(2,1)S(1)}, u32[]{:S(2)}, u32[]{:S(2)}) collective-permute-start(bf16[128,2048]{1,0:T(8,128)(2,1)S(1)} %pad_maximum_fusion.11), channel_id=1, source_target_pairs={{0,1},{1,0},{2,3},{3,2},{4,5},{5,4},{6,7},{7,6},{8,9},{9,8},{10,11... | collective-permute-start | bytes 1572872 | tf_op jit(solution)/shard_map/ppermute | solution.py:184
  47.5 44.3 %collective-permute-start.14 = (bf16[128,2048]{1,0:T(8,128)(2,1)}, bf16[128,2048]{1,0:T(8,128)(2,1)S(1)}, u32[]{:S(2)}, u32[]{:S(2)}) collective-permute-start(bf16[128,2048]{1,0:T(8,128)(2,1)} %pad_maximum_fusion.10), channel_id=1, source_target_pairs={{0,1},{1,0},{2,3},{3,2},{4,5},{5,4},{6,7},{7,6},{8,9},{9,8},{10,11... | collective-permute-start | bytes 1572872 | tf_op jit(solution)/shard_map/ppermute | solution.py:184
  50.7 43.7 %collective-permute-start.25 = (bf16[256,2048]{1,0:T(8,128)(2,1)}, bf16[256,2048]{1,0:T(8,128)(2,1)}, u32[]{:S(2)}, u32[]{:S(2)}) collective-permute-start(bf16[256,2048]{1,0:T(8,128)(2,1)} %pad_maximum_fusion.8), channel_id=1, source_target_pairs={{0,2},{2,0},{4,6},{6,4},{8,10},{10,8},{12,14},{14,12},{16,18},{18,... | collective-permute-start | bytes 3145736 | tf_op jit(solution)/shard_map/ppermute | solution.py:181
  60.1 23.4 %collective-permute-start.1 = (bf16[128,1280]{1,0:T(8,128)(2,1)}, bf16[128,1280]{1,0:T(8,128)(2,1)}, u32[]{:S(2)}, u32[]{:S(2)}) collective-permute-start(bf16[128,1280]{1,0:T(8,128)(2,1)} %pad_maximum_fusion.14), channel_id=1, source_target_pairs={{0,4},{2,6},{4,0},{6,2},{8,12},{10,14},{12,8},{14,10},{16,20},{18,... | collective-permute-start | bytes 983048 | tf_op jit(solution)/shard_map/ppermute | solution.py:181
  71.9 18.3 %collective-permute-start.2 = (bf16[128,1280]{1,0:T(8,128)(2,1)}, bf16[128,1280]{1,0:T(8,128)(2,1)}, u32[]{:S(2)}, u32[]{:S(2)}) collective-permute-start(bf16[128,1280]{1,0:T(8,128)(2,1)} %pad_maximum_fusion.15), channel_id=1, source_target_pairs={{0,6},{2,4},{4,2},{6,0},{8,14},{10,12},{12,10},{14,8},{16,22},{18,... | collective-permute-start | bytes 983048 | tf_op jit(solution)/shard_map/ppermute | solution.py:181
  83.5 29.2 %collective-permute-start.10 = (bf16[1024,512]{1,0:T(8,128)(2,1)}, bf16[1024,512]{1,0:T(8,128)(2,1)S(1)}, u32[]{:S(2)}, u32[]{:S(2)}) collective-permute-start(bf16[1024,512]{1,0:T(8,128)(2,1)} %get-tuple-element.14), channel_id=1, source_target_pairs={{0,4},{2,6},{4,0},{6,2},{8,12},{10,14},{12,8},{14,10},{16,20},{18,... | collective-permute-start | bytes 3145736 | tf_op jit(solution)/shard_map/ppermute | solution.py:181
  90.3 44.8 %collective-permute-start.11 = (bf16[1024,512]{1,0:T(8,128)(2,1)S(1)}, bf16[1024,512]{1,0:T(8,128)(2,1)S(1)}, u32[]{:S(2)}, u32[]{:S(2)}) collective-permute-start(bf16[1024,512]{1,0:T(8,128)(2,1)S(1)} %copy-done.29), channel_id=1, source_target_pairs={{0,6},{2,4},{4,2},{6,0},{8,14},{10,12},{12,10},{14,8},{16,22},{18,... | collective-permute-start | bytes 3145736 | tf_op jit(solution)/shard_map/ppermute | solution.py:181
  91.8 43.8 %collective-permute-start.9 = (bf16[1024,512]{1,0:T(8,128)(2,1)S(1)}, bf16[1024,512]{1,0:T(8,128)(2,1)S(1)}, u32[]{:S(2)}, u32[]{:S(2)}) collective-permute-start(bf16[1024,512]{1,0:T(8,128)(2,1)S(1)} %copy-done.28), channel_id=1, source_target_pairs={{0,2},{2,0},{4,6},{6,4},{8,10},{10,8},{12,14},{14,12},{16,18},{18,... | collective-permute-start | bytes 3145736 | tf_op jit(solution)/shard_map/ppermute | solution.py:181
  91.9 48.2 %collective-permute-start.20 = (bf16[256,2048]{1,0:T(8,128)(2,1)S(1)}, bf16[256,2048]{1,0:T(8,128)(2,1)S(1)}, u32[]{:S(2)}, u32[]{:S(2)}) collective-permute-start(bf16[256,2048]{1,0:T(8,128)(2,1)S(1)} %pad_maximum_fusion.7), channel_id=1, source_target_pairs={{0,2},{2,0},{4,6},{6,4},{8,10},{10,8},{12,14},{14,12},{16,18},{18,... | collective-permute-start | bytes 3145736 | tf_op jit(solution)/shard_map/ppermute | solution.py:181
  94.4 51.3 %collective-permute-start.15 = (bf16[256,2048]{1,0:T(8,128)(2,1)S(1)}, bf16[256,2048]{1,0:T(8,128)(2,1)S(1)}, u32[]{:S(2)}, u32[]{:S(2)}) collective-permute-start(bf16[256,2048]{1,0:T(8,128)(2,1)S(1)} %pad_maximum_fusion.6), channel_id=1, source_target_pairs={{0,2},{2,0},{4,6},{6,4},{8,10},{10,8},{12,14},{14,12},{16,18},{18,... | collective-permute-start | bytes 3145736 | tf_op jit(solution)/shard_map/ppermute | solution.py:181
  112.7 39.0 %collective-permute-start.3 = (bf16[4,128,256]{2,1,0:T(8,128)(2,1)S(1)}, bf16[4,128,256]{2,1,0:T(8,128)(2,1)S(1)}, u32[]{:S(2)}, u32[]{:S(2)}) collective-permute-start(bf16[4,128,256]{2,1,0:T(8,128)(2,1)S(1)} %slice.60), channel_id=1, source_target_pairs={{24,8},{26,10},{28,12},{30,14},{25,9},{27,11},{29,13},{31,15}} | collective-permute-start | bytes 786440 | tf_op jit(solution)/shard_map/ppermute | solution.py:192
  135.1 58.1 %collective-permute-start.8 = (bf16[256,2048]{1,0:T(8,128)(2,1)}, bf16[256,2048]{1,0:T(8,128)(2,1)}, u32[]{:S(2)}, u32[]{:S(2)}) collective-permute-start(bf16[256,2048]{1,0:T(8,128)(2,1)} %pad_maximum_fusion.5), channel_id=1, source_target_pairs={{0,2},{2,0},{4,6},{6,4},{8,10},{10,8},{12,14},{14,12},{16,18},{18,... | collective-permute-start | bytes 3145736 | tf_op jit(solution)/shard_map/ppermute | solution.py:181
  139.5 59.0 %collective-permute-start.26 = (bf16[512,1024]{1,0:T(8,128)(2,1)}, bf16[512,1024]{1,0:T(8,128)(2,1)}, u32[]{:S(2)}, u32[]{:S(2)}) collective-permute-start(bf16[512,1024]{1,0:T(8,128)(2,1)} %shard_map.88), channel_id=1, source_target_pairs={{0,24},{2,26},{4,28},{6,30},{8,0},{10,2},{12,4},{14,6},{16,8},{18,... | collective-permute-start | bytes 3145736 | tf_op jit(solution)/shard_map/ppermute | solution.py:188
  144.2 54.3 %collective-permute-start.21 = (bf16[512,1024]{1,0:T(8,128)(2,1)}, bf16[512,1024]{1,0:T(8,128)(2,1)}, u32[]{:S(2)}, u32[]{:S(2)}) collective-permute-start(bf16[512,1024]{1,0:T(8,128)(2,1)} %shard_map.87), channel_id=1, source_target_pairs={{0,8},{2,10},{4,12},{6,14},{8,16},{10,18},{12,20},{14,22},{16,24},... | collective-permute-start | bytes 3145736 | tf_op jit(solution)/shard_map/ppermute | solution.py:188
  149.7 82.1 %collective-permute-start.16 = (bf16[512,1024]{1,0:T(8,128)(2,1)}, bf16[512,1024]{1,0:T(8,128)(2,1)}, u32[]{:S(2)}, u32[]{:S(2)}) collective-permute-start(bf16[512,1024]{1,0:T(8,128)(2,1)} %shard_map.86), channel_id=1, source_target_pairs={{0,16},{2,18},{4,20},{6,22},{8,24},{10,26},{12,28},{14,30},{16,0},... | collective-permute-start | bytes 3145736 | tf_op jit(solution)/shard_map/ppermute | solution.py:188
  152.4 39.7 %collective-permute-start.4 = (bf16[4,128,256]{2,1,0:T(8,128)(2,1)}, bf16[4,128,256]{2,1,0:T(8,128)(2,1)}, u32[]{:S(2)}, u32[]{:S(2)}) collective-permute-start(bf16[4,128,256]{2,1,0:T(8,128)(2,1)} %broadcast_select_fusion), channel_id=1, source_target_pairs={{8,0},{10,2},{12,4},{14,6},{24,16},{26,18},{28,20},{30,22},{9,1},{... | collective-permute-start | bytes 786440 | tf_op jit(solution)/shard_map/ppermute | solution.py:192
  254.1 9.6 %collective-permute-start.30 = (bf16[512,256]{1,0:T(8,128)(2,1)S(1)}, bf16[512,256]{1,0:T(8,128)(2,1)S(1)}, u32[]{:S(2)}, u32[]{:S(2)}) collective-permute-start(bf16[512,256]{1,0:T(8,128)(2,1)S(1)} %slice.99), channel_id=1, source_target_pairs={{0,8},{2,10},{4,12},{6,14},{16,24},{18,26},{20,28},{22,30},{1,9},{... | collective-permute-start | bytes 786440 | tf_op jit(solution)/shard_map/ppermute | solution.py:192
  255.5 13.1 %collective-permute-start.27 = (bf16[128,1024]{1,0:T(8,128)(2,1)S(1)}, bf16[128,1024]{1,0:T(8,128)(2,1)S(1)}, u32[]{:S(2)}, u32[]{:S(2)}) collective-permute-start(bf16[128,1024]{1,0:T(8,128)(2,1)S(1)} %get-tuple-element.21), channel_id=1, source_target_pairs={{0,2},{2,0},{4,6},{6,4},{8,10},{10,8},{12,14},{14,12},{16,18},{18,... | collective-permute-start | bytes 786440 | tf_op jit(solution)/shard_map/ppermute | solution.py:181
  256.1 12.5 %collective-permute-start.28 = (bf16[128,1024]{1,0:T(8,128)(2,1)S(1)}, bf16[128,1024]{1,0:T(8,128)(2,1)S(1)}, u32[]{:S(2)}, u32[]{:S(2)}) collective-permute-start(bf16[128,1024]{1,0:T(8,128)(2,1)S(1)} %get-tuple-element.20), channel_id=1, source_target_pairs={{0,4},{2,6},{4,0},{6,2},{8,12},{10,14},{12,8},{14,10},{16,20},{18,... | collective-permute-start | bytes 786440 | tf_op jit(solution)/shard_map/ppermute | solution.py:181
  257.3 12.6 %collective-permute-start.29 = (bf16[128,1024]{1,0:T(8,128)(2,1)S(1)}, bf16[128,1024]{1,0:T(8,128)(2,1)S(1)}, u32[]{:S(2)}, u32[]{:S(2)}) collective-permute-start(bf16[128,1024]{1,0:T(8,128)(2,1)S(1)} %get-tuple-element.19), channel_id=1, source_target_pairs={{0,6},{2,4},{4,2},{6,0},{8,14},{10,12},{12,10},{14,8},{16,22},{18,... | collective-permute-start | bytes 786440 | tf_op jit(solution)/shard_map/ppermute | solution.py:181
  263.8 9.1 %collective-permute-start.31 = (bf16[512,256]{1,0:T(8,128)(2,1)S(1)}, bf16[512,256]{1,0:T(8,128)(2,1)S(1)}, u32[]{:S(2)}, u32[]{:S(2)}) collective-permute-start(bf16[512,256]{1,0:T(8,128)(2,1)S(1)} %fusion), channel_id=1, source_target_pairs={{8,24},{10,26},{12,28},{14,30},{9,25},{11,27},{13,29},{15,31}} | collective-permute-start | bytes 786440 | tf_op jit(solution)/shard_map/ppermute | solution.py:192
  (38 other events, 458.8 us)

commit v2 on v1

v2 whole, which is shorter than its diff:
```python
import functools

import jax
import jax.numpy as jnp
from jax import lax
from jax.experimental import pallas as pl
from jax.experimental.pallas import tpu as pltpu
from jax.sharding import PartitionSpec as P

OPT = {'vmem': 16, 'cp': 1.0, 'cs': 1.0, 'ca': 1.0, 'cf': 1, 'dual': [0, 0, 0, 1], 'z0': 0, 'merged': 1, 'home': 1, 'cut': 4, 'ties': {'y1:s': ['r3', 'W0a', 'xe2'], 'x3:s': ['r1', 'W0a', 'xe2'], 'r2:s': ['r1', 'r3'], 'k1:s': ['r1'], 'k2:s': ['r1'], 'k3:s': ['r1'], 'W1b:s': ['r1'], 'x1:s': ['x3'], 'y3:s': ['y1'], 'c1:s': ['y3', 'r2', 'k1', 'k2', 'k3'], 'c3:s': ['x1', 'r2'], 'y2:s': ['x1', 'y3'], 'y0:s': ['x1', 'y3', 'r2', 'W1b'], 'h1:s': ['x1', 'y3'], 'p01:s': ['h1'], 'p03:s': ['c1'], 'x2:s': ['p01', 'p03'], 'W1a:s': ['y2'], 'c2:s': ['a1', 'y0', 'h1'], 'a3:s': ['x2', 'a1', 'y0', 'h1'], 'x0:s': ['x2', 'a1'], 'h2:s': ['x2', 'a1'], 'p11:s': ['a3', 'W1a', 'x0', 'p02'], 'p13:s': ['p11'], 'c0:s': ['a3'], 'q1:s': ['p02'], 'q2:s': ['p02'], 'q3:s': ['p02'], 'p12:s': ['a2', 'c0', 'h2', 'q1', 'q2', 'q3'], 'p00:s': ['p12'], 'p10:s': ['p12'], 'S:s': ['p12'], 'y1:r': ['r2'], 'att1:s': ['p00']}}
DH = 128
BLOCK = 128
QUAD = 4
SCALE = DH ** (-0.5)
LOG2E = 1.4426950408889634
NT = (((1,), (1,)), ((), ()))


def after(value, *earlier):
    return lax.optimization_barrier((value,) + earlier)[0]


def project_kernel(place_ref, x_ref, *refs):
    w_refs, out_ref = refs[:QUAD], refs[-1]
    mine = place_ref[0]
    width = w_refs[0].shape[1]
    total = refs[QUAD][...].astype(jnp.float32) if len(refs) > QUAD + 1 else None
    for step, w_ref in enumerate(w_refs):
        columns = pl.ds(pl.multiple_of((mine ^ step) * width, width), width)
        term = lax.dot_general(x_ref[:, columns], w_ref[...], NT, preferred_element_type=jnp.float32)
        total = term if total is None else total + term
    out_ref[...] = total.astype(out_ref.dtype)


def project(place, x, w_out, others, base, dtype, more=None):
    rows, depth = x.shape
    _, columns, width = others[0][0].shape
    tile = min(256, columns & -columns)
    steps = columns // tile
    per_place = w_out.shape[0] // QUAD // tile
    offset = base // tile
    out_spec = pl.BlockSpec((rows, tile), lambda n, s: (0, n))
    in_specs = [pl.BlockSpec((rows, depth), lambda n, s: (0, 0))]
    in_specs.append(pl.BlockSpec((tile, width), lambda n, s: (s[0] * per_place + offset + n, 0)))
    for _, pick in others:
        in_specs.append(pl.BlockSpec((None, tile, width), lambda n, s, pick=pick: (pick(s[0]), n, 0)))
    operands = [x, w_out, *(array for array, _ in others)]
    if more is not None:
        in_specs.append(out_spec)
        operands.append(more)
    return pl.pallas_call(
        project_kernel,
        grid_spec=pltpu.PrefetchScalarGridSpec(
            num_scalar_prefetch=1, grid=(steps,), in_specs=in_specs, out_specs=out_spec
        ),
        out_shape=jax.ShapeDtypeStruct((rows, columns), dtype),
        compiler_params=pltpu.CompilerParams(vmem_limit_bytes=OPT['vmem'] * 2**20),
        cost_estimate=pl.CostEstimate(
            flops=int(OPT['cp'] * (2 * rows * depth * columns)),
            bytes_accessed=int(OPT['cp'] * (2 * (rows * depth + depth * columns + rows * columns))),
            transcendentals=0,
        ),
    )(place, *operands)


def lay_out(place_ref, own_ref, late_ref, out):
    for b in range(QUAD):
        out[pl.ds(b * BLOCK, BLOCK), :] = own_ref[b ^ place_ref[0]]
        out[pl.ds((QUAD + b) * BLOCK, BLOCK), :] = late_ref[b ^ place_ref[0]]


def lay_by(place_ref, refs, out):
    for step, ref in enumerate(refs):
        out[pl.ds(pl.multiple_of((step ^ place_ref[0]) * BLOCK, BLOCK), BLOCK), :] = ref[...]


def weigh_kernel(place_ref, k_ref, kp_ref, *refs):
    q_refs, (prob_ref, keys, queries, triangle) = refs[:QUAD], refs[QUAD:]
    mine, root = place_ref[0], place_ref[2]
    own = QUAD * BLOCK
    half = own // 2

    @pl.when(pl.program_id(0) == 0)
    def first():
        lay_out(place_ref, k_ref, kp_ref, keys)
        row = lax.broadcasted_iota(jnp.int32, (half, half), 0)
        col = lax.broadcasted_iota(jnp.int32, (half, half), 1)
        seen = (row // BLOCK > col // BLOCK) | ((row // BLOCK == col // BLOCK) & (row <= col))
        triangle[...] = jnp.where(seen, 0.0, -1e30)

    lay_by(place_ref, q_refs, queries)
    for pair in range(2):
        start = pair * half
        count = 2 * own - start
        q = queries[pl.ds(start, half), :]
        scores = lax.dot_general(
            keys[pl.ds(start, count), :], q, NT, preferred_element_type=jnp.float32
        )
        late = lax.broadcasted_iota(jnp.int32, (own, half), 0) >= root * BLOCK
        parts = [scores[:half] + triangle[...]]
        if pair == 0:
            parts.append(scores[half : 2 * half])
        parts.append(jnp.where(late, scores[count - own :], -1e30))
        scores = jnp.concatenate(parts, axis=0)
        top = jnp.max(scores, axis=0, keepdims=True)
        weights = jnp.exp2((scores - top) * (SCALE * LOG2E))
        prob = weights * (1.0 / jnp.sum(weights, axis=0, keepdims=True))
        prob_ref[0, pl.ds(start, count), pl.ds(start, half)] = prob.astype(jnp.bfloat16)


def weigh(place, queries, keyval, prefix):
    own = QUAD * BLOCK
    block = (QUAD, BLOCK, DH)
    heads = queries[0].shape[1] // DH
    return pl.pallas_call(
        weigh_kernel,
        grid_spec=pltpu.PrefetchScalarGridSpec(
            num_scalar_prefetch=1,
            grid=(heads,),
            in_specs=[
                pl.BlockSpec(block, lambda n, s: (0, 0, 0)),
                pl.BlockSpec(block, lambda n, s: (0, 0, 0)),
            ]
            + [pl.BlockSpec((BLOCK, DH), lambda n, s: (0, n))] * QUAD,
            out_specs=pl.BlockSpec((1, 2 * own, own), lambda n, s: (n, 0, 0)),
            scratch_shapes=[
                pltpu.VMEM((2 * own, DH), jnp.bfloat16),
                pltpu.VMEM((own, DH), jnp.bfloat16),
                pltpu.VMEM((own // 2, own // 2), jnp.float32),
            ],
        ),
        out_shape=jax.ShapeDtypeStruct((heads, 2 * own, own), jnp.bfloat16),
        compiler_params=pltpu.CompilerParams(vmem_limit_bytes=OPT['vmem'] * 2**20),
        cost_estimate=pl.CostEstimate(
            flops=int(OPT['cs'] * (4 * own * own * DH * heads)),
            bytes_accessed=4 * own * own * heads,
            transcendentals=2 * own * own * heads,
        ),
    )(place, keyval, prefix, *queries)


def attend_kernel(head_bits, count_parts, place_ref, prob_ref, k_ref, v_ref, kp_ref, vp_ref, *refs):
    q_refs, refs = refs[:QUAD], refs[QUAD:]
    part_refs, rest = refs[:count_parts], refs[count_parts:]
    gq_ref, dk_ref, dv_ref = rest[-8:-5]
    values, keys_t, keys, queries, grads = rest[-5:]
    before = rest[:-8]
    mine, head_place = place_ref[0], place_ref[1]
    own = QUAD * BLOCK
    half = own // 2
    pieces = 1 << head_bits
    piece = BLOCK // pieces

    @pl.when(pl.program_id(0) == 0)
    def first():
        lay_out(place_ref, k_ref, kp_ref, keys)
        lay_out(place_ref, v_ref, vp_ref, values)
        keys_t[...] = keys[...].astype(jnp.float32).T.astype(jnp.bfloat16)
        if before:
            dk_ref[...] = before[0][...]
            dv_ref[...] = before[1][...]
        else:
            dk_ref[...] = jnp.zeros_like(dk_ref)
            dv_ref[...] = jnp.zeros_like(dv_ref)

    lay_by(place_ref, q_refs, queries)
    for b in range(QUAD):
        for i in range(pieces):
            at = (
                ((b >> 1) ^ (mine >> 1))
                | ((i ^ head_place) << 1)
                | (((b & 1) ^ (mine & 1)) << (1 + head_bits))
            )
            total = part_refs[0][at].astype(jnp.float32)
            for ref in part_refs[1:]:
                total = total + ref[at].astype(jnp.float32)
            grads[pl.ds(b * BLOCK + i * piece, piece), :] = total.astype(jnp.bfloat16)

    for pair in range(2):
        start = pair * half
        q = queries[pl.ds(start, half), :]
        g = grads[pl.ds(start, half), :]
        chunks = [pl.ds(row, half) for row in reversed(range(start, 2 * own, half))]
        lows = [prob_ref[0, rows, pl.ds(start, half)] for rows in chunks]
        dprobs = [
            lax.dot_general(values[rows, :], g, NT, preferred_element_type=jnp.float32)
            for rows in chunks
        ]
        delta = sum(
            jnp.sum(low.astype(jnp.float32) * dprob, axis=0, keepdims=True)
            for low, dprob in zip(lows, dprobs)
        )
        gq = None
        for rows, low, dprob in zip(chunks, lows, dprobs):
            dscore = (low.astype(jnp.float32) * (dprob - delta)).astype(jnp.bfloat16)
            dv_ref[rows, :] += jnp.dot(low, g, preferred_element_type=jnp.float32)
            dk_ref[rows, :] += jnp.dot(dscore, q, preferred_element_type=jnp.float32) * SCALE
            term = jnp.dot(keys_t[:, rows], dscore, preferred_element_type=jnp.float32)
            gq = term if gq is None else gq + term
        gq = (gq * SCALE).T.astype(jnp.bfloat16)
        for b in range(QUAD // 2):
            gq_ref[(pair * (QUAD // 2) + b) ^ mine] = gq[b * BLOCK : (b + 1) * BLOCK]


def attend(place, prob, queries, keyval, prefix, partials, base, heads, head_bits, before=()):
    own = QUAD * BLOCK
    block = (QUAD, BLOCK, DH)
    slots, piece, _ = partials[0].shape

    def column(at):
        return pl.BlockSpec(block, lambda n, s: (0, 0, at))

    whole = pl.BlockSpec((2 * own, DH), lambda n, s: (0, 0))
    return pl.pallas_call(
        functools.partial(attend_kernel, head_bits, len(partials)),
        grid_spec=pltpu.PrefetchScalarGridSpec(
            num_scalar_prefetch=1,
            grid=(heads,),
            in_specs=[
                pl.BlockSpec((1, 2 * own, own), lambda n, s: (base + n, 0, 0)),
                column(0),
                column(1),
                column(0),
                column(1),
            ]
            + [pl.BlockSpec((BLOCK, DH), lambda n, s: (0, base + n))] * QUAD
            + [pl.BlockSpec((slots, piece, DH), lambda n, s: (0, 0, n))] * len(partials)
            + [whole] * len(before),
            out_specs=[pl.BlockSpec(block, lambda n, s: (0, 0, n)), whole, whole],
            scratch_shapes=[
                pltpu.VMEM((2 * own, DH), jnp.bfloat16),
                pltpu.VMEM((DH, 2 * own), jnp.bfloat16),
                pltpu.VMEM((2 * own, DH), jnp.bfloat16),
                pltpu.VMEM((own, DH), jnp.bfloat16),
                pltpu.VMEM((own, DH), jnp.bfloat16),
            ],
        ),
        out_shape=[
            jax.ShapeDtypeStruct((QUAD, BLOCK, heads * DH), jnp.bfloat16),
            jax.ShapeDtypeStruct((2 * own, DH), jnp.float32),
            jax.ShapeDtypeStruct((2 * own, DH), jnp.float32),
        ],
        compiler_params=pltpu.CompilerParams(vmem_limit_bytes=OPT['vmem'] * 2**20),
        cost_estimate=pl.CostEstimate(
            flops=int(OPT['ca'] * (16 * own * own * DH * heads)),
            bytes_accessed=4 * own * own * heads,
            transcendentals=0,
        ),
    )(place, prob, keyval, keyval, prefix, prefix, *queries, *partials, *before)


def per_device(query, key_in, value, grad_y, w_out, parent):
    places, sides = lax.axis_size("ctx"), lax.axis_size("head")
    layers = places // QUAD
    levels = layers.bit_length() - 1
    head_bits = sides.bit_length() - 1
    place, side = lax.axis_index("ctx"), lax.axis_index("head")
    layer, mine = place // QUAD, place % QUAD
    tokens = query.shape[0]
    groups = key_in.shape[1] // DH
    heads = query.shape[1] // DH // QUAD
    depth = QUAD * w_out.shape[1]
    rows = w_out.shape[0] // QUAD
    share = tokens // sides
    counts = [max(1, heads * OPT["cut"] // 8)]
    counts.append(heads - counts[0])
    bases = [sum(counts[:part]) for part in range(len(counts))]

    def swap(x, bits):
        return lax.ppermute(x, "ctx", [(c, c ^ bits) for c in range(places)])

    def flip(x, bits):
        return lax.ppermute(x, "head", [(s, s ^ bits) for s in range(sides)])

    def rotate(x, steps):
        shift = steps * QUAD
        return lax.ppermute(x, "ctx", [(c, (c + shift) % places) for c in range(places)])

    def hop(x, pairs):
        return lax.ppermute(
            x, "ctx", [(s * QUAD + i, t * QUAD + i) for s, t in pairs for i in range(QUAD)]
        )

    def columns(x, at, width):
        return lax.dynamic_slice_in_dim(x, at * width, width, 1)

    def take(x, at, count):
        return lax.dynamic_slice_in_dim(x, at, count, 0)

    def rows_for(part, to):
        return take(w_out, to * rows + bases[part] * DH, counts[part] * DH)

    def join(x, landed):
        return jnp.concatenate([x, landed], axis=0)

    def keyval_for(step):
        at = (mine ^ step) * groups // QUAD
        return jnp.concatenate([columns(key_in, at, DH), columns(value, at, DH)], axis=1)

    def queries_for(step):
        return columns(query, mine ^ step, heads * DH)

    def prefix_hop(prefix, level):
        reach = 1 << level
        sources = [s for s in range(layers) if (layers - 1 - s) % (2 * reach) == 0]
        landed = hop(prefix, [(s, s - reach) for s in sources])
        return jnp.where((layers - 1 - layer) % (2 * reach) == reach, landed, prefix)

    scalars = jnp.stack(
        [
            mine,
            side,
            jnp.where(
                layer == layers - 1,
                QUAD,
                parent[layer * QUAD + QUAD - 1] - (parent.shape[0] - QUAD),
            ),
        ]
    ).astype(jnp.int32)

    done = {}

    def tied(name, x):
        names = [n for n in OPT["ties"].get(name, ()) if n in done]
        if not names:
            return x
        return after(x, *(done[n] for n in names))

    def start(name, send, x):
        done[name] = send(tied(name + ":s", x))

    def land(name):
        done[name] = tied(name + ":r", done[name])
        return done[name]

    def partial(name, part, x, dtype=jnp.bfloat16, more=None):
        done[name] = project(
            tied(name + ":s", scalars), x, w_out, others[part], bases[part] * DH, dtype, more
        )
        return done[name]

    def by_2(x):
        return swap(x, 2)

    def by_1(x):
        return swap(x, 1)

    def by_x(x):
        return flip(x, 1)

    others = [None] * len(counts)
    arrived = [{} for _ in counts]
    if sides == 2 and layers == 4:
        odd = (layer + 1) % 2

        def give(at):
            return lax.dynamic_slice(grad_y, ((1 - side) * share, at * depth), (share, depth))

        def features(steps, other):
            at = (layer - steps) % layers
            held = lax.dynamic_slice(grad_y, (side * share, (at % 2) * depth), (share, depth))
            return jnp.where(at // 2 == side, held, other)

        def interleave(x, landed):
            both = [part.reshape(sides, share, depth) for part in (x, landed)]
            return jnp.stack(both, axis=1).reshape(2 * sides * share, depth)

        def weights_first(part):
            if OPT["cf"]:
                start(f"W{part}b", by_1, jnp.stack([rows_for(part, mine ^ 1), rows_for(part, mine ^ 3)]))
            else:
                first = (mine & 2) ^ 2
                start(f"W{part}a", by_2, jnp.stack([rows_for(part, first + c) for c in range(2)]))

        def weights_second(part):
            if OPT["cf"]:
                beside = land(f"W{part}b")
                start(f"W{part}a", by_2, jnp.stack([rows_for(part, mine ^ 2), beside[1]]))
            else:
                across = land(f"W{part}a")
                through = lax.dynamic_index_in_dim(across, (mine & 1) ^ 1, 0, keepdims=False)
                start(f"W{part}b", by_1, jnp.stack([rows_for(part, mine ^ 1), through]))

        def weights(part):
            if OPT["cf"]:
                across = land(f"W{part}a")
                beside = done[f"W{part}b"]
                others[part] = [(beside, lambda q: 0), (across, lambda q: 0), (across, lambda q: 1)]
            else:
                beside = land(f"W{part}b")
                across = done[f"W{part}a"]
                others[part] = [(beside, lambda q: 0), (across, lambda q: q & 1), (beside, lambda q: 1)]

        x, y, z = {}, {}, {}
        start("xe1", by_x, give(odd))
        weights_first(0)
        start("xe2", by_x, give(1 - odd))
        other = land("xe1")
        start("r1", lambda v: rotate(v, -1), features(1, other))
        start("r3", lambda v: rotate(v, -3), features(3, other))
        if OPT["cf"]:
            weights_second(0)
        other = land("xe2")
        start("r2", lambda v: rotate(v, -2), features(2, other))
        z[0] = features(0, other)

        def first_gather(steps):
            if steps:
                z[steps] = land(f"r{steps}")
            if OPT["dual"][steps]:
                start(f"x{steps}", by_x, z[steps])
            else:
                start(f"y{steps}", by_2, z[steps])

        def second_gather(steps):
            if OPT["dual"][steps]:
                x[steps] = join(z[steps], land(f"x{steps}"))
                start(f"y{steps}", by_2, x[steps])
            else:
                y[steps] = join(z[steps], land(f"y{steps}"))
                start(f"x{steps}", by_x, y[steps])

        def third_gather(steps):
            if OPT["dual"][steps]:
                z[steps] = interleave(x[steps], land(f"y{steps}"))
            else:
                z[steps] = join(y[steps], land(f"x{steps}"))
            start(f"c{steps}", by_1, z[steps])

        def all_of(steps):
            z[steps] = join(z[steps], land(f"c{steps}"))
            return z[steps]

        first_gather(1)
        first_gather(3)
        kv = [keyval_for(step) for step in range(QUAD)]
        for step in range(1, QUAD):
            start(f"k{step}", lambda v, step=step: swap(v, step), kv[step])
        if not OPT["cf"]:
            weights_second(0)
        second_gather(1)
        second_gather(3)
        first_gather(2)
        if OPT["z0"] == 0:
            first_gather(0)
        keyval = jnp.stack(kv[:1] + [land(f"k{step}") for step in range(1, QUAD)])
        start("h1", lambda v: prefix_hop(v, 1), keyval)
        third_gather(1)
        weights_first(1)
        weights(0)
        z1, z3 = all_of(1), None
        up = partial("p01", 0, z1)
        start("a1", lambda v: rotate(v, 1), up)
        third_gather(3)
        second_gather(2)
        z3 = all_of(3)
        down = partial("p03", 0, z3)
        start("a3", lambda v: rotate(v, 3), down)
        weights_second(1)
        near = land("h1")
        start("h2", lambda v: prefix_hop(v, 0), near)
        if OPT["z0"] == 1:
            first_gather(0)
        third_gather(2)
        for step in range(1, QUAD):
            start(f"q{step}", lambda v, step=step: swap(v, step), queries_for(step))
        z2 = all_of(2)
        far = partial("p02", 0, z2)
        start("a2", lambda v: rotate(v, 2), far)
        weights(1)
        up = partial("p11", 1, z1)
        down = partial("p13", 1, z3)
        if OPT["merged"]:
            start("e", lambda v: hop(v, [(0, 1), (3, 2)]), jnp.where(layer == 0, down, up))
            start("b1", lambda v: hop(v, [(0, 1), (1, 2), (2, 3)]), up)
            start("b3", lambda v: hop(v, [(1, 0), (2, 1), (3, 2)]), down)
        else:
            start("b1", lambda v: rotate(v, 1), up)
            start("b3", lambda v: rotate(v, 3), down)
        second_gather(0)
        third_gather(0)
        arrived[0][1], arrived[0][3] = land("a1"), land("a3")
        more = land("e") if OPT["merged"] else None
        far = partial("p12", 1, z2, more=more)
        start("b2", lambda v: rotate(v, 2), far)
        z0 = all_of(0)
        arrived[0][2], arrived[1][1], arrived[1][3] = land("a2"), land("b1"), land("b3")
        arrived[0][0] = partial("p00", 0, z0, dtype=jnp.float32)
        arrived[1][0] = partial("p10", 1, z0, dtype=jnp.float32)
        queries = [queries_for(0)] + [land(f"q{step}") for step in range(1, QUAD)]
        prefix = land("h2")
        prob = weigh(tied("S:s", scalars), queries, keyval, prefix)
        done["S"] = prob
        arrived[1][2] = land("b2")
    else:
        every = lax.all_to_all(grad_y, "head", 0, 1, tiled=True)
        for part in range(len(counts)):
            first = swap(jnp.stack([rows_for(part, mine ^ 1), rows_for(part, mine ^ 3)]), 1)
            second = swap(jnp.stack([rows_for(part, mine ^ 2), first[1]]), 2)
            others[part] = [(first, lambda q: 0), (second, lambda q: 0), (second, lambda q: 1)]
        kv = [keyval_for(step) for step in range(QUAD)]
        keyval = jnp.stack([swap(kv[step], step) if step else kv[0] for step in range(QUAD)])
        prefix = keyval
        for level in reversed(range(levels)):
            prefix = prefix_hop(prefix, level)
        queries = [
            swap(queries_for(step), step) if step else queries_for(step) for step in range(QUAD)
        ]
        for steps in range(layers):
            x = columns(every, (layer - steps) % layers, depth)
            x = rotate(x, -steps) if steps else x
            x = join(x, swap(x, 2))
            for bit in range(head_bits):
                x = join(x, flip(x, 1 << bit))
            x = join(x, swap(x, 1))
            for part in range(len(counts)):
                if steps:
                    arrived[part][steps] = rotate(partial("", part, x), steps)
                else:
                    arrived[part][0] = partial("", part, x, dtype=jnp.float32)
        prob = weigh(scalars, queries, keyval, prefix)

    sums, homes = (), []
    for part, (base, count) in enumerate(zip(bases, counts)):
        terms = [
            arrived[part][steps].reshape(QUAD * sides, share, count * DH) for steps in range(layers)
        ]
        grad_query, *sums = attend(
            tied(f"att{part}:s", scalars), prob, queries, keyval, prefix, terms, base, count, head_bits, tuple(sums)
        )
        done[f"att{part}"] = sums[0]
        homes.append([swap(grad_query[step], step) if step else grad_query[0] for step in range(QUAD)])
    grad_key, grad_value = sums
    if OPT["home"]:
        homes[0] = after(homes[0], grad_key)
    out_query = jnp.zeros(query.shape, query.dtype)
    for base, pieces in zip(bases, homes):
        for step, piece in enumerate(pieces):
            spot = ((mine ^ step) * heads + base) * DH
            out_query = lax.dynamic_update_slice_in_dim(out_query, piece, spot, 1)

    own = QUAD * BLOCK
    both = jnp.concatenate([grad_key, grad_value], axis=1)
    far = both[own:]
    reach = 1
    while 2 * reach < layers:
        hops = [(s, s + reach) for s in range(layers) if (layers - 1 - s) % (2 * reach) == reach]
        far = far + hop(far.astype(jnp.bfloat16), hops).astype(jnp.float32)
        reach *= 2
    narrow = far.astype(jnp.bfloat16)
    near = (both[:own] + jnp.where(layer == layers - 1, far, 0.0)).astype(jnp.bfloat16)
    source = (layers - 1 - reach) * QUAD
    landed = []
    for step in range(QUAD):
        spot = (mine ^ step) * BLOCK
        pairs = [(source + i, (layers - 1) * QUAD + (i ^ step)) for i in range(QUAD)]
        last = lax.ppermute(take(narrow, spot, BLOCK), "ctx", pairs)
        piece = take(near, spot, BLOCK)
        piece = swap(piece, step) if step else piece
        landed.append((piece, last))
    landed = [
        piece.astype(jnp.float32) + last.astype(jnp.float32)
        for piece, last in lax.optimization_barrier(landed)
    ]
    if groups < QUAD:
        added = functools.reduce(jnp.add, landed)
        return out_query, *(x.astype(jnp.bfloat16) for x in jnp.split(added, 2, axis=1))
    totals = [jnp.zeros(key_in.shape, jnp.bfloat16), jnp.zeros(value.shape, jnp.bfloat16)]
    for step, piece in enumerate(landed):
        spot = ((mine ^ step) * groups // QUAD) * DH
        halves = jnp.split(piece.astype(jnp.bfloat16), 2, axis=1)
        totals = [
            lax.dynamic_update_slice_in_dim(total, half, spot, 1)
            for total, half in zip(totals, halves)
        ]
    return out_query, *totals


def solution(mesh):
    placed = (
        P("ctx", "head"),
        P("ctx", "head"),
        P("ctx", "head"),
        P("ctx", "head"),
        P("head", "ctx"),
        P(),
    )
    return jax.shard_map(
        per_device,
        mesh=mesh,
        in_specs=placed,
        out_specs=(P("ctx", "head"), P("ctx", "head"), P("ctx", "head")),
        check_vma=False,
    )
```

time: 283 us -> 214 us (0.76)
  waiting for transfers between devices: 162 us -> 77.5 us
  local copies, waits for them, and re-layouts: 5.96 us -> 16.9 us
  Pallas kernels: 36.7 us -> 44.4 us
  other arithmetic: 16.3 us -> 12.7 us
    ppermute x6 -> x7, waiting for transfers between devices: 46 us -> 8.66 us  [rotate(): lax.ppermute(x, 'ctx', [(c, (c + shift) % places) for c in range(places)])]
    ppermute x4 -> x10, waiting for transfers between devices: 43.9 us -> 11.3 us  [the longest x6 11.3 us: hop(): lax.ppermute(x, 'ctx', [(s * QUAD + i, t * QUAD + i) for s, t in pairs fo...]
    ppermute x20 -> x27, waiting for transfers between devices: 50 us -> 21 us  [swap(): return lax.ppermute(x, 'ctx', [(c, c ^ bits) for c in range(places)])]
    ppermute x5 -> x6, waiting for transfers between devices: 21.8 us -> 36.5 us  [flip(): return lax.ppermute(x, 'head', [(s, s ^ bits) for s in range(sides)])]
    ppermute x4 -> x10, starting transfers between devices: 10.6 us -> 20.3 us  [the longest x6 12.4 us: hop(): lax.ppermute(x, 'ctx', [(s * QUAD + i, t * QUAD + i) for s, t in pairs fo...]
    unnamed x71 -> x86, local copies, waits for them, and re-layouts: 0.71 us -> 9.26 us
    ppermute x20 -> x27, starting transfers between devices: 35.4 us -> 29.7 us  [swap(): return lax.ppermute(x, 'ctx', [(c, c ^ bits) for c in range(places)])]
    concatenate x15 -> x11, other arithmetic: 9.85 us -> 4.91 us  [the longest x8 3.01 us: join(): return jnp.concatenate([x, landed], axis=0)]
  transfers between devices with their start and end apart: 35 -> 50, of which waited for: 17 -> 16; matrix products, arithmetic and copies ran while one was open for 6% -> 8% of each run, Pallas kernels for 5% -> 21%
where the time goes in v2:
time: 214 us; the launch traced here: 213 us
  waiting for transfers between devices  77.5 us (36%)
  starting transfers between devices  59.6 us (28%)
  Pallas kernels  44.4 us (21%)
  local copies, waits for them, and re-layouts  16.9 us (8%)
  other arithmetic  12.7 us (6%)
  between operations  2.29 us (1%)
    ppermute x6, waiting for transfers between devices, flip(): return lax.ppermute(x, 'head', [(s, s ^ bits) for s in range(sides)])  36.5 us
    ppermute x27, starting transfers between devices, swap(): return lax.ppermute(x, 'ctx', [(c, c ^ bits) for c in range(places)])  29.7 us
    ppermute x27, waiting for transfers between devices, swap(): return lax.ppermute(x, 'ctx', [(c, c ^ bits) for c in range(places)])  21 us
    pallas_call x8, Pallas kernels, project(): pl.pallas_call(project_kernel, grid_spec=pltpu.PrefetchScalarGridSpec(num...  18.5 us
    pallas_call x2, Pallas kernels, attend(): pl.pallas_call(functools.partial(attend_kernel, head_bits, len(partials))...  16.6 us
    ppermute x6, starting transfers between devices, hop(): lax.ppermute(x, 'ctx', [(s * QUAD + i, t * QUAD + i) for s, t in pairs fo...  12.4 us
    ppermute x6, waiting for transfers between devices, hop(): lax.ppermute(x, 'ctx', [(s * QUAD + i, t * QUAD + i) for s, t in pairs fo...  11.3 us
    unnamed x86, local copies, waits for them, and re-layouts  9.26 us
  transfers between devices with their start and end apart: 50, of which 16 were waited for; matrix products, arithmetic and copies ran while one was open for 8% of the time, Pallas kernels for 21%

profile of v2, /device:TPU:9, one launch (start us, length us, event | category | flops | bytes accessed | tf_op | source)
XLA Modules:
  0.0 213.5 jit_solution(765408126663106130)
XLA Ops:
  0.7 3.1 %dynamic-slice_bitcast_fusion = (bf16[1,512,512]{2,1,0:T(8,128)(2,1)}, bf16[1,512,512]{2,1,0:T(8,128)(2,1)S(1)}, bf16[1,512,512]{2,1,0:T(8,128)(2,1)}, bf16[1,51...) fusion(bf16[4096,512]{1,0:T(8,128)(2,1)} %refs_0_.15, s32[]{:T(128)S(6)} %select_n.306, ...), kind=kLoop, calls=%fused_computation.16 | loop fusion | bytes 6291480 | tf_op jit(solution)/shard_map/stack | solution.py:378
  8.3 4.6 %collective-permute-done = bf16[64,2048]{1,0:T(8,128)(2,1)S(1)} collective-permute-done((bf16[64,2048]{1,0:T(8,128)(2,1)S(1)}, bf16[64,2048]{1,0:T(8,128)(2,1)S(1)}, u32[]{:S(2)}, u32[]{:S(2)}) %collective-permute-start) | collective-permute-done | bytes 262176 | tf_op jit(solution)/shard_map/ppermute | solution.py:273
  15.0 2.2 %pad_maximum_fusion.3 = bf16[2,512,512]{2,1,0:T(8,128)(2,1)} fusion(bf16[1,512,512]{2,1,0:T(8,128)(2,1)S(1)} %slice.48, bf16[1,512,512]{2,1,0:T(8,128)(2,1)} %get-tuple-element.102), kind=kLoop, calls=%fused_computation.3 | loop fusion | flops 524288 | bytes 2097152 | tf_op jit(solution)/shard_map/stack | solution.py:378
  23.7 2.2 %constant_dynamic-slice_fusion.8 = (bf16[128,1024]{1,0:T(8,128)(2,1)}, bf16[128,1024]{1,0:T(8,128)(2,1)}, bf16[128,1024]{1,0:T(8,128)(2,1)}, bf16[128,1024]{1,0:T(8,128)(2,1)}) fusion(bf16[128,4096]{1,0:T(8,128)(2,1)} %param.6, s32[]{:T(128)S(6)} %select_n.309, s32[]{:T(128)S(6)} %select_n.281, s32[]{:T(128)S(6)} %select_n.282, s32[]{:T(128)S(6)} %select_n.283), kind=kLoop, calls=%fused_computation.83 | loop fusion | bytes 2097168 | tf_op jit(solution)/shard_map/dynamic_slice | solution.py:285
  25.9 7.7 %collective-permute-done.3 = bf16[64,2048]{1,0:T(8,128)(2,1)S(1)} collective-permute-done((bf16[64,2048]{1,0:T(8,128)(2,1)S(1)}, bf16[64,2048]{1,0:T(8,128)(2,1)S(1)}, u32[]{:S(2)}, u32[]{:S(2)}) %collective-permute-start.3) | collective-permute-done | bytes 262176 | tf_op jit(solution)/shard_map/ppermute | solution.py:277
  34.3 6.1 %collective-permute-done.6.refs_2_.refs_3_ = bf16[2,512,512]{2,1,0:T(8,128)(2,1)S(1)} collective-permute-done((bf16[2,512,512]{2,1,0:T(8,128)(2,1)}, bf16[2,512,512]{2,1,0:T(8,128)(2,1)S(1)}, u32[]{:S(2)}, u32[]{:S(2)}) %collective-permute-start.6) | collective-permute-done | bytes 1048608 | tf_op jit(solution)/shard_map/ppermute | solution.py:270
  41.8 2.9 %collective-permute-start.12 = (bf16[128,256]{1,0:T(8,128)(2,1)}, bf16[128,256]{1,0:T(8,128)(2,1)S(1)}, u32[]{:S(2)}, u32[]{:S(2)}) collective-permute-start(bf16[128,256]{1,0:T(8,128)(2,1)} %pad_maximum_fusion.14), channel_id=1, source_target_pairs={{0,2},{2,0},{4,6},{6,4},{8,10},{10,8},{12,14},{14,12},{16,18},{18,... | collective-permute-start | bytes 196616 | tf_op jit(solution)/shard_map/ppermute | solution.py:270
  48.0 4.6 %collective-permute-done.8 = bf16[64,2048]{1,0:T(8,128)(2,1)S(1)} collective-permute-done((bf16[64,2048]{1,0:T(8,128)(2,1)}, bf16[64,2048]{1,0:T(8,128)(2,1)S(1)}, u32[]{:S(2)}, u32[]{:S(2)}) %collective-permute-start.8) | collective-permute-done | bytes 262176 | tf_op jit(solution)/shard_map/ppermute | solution.py:273
  56.2 8.7 %collective-permute-done.9 = bf16[128,2048]{1,0:T(8,128)(2,1)S(1)} collective-permute-done((bf16[128,2048]{1,0:T(8,128)(2,1)S(1)}, bf16[128,2048]{1,0:T(8,128)(2,1)S(1)}, u32[]{:S(2)}, u32[]{:S(2)}) %collective-permute-start.9) | collective-permute-done | bytes 524320 | tf_op jit(solution)/shard_map/ppermute | solution.py:273
  65.0 2.3 %collective-permute-start.16 = (bf16[256,2048]{1,0:T(8,128)(2,1)S(1)}, bf16[256,2048]{1,0:T(8,128)(2,1)S(1)}, u32[]{:S(2)}, u32[]{:S(2)}) collective-permute-start(bf16[256,2048]{1,0:T(8,128)(2,1)S(1)} %pad_maximum_fusion.4), channel_id=1, source_target_pairs={{0,2},{2,0},{4,6},{6,4},{8,10},{10,8},{12,14},{14,12},{16,18},{18,... | collective-permute-start | bytes 3145736 | tf_op jit(solution)/shard_map/ppermute | solution.py:270
  70.1 8.0 %collective-permute-done.15 = bf16[4,128,256]{2,1,0:T(8,128)(2,1)S(1)} collective-permute-done((bf16[4,128,256]{2,1,0:T(8,128)(2,1)S(1)}, bf16[4,128,256]{2,1,0:T(8,128)(2,1)S(1)}, u32[]{:S(2)}, u32[]{:S(2)}) %collective-permute-start.15) | collective-permute-done | bytes 262176 | tf_op jit(solution)/shard_map/ppermute | solution.py:280
  80.4 2.1 shard_map.85
  84.1 2.8 %collective-permute-done.19 = bf16[64,2048]{1,0:T(8,128)(2,1)S(1)} collective-permute-done((bf16[64,2048]{1,0:T(8,128)(2,1)S(1)}, bf16[64,2048]{1,0:T(8,128)(2,1)S(1)}, u32[]{:S(2)}, u32[]{:S(2)}) %collective-permute-start.19) | collective-permute-done | bytes 262176 | tf_op jit(solution)/shard_map/ppermute | solution.py:270
  88.2 7.6 %collective-permute-done.17 = bf16[128,2048]{1,0:T(8,128)(2,1)S(1)} collective-permute-done((bf16[128,2048]{1,0:T(8,128)(2,1)S(1)}, bf16[128,2048]{1,0:T(8,128)(2,1)S(1)}, u32[]{:S(2)}, u32[]{:S(2)}) %collective-permute-start.17) | collective-permute-done | bytes 524320 | tf_op jit(solution)/shard_map/ppermute | solution.py:273
  99.7 2.1 shard_map.87
  102.0 11.0 %collective-permute-done.22 = bf16[128,2048]{1,0:T(8,128)(2,1)S(1)} collective-permute-done((bf16[128,2048]{1,0:T(8,128)(2,1)S(1)}, bf16[128,2048]{1,0:T(8,128)(2,1)S(1)}, u32[]{:S(2)}, u32[]{:S(2)}) %collective-permute-start.22) | collective-permute-done | bytes 524320 | tf_op jit(solution)/shard_map/ppermute | solution.py:273
  117.3 2.8 %shard_map.86 = bf16[512,512]{1,0:T(8,128)(2,1)} custom-call(s32[3]{0:T(128)S(1)} %pad_add_fusion.place_ref, bf16[512,2048]{1,0:T(8,128)(2,1)S(1)} %constant_dynamic-update-slice_fusion.6.x_ref, bf16[4096,512]{1,0:T(8,128)(2,1)S(1)} %copy-done, bf16[2,512,512]{2,1,0:T(8,128)(2,1)S(1)} %collective-permute-done.5.refs_1_, ...), custom_call_target="tpu_custom_call" | custom-call | flops 1073741824 | bytes 4718592 | tf_op jit(solution)/shard_map/pallas_call | solution.py:51
  121.3 2.1 shard_map.88
  123.4 2.1 shard_map.89
  132.2 4.2 %collective-permute-done.28.refs_2_ = bf16[128,1024]{1,0:T(8,128)(2,1)} collective-permute-done((bf16[128,1024]{1,0:T(8,128)(2,1)}, bf16[128,1024]{1,0:T(8,128)(2,1)}, u32[]{:S(2)}, u32[]{:S(2)}) %collective-permute-start.28) | collective-permute-done | bytes 262176 | tf_op jit(solution)/shard_map/ppermute | solution.py:270
  136.4 4.4 %collective-permute-start.38 = (bf16[512,512]{1,0:T(8,128)(2,1)}, bf16[512,512]{1,0:T(8,128)(2,1)S(1)}, u32[]{:S(2)}, u32[]{:S(2)}) collective-permute-start(bf16[512,512]{1,0:T(8,128)(2,1)} %copy-done.12), channel_id=1, source_target_pairs={{8,0},{10,2},{12,4},{14,6},{16,8},{18,10},{20,12},{22,14},{24,16},... | collective-permute-start | bytes 1572872 | tf_op jit(solution)/shard_map/ppermute | solution.py:280
  144.9 2.2 %copy-done.1 = bf16[4096,512]{1,0:T(8,128)(2,1)S(1)} copy-done((bf16[4096,512]{1,0:T(8,128)(2,1)S(1)}, bf16[4096,512]{1,0:T(8,128)(2,1)}, u32[]{:S(2)}) %copy-start.1) | copy-done | bytes 4194328
  149.9 3.0 %shard_map.90 = bf16[512,512]{1,0:T(8,128)(2,1)S(1)} custom-call(s32[3]{0:T(128)S(1)} %pad_add_fusion.place_ref, bf16[512,2048]{1,0:T(8,128)(2,1)S(1)} %copy-done.7, bf16[4096,512]{1,0:T(8,128)(2,1)S(1)} %copy-done.1, bf16[2,512,512]{2,1,0:T(8,128)(2,1)S(1)} %copy-done.4, bf16[2,512,512]{2,1,0:T(8,128)(2,1)S(1)} %collective-permute-done.31.refs_2_.refs_3_, ...), custom_call_target="tpu_custom_call" | custom-call | flops 1073741824 | bytes 4718592 | tf_op jit(solution)/shard_map/pallas_call | solution.py:51
  156.0 2.1 shard_map.92
  158.2 9.2 %shard_map.91.prob_ref = bf16[8,1024,512]{2,1,0:T(8,128)(2,1)S(1)} custom-call(s32[3]{0:T(128)S(1)} %pad_add_fusion.place_ref, bf16[4,128,256]{2,1,0:T(8,128)(2,1)S(1)} %pad_maximum_fusion.13.k_ref.v_ref, bf16[4,128,256]{2,1,0:T(8,128)(2,1)S(1)} %broadcast_select_fusion.1.kp_ref.vp_ref, bf16[128,1024]{1,0:T(8,128)(2,1)S(1)} %copy-done.8, ...), custom_call_target="tpu_custom_call" | custom-call | flops 1073741824 | bytes 8388608 | tf_op jit(solution)/shard_map/pallas_call | solution.py:115
  167.4 8.4 %shard_map.93 = (bf16[4,128,512]{2,1,0:T(8,128)(2,1)S(1)}, f32[1024,128]{1,0:T(8,128)S(1)}, f32[1024,128]{1,0:T(8,128)S(1)}) custom-call(s32[3]{0:T(128)S(1)} %pad_add_fusion.place_ref, bf16[8,1024,512]{2,1,0:T(8,128)(2,1)S(1)} %shard_map.91.prob_ref, bf16[4,128,256]{2,1,0:T(8,128)(2,1)S(1)} %pad_maximum_fusion.13.k_ref.v_ref, ...), custom_call_target="tpu_custom_call" | custom-call | flops 2147483648 | bytes 4194304 | tf_op jit(solution)/shard_map/pallas_call | solution.py:214
  176.9 2.1 shard_map.94
  180.6 8.2 %shard_map.95 = (bf16[4,128,512]{2,1,0:T(8,128)(2,1)S(1)}, f32[1024,128]{1,0:T(8,128)S(1)}, f32[1024,128]{1,0:T(8,128)S(1)}) custom-call(s32[3]{0:T(128)S(1)} %pad_add_fusion.place_ref, bf16[8,1024,512]{2,1,0:T(8,128)(2,1)S(1)} %shard_map.91.prob_ref, bf16[4,128,256]{2,1,0:T(8,128)(2,1)S(1)} %pad_maximum_fusion.13.k_ref.v_ref, ...), custom_call_target="tpu_custom_call" | custom-call | flops 2147483648 | bytes 4194304 | tf_op jit(solution)/shard_map/pallas_call | solution.py:214
  192.8 2.4 %collective-permute-done.40 = bf16[128,512]{1,0:T(8,128)(2,1)S(1)} collective-permute-done((bf16[128,512]{1,0:T(8,128)(2,1)S(1)}, bf16[128,512]{1,0:T(8,128)(2,1)S(1)}, u32[]{:S(2)}, u32[]{:S(2)}) %collective-permute-start.40) | collective-permute-done | bytes 131104 | tf_op jit(solution)/shard_map/ppermute | solution.py:270
  195.3 3.3 %collective-permute-done.42 = bf16[512,256]{1,0:T(8,128)(2,1)S(1)} collective-permute-done((bf16[512,256]{1,0:T(8,128)(2,1)S(1)}, bf16[512,256]{1,0:T(8,128)(2,1)S(1)}, u32[]{:S(2)}, u32[]{:S(2)}) %collective-permute-start.42) | collective-permute-done | bytes 262176 | tf_op jit(solution)/shard_map/ppermute | solution.py:280
  198.7 2.6 %collective-permute-start.43 = (bf16[128,256]{1,0:T(8,128)(2,1)S(1)}, bf16[128,256]{1,0:T(8,128)(2,1)S(1)}, u32[]{:S(2)}, u32[]{:S(2)}) collective-permute-start(bf16[128,256]{1,0:T(8,128)(2,1)S(1)} %get-tuple-element.124), channel_id=1, source_target_pairs={{8,24},{10,26},{12,28},{14,30},{9,25},{11,27},{13,29},{15,31}} | collective-permute-start | bytes 196616 | tf_op jit(solution)/shard_map/ppermute | solution.py:557
  201.3 2.8 %collective-permute-start.45 = (bf16[128,256]{1,0:T(8,128)(2,1)S(1)}, bf16[128,256]{1,0:T(8,128)(2,1)S(1)}, u32[]{:S(2)}, u32[]{:S(2)}) collective-permute-start(bf16[128,256]{1,0:T(8,128)(2,1)S(1)} %get-tuple-element.123), channel_id=1, source_target_pairs={{8,26},{10,24},{12,30},{14,28},{9,27},{11,25},{13,31},{15,29}} | collective-permute-start | bytes 196616 | tf_op jit(solution)/shard_map/ppermute | solution.py:557
  (226 shorter events, 70.9 us)
Async XLA Ops:
  4.8 10.1 %collective-permute-start.5 = (bf16[2,512,512]{2,1,0:T(8,128)(2,1)}, bf16[2,512,512]{2,1,0:T(8,128)(2,1)S(1)}, u32[]{:S(2)}, u32[]{:S(2)}) collective-permute-start(bf16[2,512,512]{2,1,0:T(8,128)(2,1)} %pad_maximum_fusion.2), channel_id=1, source_target_pairs={{0,2},{2,0},{4,6},{6,4},{8,10},{10,8},{12,14},{14,12},{16,18},{18,... | collective-permute-start | bytes 3145736 | tf_op jit(solution)/shard_map/ppermute | solution.py:270
  17.2 23.2 %collective-permute-start.6 = (bf16[2,512,512]{2,1,0:T(8,128)(2,1)}, bf16[2,512,512]{2,1,0:T(8,128)(2,1)S(1)}, u32[]{:S(2)}, u32[]{:S(2)}) collective-permute-start(bf16[2,512,512]{2,1,0:T(8,128)(2,1)} %pad_maximum_fusion.3), channel_id=1, source_target_pairs={{0,4},{2,6},{4,0},{6,2},{8,12},{10,14},{12,8},{14,10},{16,20},{18,... | collective-permute-start | bytes 3145736 | tf_op jit(solution)/shard_map/ppermute | solution.py:270
  20.9 12.7 %collective-permute-start.3 = (bf16[64,2048]{1,0:T(8,128)(2,1)S(1)}, bf16[64,2048]{1,0:T(8,128)(2,1)S(1)}, u32[]{:S(2)}, u32[]{:S(2)}) collective-permute-start(bf16[64,2048]{1,0:T(8,128)(2,1)S(1)} %get-tuple-element.107), channel_id=1, source_target_pairs={{0,8},{2,10},{4,12},{6,14},{8,16},{10,18},{12,20},{14,22},{16,24},... | collective-permute-start | bytes 786440 | tf_op jit(solution)/shard_map/ppermute | solution.py:277
  33.6 12.5 %collective-permute-start.4 = (bf16[64,2048]{1,0:T(8,128)(2,1)}, bf16[64,2048]{1,0:T(8,128)(2,1)S(1)}, u32[]{:S(2)}, u32[]{:S(2)}) collective-permute-start(bf16[64,2048]{1,0:T(8,128)(2,1)} %get-tuple-element.50), channel_id=1, source_target_pairs={{0,16},{2,18},{4,20},{6,22},{8,24},{10,26},{12,28},{14,30},{16,0},... | collective-permute-start | bytes 786440 | tf_op jit(solution)/shard_map/ppermute | solution.py:277
  41.8 12.5 %collective-permute-start.12 = (bf16[128,256]{1,0:T(8,128)(2,1)}, bf16[128,256]{1,0:T(8,128)(2,1)S(1)}, u32[]{:S(2)}, u32[]{:S(2)}) collective-permute-start(bf16[128,256]{1,0:T(8,128)(2,1)} %pad_maximum_fusion.14), channel_id=1, source_target_pairs={{0,2},{2,0},{4,6},{6,4},{8,10},{10,8},{12,14},{14,12},{16,18},{18,... | collective-permute-start | bytes 196616 | tf_op jit(solution)/shard_map/ppermute | solution.py:270
  44.7 11.4 %collective-permute-start.13 = (bf16[128,256]{1,0:T(8,128)(2,1)}, bf16[128,256]{1,0:T(8,128)(2,1)S(1)}, u32[]{:S(2)}, u32[]{:S(2)}) collective-permute-start(bf16[128,256]{1,0:T(8,128)(2,1)} %pad_maximum_fusion.15), channel_id=1, source_target_pairs={{0,4},{2,6},{4,0},{6,2},{8,12},{10,14},{12,8},{14,10},{16,20},{18,... | collective-permute-start | bytes 196616 | tf_op jit(solution)/shard_map/ppermute | solution.py:270
  52.7 12.2 %collective-permute-start.9 = (bf16[128,2048]{1,0:T(8,128)(2,1)S(1)}, bf16[128,2048]{1,0:T(8,128)(2,1)S(1)}, u32[]{:S(2)}, u32[]{:S(2)}) collective-permute-start(bf16[128,2048]{1,0:T(8,128)(2,1)S(1)} %pad_maximum_fusion.10), channel_id=1, source_target_pairs={{0,1},{1,0},{2,3},{3,2},{4,5},{5,4},{6,7},{7,6},{8,9},{9,8},{10,11... | collective-permute-start | bytes 1572872 | tf_op jit(solution)/shard_map/ppermute | solution.py:273
  52.9 12.1 %collective-permute-start.10 = (bf16[128,2048]{1,0:T(8,128)(2,1)S(1)}, bf16[128,2048]{1,0:T(8,128)(2,1)S(1)}, u32[]{:S(2)}, u32[]{:S(2)}) collective-permute-start(bf16[128,2048]{1,0:T(8,128)(2,1)S(1)} %constant_dynamic-update-slice_fusion), channel_id=1, source_target_pairs={{0,4},{2,6},{4,0},{6,2},{8,12},{10,14},{12,8},{14,10},{16,20},{18,... | collective-permute-start | bytes 1572872 | tf_op jit(solution)/shard_map/ppermute | solution.py:270
  54.3 73.5 %collective-permute-start.27 = (bf16[128,1024]{1,0:T(8,128)(2,1)}, bf16[128,1024]{1,0:T(8,128)(2,1)S(1)}, u32[]{:S(2)}, u32[]{:S(2)}) collective-permute-start(bf16[128,1024]{1,0:T(8,128)(2,1)} %get-tuple-element.111), channel_id=1, source_target_pairs={{0,2},{2,0},{4,6},{6,4},{8,10},{10,8},{12,14},{14,12},{16,18},{18,... | collective-permute-start | bytes 786440 | tf_op jit(solution)/shard_map/ppermute | solution.py:270
  56.1 27.8 %collective-permute-start.30 = (bf16[2,512,512]{2,1,0:T(8,128)(2,1)S(1)}, bf16[2,512,512]{2,1,0:T(8,128)(2,1)S(1)}, u32[]{:S(2)}, u32[]{:S(2)}) collective-permute-start(bf16[2,512,512]{2,1,0:T(8,128)(2,1)S(1)} %copy-done.30), channel_id=1, source_target_pairs={{0,2},{2,0},{4,6},{6,4},{8,10},{10,8},{12,14},{14,12},{16,18},{18,... | collective-permute-start | bytes 3145736 | tf_op jit(solution)/shard_map/ppermute | solution.py:270
  65.0 15.3 %collective-permute-start.16 = (bf16[256,2048]{1,0:T(8,128)(2,1)S(1)}, bf16[256,2048]{1,0:T(8,128)(2,1)S(1)}, u32[]{:S(2)}, u32[]{:S(2)}) collective-permute-start(bf16[256,2048]{1,0:T(8,128)(2,1)S(1)} %pad_maximum_fusion.4), channel_id=1, source_target_pairs={{0,2},{2,0},{4,6},{6,4},{8,10},{10,8},{12,14},{14,12},{16,18},{18,... | collective-permute-start | bytes 3145736 | tf_op jit(solution)/shard_map/ppermute | solution.py:270
  67.4 10.7 %collective-permute-start.15 = (bf16[4,128,256]{2,1,0:T(8,128)(2,1)S(1)}, bf16[4,128,256]{2,1,0:T(8,128)(2,1)S(1)}, u32[]{:S(2)}, u32[]{:S(2)}) collective-permute-start(bf16[4,128,256]{2,1,0:T(8,128)(2,1)S(1)} %pad_maximum_fusion.13.k_ref.v_ref), channel_id=1, source_target_pairs={{24,8},{26,10},{28,12},{30,14},{25,9},{27,11},{29,13},{31,15}} | collective-permute-start | bytes 786440 | tf_op jit(solution)/shard_map/ppermute | solution.py:280
  68.7 10.3 %collective-permute-start.11 = (bf16[64,2048]{1,0:T(8,128)(2,1)S(1)}, bf16[64,2048]{1,0:T(8,128)(2,1)S(1)}, u32[]{:S(2)}, u32[]{:S(2)}) collective-permute-start(bf16[64,2048]{1,0:T(8,128)(2,1)S(1)} %collective-permute-done.4), channel_id=1, source_target_pairs={{0,4},{2,6},{4,0},{6,2},{8,12},{10,14},{12,8},{14,10},{16,20},{18,... | collective-permute-start | bytes 786440 | tf_op jit(solution)/shard_map/ppermute | solution.py:270
  78.1 21.0 %collective-permute-start.23 = (bf16[256,2048]{1,0:T(8,128)(2,1)S(1)}, bf16[256,2048]{1,0:T(8,128)(2,1)S(1)}, u32[]{:S(2)}, u32[]{:S(2)}) collective-permute-start(bf16[256,2048]{1,0:T(8,128)(2,1)S(1)} %bitcast.59), channel_id=1, source_target_pairs={{0,2},{2,0},{4,6},{6,4},{8,10},{10,8},{12,14},{14,12},{16,18},{18,... | collective-permute-start | bytes 3145736 | tf_op jit(solution)/shard_map/ppermute | solution.py:270
  82.6 13.3 %collective-permute-start.17 = (bf16[128,2048]{1,0:T(8,128)(2,1)S(1)}, bf16[128,2048]{1,0:T(8,128)(2,1)S(1)}, u32[]{:S(2)}, u32[]{:S(2)}) collective-permute-start(bf16[128,2048]{1,0:T(8,128)(2,1)S(1)} %pad_maximum_fusion.11), channel_id=1, source_target_pairs={{0,1},{1,0},{2,3},{3,2},{4,5},{5,4},{6,7},{7,6},{8,9},{9,8},{10,11... | collective-permute-start | bytes 1572872 | tf_op jit(solution)/shard_map/ppermute | solution.py:273
  83.9 13.0 %collective-permute-start.18 = (bf16[512,512]{1,0:T(8,128)(2,1)S(1)}, bf16[512,512]{1,0:T(8,128)(2,1)S(1)}, u32[]{:S(2)}, u32[]{:S(2)}) collective-permute-start(bf16[512,512]{1,0:T(8,128)(2,1)S(1)} %shard_map.85), channel_id=1, source_target_pairs={{0,8},{2,10},{4,12},{6,14},{8,16},{10,18},{12,20},{14,22},{16,24},... | collective-permute-start | bytes 1572872 | tf_op jit(solution)/shard_map/ppermute | solution.py:277
  86.9 34.3 %collective-permute-start.31 = (bf16[2,512,512]{2,1,0:T(8,128)(2,1)S(1)}, bf16[2,512,512]{2,1,0:T(8,128)(2,1)S(1)}, u32[]{:S(2)}, u32[]{:S(2)}) collective-permute-start(bf16[2,512,512]{2,1,0:T(8,128)(2,1)S(1)} %pad_maximum_fusion.9), channel_id=1, source_target_pairs={{0,4},{2,6},{4,0},{6,2},{8,12},{10,14},{12,8},{14,10},{16,20},{18,... | collective-permute-start | bytes 3145736 | tf_op jit(solution)/shard_map/ppermute | solution.py:270
  97.7 19.4 %collective-permute-start.20 = (bf16[256,2048]{1,0:T(8,128)(2,1)S(1)}, bf16[256,2048]{1,0:T(8,128)(2,1)S(1)}, u32[]{:S(2)}, u32[]{:S(2)}) collective-permute-start(bf16[256,2048]{1,0:T(8,128)(2,1)S(1)} %pad_maximum_fusion.5), channel_id=1, source_target_pairs={{0,2},{2,0},{4,6},{6,4},{8,10},{10,8},{12,14},{14,12},{16,18},{18,... | collective-permute-start | bytes 3145736 | tf_op jit(solution)/shard_map/ppermute | solution.py:270
  99.4 13.6 %collective-permute-start.22 = (bf16[128,2048]{1,0:T(8,128)(2,1)S(1)}, bf16[128,2048]{1,0:T(8,128)(2,1)S(1)}, u32[]{:S(2)}, u32[]{:S(2)}) collective-permute-start(bf16[128,2048]{1,0:T(8,128)(2,1)S(1)} %pad_maximum_fusion.12), channel_id=1, source_target_pairs={{0,1},{1,0},{2,3},{3,2},{4,5},{5,4},{6,7},{7,6},{8,9},{9,8},{10,11... | collective-permute-start | bytes 1572872 | tf_op jit(solution)/shard_map/ppermute | solution.py:273
  101.8 14.3 %collective-permute-start.24 = (bf16[512,512]{1,0:T(8,128)(2,1)S(1)}, bf16[512,512]{1,0:T(8,128)(2,1)S(1)}, u32[]{:S(2)}, u32[]{:S(2)}) collective-permute-start(bf16[512,512]{1,0:T(8,128)(2,1)S(1)} %shard_map.87), channel_id=1, source_target_pairs={{0,24},{2,26},{4,28},{6,30},{8,0},{10,2},{12,4},{14,6},{16,8},{18,... | collective-permute-start | bytes 1572872 | tf_op jit(solution)/shard_map/ppermute | solution.py:277
  113.0 15.7 %collective-permute-start.26 = (bf16[4,128,256]{2,1,0:T(8,128)(2,1)S(1)}, bf16[4,128,256]{2,1,0:T(8,128)(2,1)S(1)}, u32[]{:S(2)}, u32[]{:S(2)}) collective-permute-start(bf16[4,128,256]{2,1,0:T(8,128)(2,1)S(1)} %broadcast_select_fusion.2), channel_id=1, source_target_pairs={{8,0},{10,2},{12,4},{14,6},{24,16},{26,18},{28,20},{30,22},{9,1},{... | collective-permute-start | bytes 786440 | tf_op jit(solution)/shard_map/ppermute | solution.py:280
  116.1 28.8 %collective-permute-start.25 = (bf16[256,2048]{1,0:T(8,128)(2,1)}, bf16[256,2048]{1,0:T(8,128)(2,1)}, u32[]{:S(2)}, u32[]{:S(2)}) collective-permute-start(bf16[256,2048]{1,0:T(8,128)(2,1)} %pad_maximum_fusion.6), channel_id=1, source_target_pairs={{0,2},{2,0},{4,6},{6,4},{8,10},{10,8},{12,14},{14,12},{16,18},{18,... | collective-permute-start | bytes 3145736 | tf_op jit(solution)/shard_map/ppermute | solution.py:270
  120.1 24.8 %collective-permute-start.21 = (bf16[512,512]{1,0:T(8,128)(2,1)}, bf16[512,512]{1,0:T(8,128)(2,1)}, u32[]{:S(2)}, u32[]{:S(2)}) collective-permute-start(bf16[512,512]{1,0:T(8,128)(2,1)} %shard_map.86), channel_id=1, source_target_pairs={{0,16},{2,18},{4,20},{6,22},{8,24},{10,26},{12,28},{14,30},{16,0},... | collective-permute-start | bytes 1572872 | tf_op jit(solution)/shard_map/ppermute | solution.py:277
  126.5 18.4 %collective-permute-start.32 = (bf16[512,512]{1,0:T(8,128)(2,1)}, bf16[512,512]{1,0:T(8,128)(2,1)}, u32[]{:S(2)}, u32[]{:S(2)}) collective-permute-start(bf16[512,512]{1,0:T(8,128)(2,1)} %broadcast_select_fusion), channel_id=1, source_target_pairs={{0,8},{2,10},{4,12},{6,14},{24,16},{26,18},{28,20},{30,22},{1,9},{... | collective-permute-start | bytes 1572872 | tf_op jit(solution)/shard_map/ppermute | solution.py:280
  129.4 13.3 %collective-permute-start.29 = (bf16[128,1024]{1,0:T(8,128)(2,1)}, bf16[128,1024]{1,0:T(8,128)(2,1)}, u32[]{:S(2)}, u32[]{:S(2)}) collective-permute-start(bf16[128,1024]{1,0:T(8,128)(2,1)} %get-tuple-element.112), channel_id=1, source_target_pairs={{0,6},{2,4},{4,2},{6,0},{8,14},{10,12},{12,10},{14,8},{16,22},{18,... | collective-permute-start | bytes 786440 | tf_op jit(solution)/shard_map/ppermute | solution.py:270
  136.4 42.6 %collective-permute-start.38 = (bf16[512,512]{1,0:T(8,128)(2,1)}, bf16[512,512]{1,0:T(8,128)(2,1)S(1)}, u32[]{:S(2)}, u32[]{:S(2)}) collective-permute-start(bf16[512,512]{1,0:T(8,128)(2,1)} %copy-done.12), channel_id=1, source_target_pairs={{8,0},{10,2},{12,4},{14,6},{16,8},{18,10},{20,12},{22,14},{24,16},... | collective-permute-start | bytes 1572872 | tf_op jit(solution)/shard_map/ppermute | solution.py:280
  142.8 37.8 %collective-permute-start.36 = (bf16[512,512]{1,0:T(8,128)(2,1)}, bf16[512,512]{1,0:T(8,128)(2,1)S(1)}, u32[]{:S(2)}, u32[]{:S(2)}) collective-permute-start(bf16[512,512]{1,0:T(8,128)(2,1)} %copy-done.11), channel_id=1, source_target_pairs={{0,8},{2,10},{4,12},{6,14},{8,16},{10,18},{12,20},{14,22},{16,24},... | collective-permute-start | bytes 1572872 | tf_op jit(solution)/shard_map/ppermute | solution.py:280
  153.0 27.6 %collective-permute-start.37 = (bf16[512,512]{1,0:T(8,128)(2,1)S(1)}, bf16[512,512]{1,0:T(8,128)(2,1)S(1)}, u32[]{:S(2)}, u32[]{:S(2)}) collective-permute-start(bf16[512,512]{1,0:T(8,128)(2,1)S(1)} %shard_map.90), channel_id=1, source_target_pairs={{0,16},{2,18},{4,20},{6,22},{8,24},{10,26},{12,28},{14,30},{16,0},... | collective-permute-start | bytes 1572872 | tf_op jit(solution)/shard_map/ppermute | solution.py:277
  175.9 14.4 %collective-permute-start.33 = (bf16[128,512]{1,0:T(8,128)(2,1)S(1)}, bf16[128,512]{1,0:T(8,128)(2,1)S(1)}, u32[]{:S(2)}, u32[]{:S(2)}) collective-permute-start(bf16[128,512]{1,0:T(8,128)(2,1)S(1)} %get-tuple-element.119), channel_id=1, source_target_pairs={{0,2},{2,0},{4,6},{6,4},{8,10},{10,8},{12,14},{14,12},{16,18},{18,... | collective-permute-start | bytes 393224 | tf_op jit(solution)/shard_map/ppermute | solution.py:270
  176.7 13.6 %collective-permute-start.34 = (bf16[128,512]{1,0:T(8,128)(2,1)S(1)}, bf16[128,512]{1,0:T(8,128)(2,1)S(1)}, u32[]{:S(2)}, u32[]{:S(2)}) collective-permute-start(bf16[128,512]{1,0:T(8,128)(2,1)S(1)} %get-tuple-element.118), channel_id=1, source_target_pairs={{0,4},{2,6},{4,0},{6,2},{8,12},{10,14},{12,8},{14,10},{16,20},{18,... | collective-permute-start | bytes 393224 | tf_op jit(solution)/shard_map/ppermute | solution.py:270
  179.0 11.2 %collective-permute-start.35 = (bf16[128,512]{1,0:T(8,128)(2,1)S(1)}, bf16[128,512]{1,0:T(8,128)(2,1)S(1)}, u32[]{:S(2)}, u32[]{:S(2)}) collective-permute-start(bf16[128,512]{1,0:T(8,128)(2,1)S(1)} %get-tuple-element.117), channel_id=1, source_target_pairs={{0,6},{2,4},{4,2},{6,0},{8,14},{10,12},{12,10},{14,8},{16,22},{18,... | collective-permute-start | bytes 393224 | tf_op jit(solution)/shard_map/ppermute | solution.py:270
  190.8 16.0 %collective-permute-start.41 = (bf16[128,512]{1,0:T(8,128)(2,1)S(1)}, bf16[128,512]{1,0:T(8,128)(2,1)S(1)}, u32[]{:S(2)}, u32[]{:S(2)}) collective-permute-start(bf16[128,512]{1,0:T(8,128)(2,1)S(1)} %get-tuple-element.114), channel_id=1, source_target_pairs={{0,6},{2,4},{4,2},{6,0},{8,14},{10,12},{12,10},{14,8},{16,22},{18,... | collective-permute-start | bytes 393224 | tf_op jit(solution)/shard_map/ppermute | solution.py:270
  (57 other events, 517.2 us)

commit v3 on v2

--- a/solution.py
+++ b/solution.py
@@ -7,7 +7,7 @@
 from jax.experimental.pallas import tpu as pltpu
 from jax.sharding import PartitionSpec as P
 
-OPT = {'vmem': 16, 'cp': 1.0, 'cs': 1.0, 'ca': 1.0, 'cf': 1, 'dual': [0, 0, 0, 1], 'z0': 0, 'merged': 1, 'home': 1, 'cut': 4, 'ties': {'y1:s': ['r3', 'W0a', 'xe2'], 'x3:s': ['r1', 'W0a', 'xe2'], 'r2:s': ['r1', 'r3'], 'k1:s': ['r1'], 'k2:s': ['r1'], 'k3:s': ['r1'], 'W1b:s': ['r1'], 'x1:s': ['x3'], 'y3:s': ['y1'], 'c1:s': ['y3', 'r2', 'k1', 'k2', 'k3'], 'c3:s': ['x1', 'r2'], 'y2:s': ['x1', 'y3'], 'y0:s': ['x1', 'y3', 'r2', 'W1b'], 'h1:s': ['x1', 'y3'], 'p01:s': ['h1'], 'p03:s': ['c1'], 'x2:s': ['p01', 'p03'], 'W1a:s': ['y2'], 'c2:s': ['a1', 'y0', 'h1'], 'a3:s': ['x2', 'a1', 'y0', 'h1'], 'x0:s': ['x2', 'a1'], 'h2:s': ['x2', 'a1'], 'p11:s': ['a3', 'W1a', 'x0', 'p02'], 'p13:s': ['p11'], 'c0:s': ['a3'], 'q1:s': ['p02'], 'q2:s': ['p02'], 'q3:s': ['p02'], 'p12:s': ['a2', 'c0', 'h2', 'q1', 'q2', 'q3'], 'p00:s': ['p12'], 'p10:s': ['p12'], 'S:s': ['p12'], 'y1:r': ['r2'], 'att1:s': ['p00']}}
+OPT = {'vmem': 16, 'cp': 1.0, 'cs': 1.0, 'ca': 1.0, 'cf': 1, 'dual': [0, 0, 0, 1], 'z0': 0, 'merged': 1, 'home': 1, 'cut': 4, 'ties': {'y1:s': ['r3', 'W0a', 'xe2'], 'x3:s': ['r1', 'W0a', 'xe2'], 'r2:s': ['r1', 'r3'], 'k1:s': ['r1', 'y1'], 'k2:s': ['r1'], 'k3:s': ['r1'], 'W1b:s': ['r1'], 'x1:s': ['x3'], 'y3:s': ['y1'], 'c1:s': ['y3', 'r2', 'k1', 'k2', 'k3'], 'c3:s': ['x1', 'r2'], 'y2:s': ['x1', 'y3'], 'y0:s': ['x1', 'y3', 'r2', 'W1b'], 'h1:s': ['x1', 'y3'], 'p01:s': ['h1'], 'p03:s': ['c1'], 'x2:s': ['p01', 'p03'], 'W1a:s': ['y2'], 'c2:s': ['a1', 'y0', 'h1'], 'a3:s': ['x2', 'a1', 'y0', 'h1'], 'x0:s': ['x2', 'a1'], 'h2:s': ['x2', 'a1'], 'p11:s': ['a3', 'W1a', 'x0', 'p02'], 'p13:s': ['p11'], 'c0:s': ['a3'], 'q1:s': ['p02'], 'q2:s': ['p02'], 'q3:s': ['p02'], 'p12:s': ['a2', 'c0', 'h2', 'q1', 'q2', 'q3'], 'p00:s': ['p12'], 'p10:s': ['p12'], 'S:s': ['p12'], 'y1:r': ['r2'], 'att1:s': ['p00']}}
 DH = 128
 BLOCK = 128
 QUAD = 4

time: 214 us -> 212 us (level)
  waiting for transfers between devices: 77.5 us -> 73.7 us
    ppermute x6, waiting for transfers between devices: 36.5 us -> 29.7 us  [flip(): return lax.ppermute(x, 'head', [(s, s ^ bits) for s in range(sides)])]
    unnamed x86 -> x82, local copies, waits for them, and re-layouts: 9.26 us -> 8.55 us
  transfers between devices with their start and end apart: 50 -> 50, of which waited for: 16 -> 19; matrix products, arithmetic and copies ran while one was open for 8% -> 8% of each run, Pallas kernels for 21% -> 21%
where the time goes in v3:
time: 212 us; the launch traced here: 211 us
  waiting for transfers between devices  73.7 us (35%)
  starting transfers between devices  61 us (29%)
  Pallas kernels  44.3 us (21%)
  local copies, waits for them, and re-layouts  15.3 us (7%)
  other arithmetic  14.3 us (7%)
  between operations  2.31 us (1%)
    ppermute x6, waiting for transfers between devices, flip(): return lax.ppermute(x, 'head', [(s, s ^ bits) for s in range(sides)])  29.7 us
    ppermute x27, starting transfers between devices, swap(): return lax.ppermute(x, 'ctx', [(c, c ^ bits) for c in range(places)])  28.3 us
    ppermute x27, waiting for transfers between devices, swap(): return lax.ppermute(x, 'ctx', [(c, c ^ bits) for c in range(places)])  22.3 us
    pallas_call x8, Pallas kernels, project(): pl.pallas_call(project_kernel, grid_spec=pltpu.PrefetchScalarGridSpec(num...  18.5 us
    pallas_call x2, Pallas kernels, attend(): pl.pallas_call(functools.partial(attend_kernel, head_bits, len(partials))...  16.6 us
    ppermute x6, starting transfers between devices, hop(): lax.ppermute(x, 'ctx', [(s * QUAD + i, t * QUAD + i) for s, t in pairs fo...  13.6 us
    ppermute x6, waiting for transfers between devices, hop(): lax.ppermute(x, 'ctx', [(s * QUAD + i, t * QUAD + i) for s, t in pairs fo...  11.4 us
    ppermute x7, waiting for transfers between devices, rotate(): lax.ppermute(x, 'ctx', [(c, (c + shift) % places) for c in range(places)])  10.3 us
  transfers between devices with their start and end apart: 50, of which 19 were waited for; matrix products, arithmetic and copies ran while one was open for 8% of the time, Pallas kernels for 21%

profile of v3, /device:TPU:9, one launch (start us, length us, event | category | flops | bytes accessed | tf_op | source)
XLA Modules:
  0.0 210.9 jit_solution(9305899054636624641)
XLA Ops:
  0.7 3.1 %dynamic-slice_bitcast_fusion = (bf16[1,512,512]{2,1,0:T(8,128)(2,1)}, bf16[1,512,512]{2,1,0:T(8,128)(2,1)S(1)}, bf16[1,512,512]{2,1,0:T(8,128)(2,1)}, bf16[1,51...) fusion(bf16[4096,512]{1,0:T(8,128)(2,1)} %refs_0_.15, s32[]{:T(128)S(6)} %select_n.306, ...), kind=kLoop, calls=%fused_computation.16 | loop fusion | bytes 6291480 | tf_op jit(solution)/shard_map/stack | solution.py:378
  6.8 2.2 %constant_dynamic-slice_fusion.8 = (bf16[128,1024]{1,0:T(8,128)(2,1)}, bf16[128,1024]{1,0:T(8,128)(2,1)}, bf16[128,1024]{1,0:T(8,128)(2,1)}, bf16[128,1024]{1,0:T(8,128)(2,1)}) fusion(bf16[128,4096]{1,0:T(8,128)(2,1)} %param.6, s32[]{:T(128)S(6)} %select_n.309, s32[]{:T(128)S(6)} %select_n.281, s32[]{:T(128)S(6)} %select_n.282, s32[]{:T(128)S(6)} %select_n.283), kind=kLoop, calls=%fused_computation.83 | loop fusion | bytes 2097168 | tf_op jit(solution)/shard_map/dynamic_slice | solution.py:285
  9.8 3.1 %collective-permute-done = bf16[64,2048]{1,0:T(8,128)(2,1)S(1)} collective-permute-done((bf16[64,2048]{1,0:T(8,128)(2,1)S(1)}, bf16[64,2048]{1,0:T(8,128)(2,1)S(1)}, u32[]{:S(2)}, u32[]{:S(2)}) %collective-permute-start) | collective-permute-done | bytes 262176 | tf_op jit(solution)/shard_map/ppermute | solution.py:273
  15.0 2.1 %pad_maximum_fusion.3 = bf16[2,512,512]{2,1,0:T(8,128)(2,1)} fusion(bf16[1,512,512]{2,1,0:T(8,128)(2,1)S(1)} %slice.48, bf16[1,512,512]{2,1,0:T(8,128)(2,1)} %get-tuple-element.102), kind=kLoop, calls=%fused_computation.3 | loop fusion | flops 524288 | bytes 2097152 | tf_op jit(solution)/shard_map/stack | solution.py:378
  24.3 2.1 pad_maximum_fusion.8
  26.7 7.8 %collective-permute-done.3 = bf16[64,2048]{1,0:T(8,128)(2,1)} collective-permute-done((bf16[64,2048]{1,0:T(8,128)(2,1)S(1)}, bf16[64,2048]{1,0:T(8,128)(2,1)}, u32[]{:S(2)}, u32[]{:S(2)}) %collective-permute-start.3) | collective-permute-done | bytes 262176 | tf_op jit(solution)/shard_map/ppermute | solution.py:277
  34.5 5.8 %collective-permute-done.6.refs_2_.refs_3_ = bf16[2,512,512]{2,1,0:T(8,128)(2,1)S(1)} collective-permute-done((bf16[2,512,512]{2,1,0:T(8,128)(2,1)}, bf16[2,512,512]{2,1,0:T(8,128)(2,1)S(1)}, u32[]{:S(2)}, u32[]{:S(2)}) %collective-permute-start.6) | collective-permute-done | bytes 1048608 | tf_op jit(solution)/shard_map/ppermute | solution.py:270
  45.5 2.6 %collective-permute-start.14 = (bf16[128,256]{1,0:T(8,128)(2,1)}, bf16[128,256]{1,0:T(8,128)(2,1)S(1)}, u32[]{:S(2)}, u32[]{:S(2)}) collective-permute-start(bf16[128,256]{1,0:T(8,128)(2,1)} %pad_maximum_fusion.16), channel_id=1, source_target_pairs={{0,6},{2,4},{4,2},{6,0},{8,14},{10,12},{12,10},{14,8},{16,22},{18,... | collective-permute-start | bytes 196616 | tf_op jit(solution)/shard_map/ppermute | solution.py:270
  49.8 8.8 %collective-permute-done.9 = bf16[128,2048]{1,0:T(8,128)(2,1)S(1)} collective-permute-done((bf16[128,2048]{1,0:T(8,128)(2,1)S(1)}, bf16[128,2048]{1,0:T(8,128)(2,1)S(1)}, u32[]{:S(2)}, u32[]{:S(2)}) %collective-permute-start.9) | collective-permute-done | bytes 524320 | tf_op jit(solution)/shard_map/ppermute | solution.py:273
  58.6 4.3 %collective-permute-start.12 = (bf16[128,256]{1,0:T(8,128)(2,1)S(1)}, bf16[128,256]{1,0:T(8,128)(2,1)S(1)}, u32[]{:S(2)}, u32[]{:S(2)}) collective-permute-start(bf16[128,256]{1,0:T(8,128)(2,1)S(1)} %copy-done.35), channel_id=1, source_target_pairs={{0,2},{2,0},{4,6},{6,4},{8,10},{10,8},{12,14},{14,12},{16,18},{18,... | collective-permute-start | bytes 196616 | tf_op jit(solution)/shard_map/ppermute | solution.py:270
  66.9 7.8 %collective-permute-done.15 = bf16[4,128,256]{2,1,0:T(8,128)(2,1)S(1)} collective-permute-done((bf16[4,128,256]{2,1,0:T(8,128)(2,1)S(1)}, bf16[4,128,256]{2,1,0:T(8,128)(2,1)S(1)}, u32[]{:S(2)}, u32[]{:S(2)}) %collective-permute-start.15) | collective-permute-done | bytes 262176 | tf_op jit(solution)/shard_map/ppermute | solution.py:280
  80.1 3.7 %collective-permute-done.19 = bf16[64,2048]{1,0:T(8,128)(2,1)S(1)} collective-permute-done((bf16[64,2048]{1,0:T(8,128)(2,1)S(1)}, bf16[64,2048]{1,0:T(8,128)(2,1)S(1)}, u32[]{:S(2)}, u32[]{:S(2)}) %collective-permute-start.19) | collective-permute-done | bytes 262176 | tf_op jit(solution)/shard_map/ppermute | solution.py:270
  85.0 7.6 %collective-permute-done.17 = bf16[128,2048]{1,0:T(8,128)(2,1)S(1)} collective-permute-done((bf16[128,2048]{1,0:T(8,128)(2,1)S(1)}, bf16[128,2048]{1,0:T(8,128)(2,1)S(1)}, u32[]{:S(2)}, u32[]{:S(2)}) %collective-permute-start.17) | collective-permute-done | bytes 524320 | tf_op jit(solution)/shard_map/ppermute | solution.py:273
  99.3 9.6 %collective-permute-done.22 = bf16[128,2048]{1,0:T(8,128)(2,1)S(1)} collective-permute-done((bf16[128,2048]{1,0:T(8,128)(2,1)S(1)}, bf16[128,2048]{1,0:T(8,128)(2,1)S(1)}, u32[]{:S(2)}, u32[]{:S(2)}) %collective-permute-start.22) | collective-permute-done | bytes 524320 | tf_op jit(solution)/shard_map/ppermute | solution.py:273
  108.9 3.3 %collective-permute-start.26 = (bf16[4,128,256]{2,1,0:T(8,128)(2,1)S(1)}, bf16[4,128,256]{2,1,0:T(8,128)(2,1)S(1)}, u32[]{:S(2)}, u32[]{:S(2)}) collective-permute-start(bf16[4,128,256]{2,1,0:T(8,128)(2,1)S(1)} %broadcast_select_fusion.2), channel_id=1, source_target_pairs={{8,0},{10,2},{12,4},{14,6},{24,16},{26,18},{28,20},{30,22},{9,1},{... | collective-permute-start | bytes 786440 | tf_op jit(solution)/shard_map/ppermute | solution.py:280
  114.5 2.8 %shard_map.86 = bf16[512,512]{1,0:T(8,128)(2,1)} custom-call(s32[3]{0:T(128)S(1)} %pad_add_fusion.place_ref, bf16[512,2048]{1,0:T(8,128)(2,1)S(1)} %constant_dynamic-update-slice_fusion.6.x_ref, bf16[4096,512]{1,0:T(8,128)(2,1)S(1)} %copy-done, bf16[2,512,512]{2,1,0:T(8,128)(2,1)S(1)} %collective-permute-done.5.refs_1_, ...), custom_call_target="tpu_custom_call" | custom-call | flops 1073741824 | bytes 4718592 | tf_op jit(solution)/shard_map/pallas_call | solution.py:51
  117.9 2.1 shard_map.88
  120.0 2.1 %shard_map.89 = bf16[512,512]{1,0:T(8,128)(2,1)S(1)} custom-call(s32[3]{0:T(128)S(1)} %pad_add_fusion.place_ref, bf16[512,2048]{1,0:T(8,128)(2,1)S(1)} %pad_maximum_fusion.x_ref, bf16[4096,512]{1,0:T(8,128)(2,1)S(1)} %copy-done, bf16[2,512,512]{2,1,0:T(8,128)(2,1)S(1)} %collective-permute-done.30.refs_1_, ...), custom_call_target="tpu_custom_call" | custom-call | flops 1073741824 | bytes 4718592 | tf_op jit(solution)/shard_map/pallas_call | solution.py:51
  128.2 4.2 %collective-permute-done.28.refs_2_ = bf16[128,1024]{1,0:T(8,128)(2,1)} collective-permute-done((bf16[128,1024]{1,0:T(8,128)(2,1)}, bf16[128,1024]{1,0:T(8,128)(2,1)}, u32[]{:S(2)}, u32[]{:S(2)}) %collective-permute-start.28) | collective-permute-done | bytes 262176 | tf_op jit(solution)/shard_map/ppermute | solution.py:270
  132.5 4.4 %collective-permute-start.38 = (bf16[512,512]{1,0:T(8,128)(2,1)}, bf16[512,512]{1,0:T(8,128)(2,1)S(1)}, u32[]{:S(2)}, u32[]{:S(2)}) collective-permute-start(bf16[512,512]{1,0:T(8,128)(2,1)} %copy-done.10), channel_id=1, source_target_pairs={{8,0},{10,2},{12,4},{14,6},{16,8},{18,10},{20,12},{22,14},{24,16},... | collective-permute-start | bytes 1572872 | tf_op jit(solution)/shard_map/ppermute | solution.py:280
  140.9 2.2 %copy-done.1 = bf16[4096,512]{1,0:T(8,128)(2,1)S(1)} copy-done((bf16[4096,512]{1,0:T(8,128)(2,1)S(1)}, bf16[4096,512]{1,0:T(8,128)(2,1)}, u32[]{:S(2)}) %copy-start.1) | copy-done | bytes 4194328
  145.9 3.0 %shard_map.90 = bf16[512,512]{1,0:T(8,128)(2,1)S(1)} custom-call(s32[3]{0:T(128)S(1)} %pad_add_fusion.place_ref, bf16[512,2048]{1,0:T(8,128)(2,1)S(1)} %copy-done.7, bf16[4096,512]{1,0:T(8,128)(2,1)S(1)} %copy-done.1, bf16[2,512,512]{2,1,0:T(8,128)(2,1)S(1)} %copy-done.4, bf16[2,512,512]{2,1,0:T(8,128)(2,1)S(1)} %collective-permute-done.31.refs_2_.refs_3_, ...), custom_call_target="tpu_custom_call" | custom-call | flops 1073741824 | bytes 4718592 | tf_op jit(solution)/shard_map/pallas_call | solution.py:51
  149.0 2.3 %collective-permute-start.37 = (bf16[512,512]{1,0:T(8,128)(2,1)S(1)}, bf16[512,512]{1,0:T(8,128)(2,1)S(1)}, u32[]{:S(2)}, u32[]{:S(2)}) collective-permute-start(bf16[512,512]{1,0:T(8,128)(2,1)S(1)} %shard_map.90), channel_id=1, source_target_pairs={{0,16},{2,18},{4,20},{6,22},{8,24},{10,26},{12,28},{14,30},{16,0},... | collective-permute-start | bytes 1572872 | tf_op jit(solution)/shard_map/ppermute | solution.py:277
  152.8 2.1 %shard_map.92 = f32[512,512]{1,0:T(8,128)S(1)} custom-call(s32[3]{0:T(128)S(1)} %pad_add_fusion.place_ref, bf16[512,2048]{1,0:T(8,128)(2,1)S(1)} %pad_maximum_fusion.1.x_ref, bf16[4096,512]{1,0:T(8,128)(2,1)S(1)} %copy-done.2, bf16[2,512,512]{2,1,0:T(8,128)(2,1)S(1)} %collective-permute-done.5.refs_1_, ...), custom_call_target="tpu_custom_call" | custom-call | flops 1073741824 | bytes 4718592 | tf_op jit(solution)/shard_map/pallas_call | solution.py:51
  154.9 9.2 %shard_map.91.prob_ref = bf16[8,1024,512]{2,1,0:T(8,128)(2,1)S(1)} custom-call(s32[3]{0:T(128)S(1)} %pad_add_fusion.place_ref, bf16[4,128,256]{2,1,0:T(8,128)(2,1)S(1)} %pad_maximum_fusion.13.k_ref.v_ref, bf16[4,128,256]{2,1,0:T(8,128)(2,1)S(1)} %broadcast_select_fusion.1.kp_ref.vp_ref, bf16[128,1024]{1,0:T(8,128)(2,1)S(1)} %copy-done.8, ...), custom_call_target="tpu_custom_call" | custom-call | flops 1073741824 | bytes 8388608 | tf_op jit(solution)/shard_map/pallas_call | solution.py:115
  164.2 8.4 %shard_map.93 = (bf16[4,128,512]{2,1,0:T(8,128)(2,1)S(1)}, f32[1024,128]{1,0:T(8,128)S(1)}, f32[1024,128]{1,0:T(8,128)S(1)}) custom-call(s32[3]{0:T(128)S(1)} %pad_add_fusion.place_ref, bf16[8,1024,512]{2,1,0:T(8,128)(2,1)S(1)} %shard_map.91.prob_ref, bf16[4,128,256]{2,1,0:T(8,128)(2,1)S(1)} %pad_maximum_fusion.13.k_ref.v_ref, ...), custom_call_target="tpu_custom_call" | custom-call | flops 2147483648 | bytes 4194304 | tf_op jit(solution)/shard_map/pallas_call | solution.py:214
  174.9 2.1 %shard_map.94 = f32[512,512]{1,0:T(8,128)S(1)} custom-call(s32[3]{0:T(128)S(1)} %pad_add_fusion.place_ref, bf16[512,2048]{1,0:T(8,128)(2,1)S(1)} %pad_maximum_fusion.1.x_ref, bf16[4096,512]{1,0:T(8,128)(2,1)S(1)} %copy-done.2, bf16[2,512,512]{2,1,0:T(8,128)(2,1)S(1)} %copy-done.5, bf16[2,512,512]{2,1,0:T(8,128)(2,1)S(1)} %collective-permute-done.31.refs_2_.refs_3_, ...), custom_call_target="tpu_custom_call" | custom-call | flops 1073741824 | bytes 4718592 | tf_op jit(solution)/shard_map/pallas_call | solution.py:51
  177.5 8.2 %shard_map.95 = (bf16[4,128,512]{2,1,0:T(8,128)(2,1)S(1)}, f32[1024,128]{1,0:T(8,128)S(1)}, f32[1024,128]{1,0:T(8,128)S(1)}) custom-call(s32[3]{0:T(128)S(1)} %pad_add_fusion.place_ref, bf16[8,1024,512]{2,1,0:T(8,128)(2,1)S(1)} %shard_map.91.prob_ref, bf16[4,128,256]{2,1,0:T(8,128)(2,1)S(1)} %pad_maximum_fusion.13.k_ref.v_ref, ...), custom_call_target="tpu_custom_call" | custom-call | flops 2147483648 | bytes 4194304 | tf_op jit(solution)/shard_map/pallas_call | solution.py:214
  189.7 2.5 %collective-permute-done.40 = bf16[128,512]{1,0:T(8,128)(2,1)S(1)} collective-permute-done((bf16[128,512]{1,0:T(8,128)(2,1)S(1)}, bf16[128,512]{1,0:T(8,128)(2,1)S(1)}, u32[]{:S(2)}, u32[]{:S(2)}) %collective-permute-start.40) | collective-permute-done | bytes 131104 | tf_op jit(solution)/shard_map/ppermute | solution.py:270
  192.2 3.6 %collective-permute-done.42 = bf16[512,256]{1,0:T(8,128)(2,1)S(1)} collective-permute-done((bf16[512,256]{1,0:T(8,128)(2,1)S(1)}, bf16[512,256]{1,0:T(8,128)(2,1)S(1)}, u32[]{:S(2)}, u32[]{:S(2)}) %collective-permute-start.42) | collective-permute-done | bytes 262176 | tf_op jit(solution)/shard_map/ppermute | solution.py:280
  196.0 2.4 %collective-permute-start.43 = (bf16[128,256]{1,0:T(8,128)(2,1)S(1)}, bf16[128,256]{1,0:T(8,128)(2,1)S(1)}, u32[]{:S(2)}, u32[]{:S(2)}) collective-permute-start(bf16[128,256]{1,0:T(8,128)(2,1)S(1)} %get-tuple-element.124), channel_id=1, source_target_pairs={{8,24},{10,26},{12,28},{14,30},{9,25},{11,27},{13,29},{15,31}} | collective-permute-start | bytes 196616 | tf_op jit(solution)/shard_map/ppermute | solution.py:557
  198.4 2.2 %collective-permute-start.45 = (bf16[128,256]{1,0:T(8,128)(2,1)S(1)}, bf16[128,256]{1,0:T(8,128)(2,1)S(1)}, u32[]{:S(2)}, u32[]{:S(2)}) collective-permute-start(bf16[128,256]{1,0:T(8,128)(2,1)S(1)} %get-tuple-element.123), channel_id=1, source_target_pairs={{8,26},{10,24},{12,30},{14,28},{9,27},{11,25},{13,31},{15,29}} | collective-permute-start | bytes 196616 | tf_op jit(solution)/shard_map/ppermute | solution.py:557
  (222 shorter events, 70.8 us)
Async XLA Ops:
  4.8 10.1 %collective-permute-start.5 = (bf16[2,512,512]{2,1,0:T(8,128)(2,1)}, bf16[2,512,512]{2,1,0:T(8,128)(2,1)S(1)}, u32[]{:S(2)}, u32[]{:S(2)}) collective-permute-start(bf16[2,512,512]{2,1,0:T(8,128)(2,1)} %pad_maximum_fusion.2), channel_id=1, source_target_pairs={{0,2},{2,0},{4,6},{6,4},{8,10},{10,8},{12,14},{14,12},{16,18},{18,... | collective-permute-start | bytes 3145736 | tf_op jit(solution)/shard_map/ppermute | solution.py:270
  9.0 115.5 %collective-permute-start.27 = (bf16[128,1024]{1,0:T(8,128)(2,1)}, bf16[128,1024]{1,0:T(8,128)(2,1)}, u32[]{:S(2)}, u32[]{:S(2)}) collective-permute-start(bf16[128,1024]{1,0:T(8,128)(2,1)} %get-tuple-element.111), channel_id=1, source_target_pairs={{0,2},{2,0},{4,6},{6,4},{8,10},{10,8},{12,14},{14,12},{16,18},{18,... | collective-permute-start | bytes 786440 | tf_op jit(solution)/shard_map/ppermute | solution.py:270
  17.1 23.2 %collective-permute-start.6 = (bf16[2,512,512]{2,1,0:T(8,128)(2,1)}, bf16[2,512,512]{2,1,0:T(8,128)(2,1)S(1)}, u32[]{:S(2)}, u32[]{:S(2)}) collective-permute-start(bf16[2,512,512]{2,1,0:T(8,128)(2,1)} %pad_maximum_fusion.3), channel_id=1, source_target_pairs={{0,4},{2,6},{4,0},{6,2},{8,12},{10,14},{12,8},{14,10},{16,20},{18,... | collective-permute-start | bytes 3145736 | tf_op jit(solution)/shard_map/ppermute | solution.py:270
  21.6 13.0 %collective-permute-start.3 = (bf16[64,2048]{1,0:T(8,128)(2,1)S(1)}, bf16[64,2048]{1,0:T(8,128)(2,1)}, u32[]{:S(2)}, u32[]{:S(2)}) collective-permute-start(bf16[64,2048]{1,0:T(8,128)(2,1)S(1)} %get-tuple-element.107), channel_id=1, source_target_pairs={{0,8},{2,10},{4,12},{6,14},{8,16},{10,18},{12,20},{14,22},{16,24},... | collective-permute-start | bytes 786440 | tf_op jit(solution)/shard_map/ppermute | solution.py:277
  34.5 10.9 %collective-permute-start.4 = (bf16[64,2048]{1,0:T(8,128)(2,1)}, bf16[64,2048]{1,0:T(8,128)(2,1)S(1)}, u32[]{:S(2)}, u32[]{:S(2)}) collective-permute-start(bf16[64,2048]{1,0:T(8,128)(2,1)} %get-tuple-element.50), channel_id=1, source_target_pairs={{0,16},{2,18},{4,20},{6,22},{8,24},{10,26},{12,28},{14,30},{16,0},... | collective-permute-start | bytes 786440 | tf_op jit(solution)/shard_map/ppermute | solution.py:277
  41.6 21.3 %collective-permute-start.13 = (bf16[128,256]{1,0:T(8,128)(2,1)}, bf16[128,256]{1,0:T(8,128)(2,1)S(1)}, u32[]{:S(2)}, u32[]{:S(2)}) collective-permute-start(bf16[128,256]{1,0:T(8,128)(2,1)} %pad_maximum_fusion.15), channel_id=1, source_target_pairs={{0,4},{2,6},{4,0},{6,2},{8,12},{10,14},{12,8},{14,10},{16,20},{18,... | collective-permute-start | bytes 196616 | tf_op jit(solution)/shard_map/ppermute | solution.py:270
  45.5 17.6 %collective-permute-start.14 = (bf16[128,256]{1,0:T(8,128)(2,1)}, bf16[128,256]{1,0:T(8,128)(2,1)S(1)}, u32[]{:S(2)}, u32[]{:S(2)}) collective-permute-start(bf16[128,256]{1,0:T(8,128)(2,1)} %pad_maximum_fusion.16), channel_id=1, source_target_pairs={{0,6},{2,4},{4,2},{6,0},{8,14},{10,12},{12,10},{14,8},{16,22},{18,... | collective-permute-start | bytes 196616 | tf_op jit(solution)/shard_map/ppermute | solution.py:270
  48.2 10.4 %collective-permute-start.9 = (bf16[128,2048]{1,0:T(8,128)(2,1)S(1)}, bf16[128,2048]{1,0:T(8,128)(2,1)S(1)}, u32[]{:S(2)}, u32[]{:S(2)}) collective-permute-start(bf16[128,2048]{1,0:T(8,128)(2,1)S(1)} %pad_maximum_fusion.10), channel_id=1, source_target_pairs={{0,1},{1,0},{2,3},{3,2},{4,5},{5,4},{6,7},{7,6},{8,9},{9,8},{10,11... | collective-permute-start | bytes 1572872 | tf_op jit(solution)/shard_map/ppermute | solution.py:273
  49.5 14.3 %collective-permute-start.10 = (bf16[128,2048]{1,0:T(8,128)(2,1)S(1)}, bf16[128,2048]{1,0:T(8,128)(2,1)S(1)}, u32[]{:S(2)}, u32[]{:S(2)}) collective-permute-start(bf16[128,2048]{1,0:T(8,128)(2,1)S(1)} %constant_dynamic-update-slice_fusion), channel_id=1, source_target_pairs={{0,4},{2,6},{4,0},{6,2},{8,12},{10,14},{12,8},{14,10},{16,20},{18,... | collective-permute-start | bytes 1572872 | tf_op jit(solution)/shard_map/ppermute | solution.py:270
  63.0 16.8 %collective-permute-start.30 = (bf16[2,512,512]{2,1,0:T(8,128)(2,1)S(1)}, bf16[2,512,512]{2,1,0:T(8,128)(2,1)S(1)}, u32[]{:S(2)}, u32[]{:S(2)}) collective-permute-start(bf16[2,512,512]{2,1,0:T(8,128)(2,1)S(1)} %copy-done.27), channel_id=1, source_target_pairs={{0,2},{2,0},{4,6},{6,4},{8,10},{10,8},{12,14},{14,12},{16,18},{18,... | collective-permute-start | bytes 3145736 | tf_op jit(solution)/shard_map/ppermute | solution.py:270
  63.8 13.3 %collective-permute-start.16 = (bf16[256,2048]{1,0:T(8,128)(2,1)S(1)}, bf16[256,2048]{1,0:T(8,128)(2,1)S(1)}, u32[]{:S(2)}, u32[]{:S(2)}) collective-permute-start(bf16[256,2048]{1,0:T(8,128)(2,1)S(1)} %pad_maximum_fusion.4), channel_id=1, source_target_pairs={{0,2},{2,0},{4,6},{6,4},{8,10},{10,8},{12,14},{14,12},{16,18},{18,... | collective-permute-start | bytes 3145736 | tf_op jit(solution)/shard_map/ppermute | solution.py:270
  64.2 10.6 %collective-permute-start.15 = (bf16[4,128,256]{2,1,0:T(8,128)(2,1)S(1)}, bf16[4,128,256]{2,1,0:T(8,128)(2,1)S(1)}, u32[]{:S(2)}, u32[]{:S(2)}) collective-permute-start(bf16[4,128,256]{2,1,0:T(8,128)(2,1)S(1)} %pad_maximum_fusion.13.k_ref.v_ref), channel_id=1, source_target_pairs={{24,8},{26,10},{28,12},{30,14},{25,9},{27,11},{29,13},{31,15}} | collective-permute-start | bytes 786440 | tf_op jit(solution)/shard_map/ppermute | solution.py:280
  65.5 10.3 %collective-permute-start.11 = (bf16[64,2048]{1,0:T(8,128)(2,1)S(1)}, bf16[64,2048]{1,0:T(8,128)(2,1)S(1)}, u32[]{:S(2)}, u32[]{:S(2)}) collective-permute-start(bf16[64,2048]{1,0:T(8,128)(2,1)S(1)} %collective-permute-done.4), channel_id=1, source_target_pairs={{0,4},{2,6},{4,0},{6,2},{8,12},{10,14},{12,8},{14,10},{16,20},{18,... | collective-permute-start | bytes 786440 | tf_op jit(solution)/shard_map/ppermute | solution.py:270
  74.7 20.3 %collective-permute-start.23 = (bf16[256,2048]{1,0:T(8,128)(2,1)S(1)}, bf16[256,2048]{1,0:T(8,128)(2,1)S(1)}, u32[]{:S(2)}, u32[]{:S(2)}) collective-permute-start(bf16[256,2048]{1,0:T(8,128)(2,1)S(1)} %bitcast.59), channel_id=1, source_target_pairs={{0,2},{2,0},{4,6},{6,4},{8,10},{10,8},{12,14},{14,12},{16,18},{18,... | collective-permute-start | bytes 3145736 | tf_op jit(solution)/shard_map/ppermute | solution.py:270
  79.4 13.3 %collective-permute-start.17 = (bf16[128,2048]{1,0:T(8,128)(2,1)S(1)}, bf16[128,2048]{1,0:T(8,128)(2,1)S(1)}, u32[]{:S(2)}, u32[]{:S(2)}) collective-permute-start(bf16[128,2048]{1,0:T(8,128)(2,1)S(1)} %pad_maximum_fusion.11), channel_id=1, source_target_pairs={{0,1},{1,0},{2,3},{3,2},{4,5},{5,4},{6,7},{7,6},{8,9},{9,8},{10,11... | collective-permute-start | bytes 1572872 | tf_op jit(solution)/shard_map/ppermute | solution.py:273
  79.9 13.0 %collective-permute-start.18 = (bf16[512,512]{1,0:T(8,128)(2,1)S(1)}, bf16[512,512]{1,0:T(8,128)(2,1)S(1)}, u32[]{:S(2)}, u32[]{:S(2)}) collective-permute-start(bf16[512,512]{1,0:T(8,128)(2,1)S(1)} %shard_map.85), channel_id=1, source_target_pairs={{0,8},{2,10},{4,12},{6,14},{8,16},{10,18},{12,20},{14,22},{16,24},... | collective-permute-start | bytes 1572872 | tf_op jit(solution)/shard_map/ppermute | solution.py:277
  83.7 34.2 %collective-permute-start.31 = (bf16[2,512,512]{2,1,0:T(8,128)(2,1)S(1)}, bf16[2,512,512]{2,1,0:T(8,128)(2,1)S(1)}, u32[]{:S(2)}, u32[]{:S(2)}) collective-permute-start(bf16[2,512,512]{2,1,0:T(8,128)(2,1)S(1)} %pad_maximum_fusion.9), channel_id=1, source_target_pairs={{0,4},{2,6},{4,0},{6,2},{8,12},{10,14},{12,8},{14,10},{16,20},{18,... | collective-permute-start | bytes 3145736 | tf_op jit(solution)/shard_map/ppermute | solution.py:270
  93.6 20.8 %collective-permute-start.20 = (bf16[256,2048]{1,0:T(8,128)(2,1)S(1)}, bf16[256,2048]{1,0:T(8,128)(2,1)S(1)}, u32[]{:S(2)}, u32[]{:S(2)}) collective-permute-start(bf16[256,2048]{1,0:T(8,128)(2,1)S(1)} %pad_maximum_fusion.5), channel_id=1, source_target_pairs={{0,2},{2,0},{4,6},{6,4},{8,10},{10,8},{12,14},{14,12},{16,18},{18,... | collective-permute-start | bytes 3145736 | tf_op jit(solution)/shard_map/ppermute | solution.py:270
  95.3 13.6 %collective-permute-start.22 = (bf16[128,2048]{1,0:T(8,128)(2,1)S(1)}, bf16[128,2048]{1,0:T(8,128)(2,1)S(1)}, u32[]{:S(2)}, u32[]{:S(2)}) collective-permute-start(bf16[128,2048]{1,0:T(8,128)(2,1)S(1)} %pad_maximum_fusion.12), channel_id=1, source_target_pairs={{0,1},{1,0},{2,3},{3,2},{4,5},{5,4},{6,7},{7,6},{8,9},{9,8},{10,11... | collective-permute-start | bytes 1572872 | tf_op jit(solution)/shard_map/ppermute | solution.py:273
  98.6 14.8 %collective-permute-start.24 = (bf16[512,512]{1,0:T(8,128)(2,1)S(1)}, bf16[512,512]{1,0:T(8,128)(2,1)S(1)}, u32[]{:S(2)}, u32[]{:S(2)}) collective-permute-start(bf16[512,512]{1,0:T(8,128)(2,1)S(1)} %shard_map.87), channel_id=1, source_target_pairs={{0,24},{2,26},{4,28},{6,30},{8,0},{10,2},{12,4},{14,6},{16,8},{18,... | collective-permute-start | bytes 1572872 | tf_op jit(solution)/shard_map/ppermute | solution.py:277
  108.9 16.3 %collective-permute-start.26 = (bf16[4,128,256]{2,1,0:T(8,128)(2,1)S(1)}, bf16[4,128,256]{2,1,0:T(8,128)(2,1)S(1)}, u32[]{:S(2)}, u32[]{:S(2)}) collective-permute-start(bf16[4,128,256]{2,1,0:T(8,128)(2,1)S(1)} %broadcast_select_fusion.2), channel_id=1, source_target_pairs={{8,0},{10,2},{12,4},{14,6},{24,16},{26,18},{28,20},{30,22},{9,1},{... | collective-permute-start | bytes 786440 | tf_op jit(solution)/shard_map/ppermute | solution.py:280
  113.3 27.5 %collective-permute-start.25 = (bf16[256,2048]{1,0:T(8,128)(2,1)}, bf16[256,2048]{1,0:T(8,128)(2,1)}, u32[]{:S(2)}, u32[]{:S(2)}) collective-permute-start(bf16[256,2048]{1,0:T(8,128)(2,1)} %pad_maximum_fusion.6), channel_id=1, source_target_pairs={{0,2},{2,0},{4,6},{6,4},{8,10},{10,8},{12,14},{14,12},{16,18},{18,... | collective-permute-start | bytes 3145736 | tf_op jit(solution)/shard_map/ppermute | solution.py:270
  117.4 23.5 %collective-permute-start.21 = (bf16[512,512]{1,0:T(8,128)(2,1)}, bf16[512,512]{1,0:T(8,128)(2,1)}, u32[]{:S(2)}, u32[]{:S(2)}) collective-permute-start(bf16[512,512]{1,0:T(8,128)(2,1)} %shard_map.86), channel_id=1, source_target_pairs={{0,16},{2,18},{4,20},{6,22},{8,24},{10,26},{12,28},{14,30},{16,0},... | collective-permute-start | bytes 1572872 | tf_op jit(solution)/shard_map/ppermute | solution.py:277
  123.2 17.7 %collective-permute-start.32 = (bf16[512,512]{1,0:T(8,128)(2,1)}, bf16[512,512]{1,0:T(8,128)(2,1)}, u32[]{:S(2)}, u32[]{:S(2)}) collective-permute-start(bf16[512,512]{1,0:T(8,128)(2,1)} %broadcast_select_fusion), channel_id=1, source_target_pairs={{0,8},{2,10},{4,12},{6,14},{24,16},{26,18},{28,20},{30,22},{1,9},{... | collective-permute-start | bytes 1572872 | tf_op jit(solution)/shard_map/ppermute | solution.py:280
  126.0 12.8 %collective-permute-start.29 = (bf16[128,1024]{1,0:T(8,128)(2,1)}, bf16[128,1024]{1,0:T(8,128)(2,1)}, u32[]{:S(2)}, u32[]{:S(2)}) collective-permute-start(bf16[128,1024]{1,0:T(8,128)(2,1)} %get-tuple-element.112), channel_id=1, source_target_pairs={{0,6},{2,4},{4,2},{6,0},{8,14},{10,12},{12,10},{14,8},{16,22},{18,... | collective-permute-start | bytes 786440 | tf_op jit(solution)/shard_map/ppermute | solution.py:270
  132.5 44.5 %collective-permute-start.38 = (bf16[512,512]{1,0:T(8,128)(2,1)}, bf16[512,512]{1,0:T(8,128)(2,1)S(1)}, u32[]{:S(2)}, u32[]{:S(2)}) collective-permute-start(bf16[512,512]{1,0:T(8,128)(2,1)} %copy-done.10), channel_id=1, source_target_pairs={{8,0},{10,2},{12,4},{14,6},{16,8},{18,10},{20,12},{22,14},{24,16},... | collective-permute-start | bytes 1572872 | tf_op jit(solution)/shard_map/ppermute | solution.py:280
  138.8 38.7 %collective-permute-start.36 = (bf16[512,512]{1,0:T(8,128)(2,1)}, bf16[512,512]{1,0:T(8,128)(2,1)S(1)}, u32[]{:S(2)}, u32[]{:S(2)}) collective-permute-start(bf16[512,512]{1,0:T(8,128)(2,1)} %copy-done.9), channel_id=1, source_target_pairs={{0,8},{2,10},{4,12},{6,14},{8,16},{10,18},{12,20},{14,22},{16,24},... | collective-permute-start | bytes 1572872 | tf_op jit(solution)/shard_map/ppermute | solution.py:280
  149.0 28.5 %collective-permute-start.37 = (bf16[512,512]{1,0:T(8,128)(2,1)S(1)}, bf16[512,512]{1,0:T(8,128)(2,1)S(1)}, u32[]{:S(2)}, u32[]{:S(2)}) collective-permute-start(bf16[512,512]{1,0:T(8,128)(2,1)S(1)} %shard_map.90), channel_id=1, source_target_pairs={{0,16},{2,18},{4,20},{6,22},{8,24},{10,26},{12,28},{14,30},{16,0},... | collective-permute-start | bytes 1572872 | tf_op jit(solution)/shard_map/ppermute | solution.py:277
  172.6 14.6 %collective-permute-start.33 = (bf16[128,512]{1,0:T(8,128)(2,1)S(1)}, bf16[128,512]{1,0:T(8,128)(2,1)S(1)}, u32[]{:S(2)}, u32[]{:S(2)}) collective-permute-start(bf16[128,512]{1,0:T(8,128)(2,1)S(1)} %get-tuple-element.119), channel_id=1, source_target_pairs={{0,2},{2,0},{4,6},{6,4},{8,10},{10,8},{12,14},{14,12},{16,18},{18,... | collective-permute-start | bytes 393224 | tf_op jit(solution)/shard_map/ppermute | solution.py:270
  173.6 13.6 %collective-permute-start.34 = (bf16[128,512]{1,0:T(8,128)(2,1)S(1)}, bf16[128,512]{1,0:T(8,128)(2,1)S(1)}, u32[]{:S(2)}, u32[]{:S(2)}) collective-permute-start(bf16[128,512]{1,0:T(8,128)(2,1)S(1)} %get-tuple-element.118), channel_id=1, source_target_pairs={{0,4},{2,6},{4,0},{6,2},{8,12},{10,14},{12,8},{14,10},{16,20},{18,... | collective-permute-start | bytes 393224 | tf_op jit(solution)/shard_map/ppermute | solution.py:270
  177.0 10.2 %collective-permute-start.35 = (bf16[128,512]{1,0:T(8,128)(2,1)S(1)}, bf16[128,512]{1,0:T(8,128)(2,1)S(1)}, u32[]{:S(2)}, u32[]{:S(2)}) collective-permute-start(bf16[128,512]{1,0:T(8,128)(2,1)S(1)} %get-tuple-element.117), channel_id=1, source_target_pairs={{0,6},{2,4},{4,2},{6,0},{8,14},{10,12},{12,10},{14,8},{16,22},{18,... | collective-permute-start | bytes 393224 | tf_op jit(solution)/shard_map/ppermute | solution.py:270
  188.7 15.5 %collective-permute-start.41 = (bf16[128,512]{1,0:T(8,128)(2,1)S(1)}, bf16[128,512]{1,0:T(8,128)(2,1)S(1)}, u32[]{:S(2)}, u32[]{:S(2)}) collective-permute-start(bf16[128,512]{1,0:T(8,128)(2,1)S(1)} %get-tuple-element.114), channel_id=1, source_target_pairs={{0,6},{2,4},{4,2},{6,0},{8,14},{10,12},{12,10},{14,8},{16,22},{18,... | collective-permute-start | bytes 393224 | tf_op jit(solution)/shard_map/ppermute | solution.py:270
  (55 other events, 527.2 us)

commit v4 on v3

--- a/solution.py
+++ b/solution.py
@@ -176,30 +176,30 @@
                 total = total + ref[at].astype(jnp.float32)
             grads[pl.ds(b * BLOCK + i * piece, piece), :] = total.astype(jnp.bfloat16)
 
-    for pair in range(2):
-        start = pair * half
-        q = queries[pl.ds(start, half), :]
-        g = grads[pl.ds(start, half), :]
-        chunks = [pl.ds(row, half) for row in reversed(range(start, 2 * own, half))]
-        lows = [prob_ref[0, rows, pl.ds(start, half)] for rows in chunks]
-        dprobs = [
-            lax.dot_general(values[rows, :], g, NT, preferred_element_type=jnp.float32)
-            for rows in chunks
-        ]
-        delta = sum(
-            jnp.sum(low.astype(jnp.float32) * dprob, axis=0, keepdims=True)
-            for low, dprob in zip(lows, dprobs)
-        )
-        gq = None
-        for rows, low, dprob in zip(chunks, lows, dprobs):
-            dscore = (low.astype(jnp.float32) * (dprob - delta)).astype(jnp.bfloat16)
-            dv_ref[rows, :] += jnp.dot(low, g, preferred_element_type=jnp.float32)
-            dk_ref[rows, :] += jnp.dot(dscore, q, preferred_element_type=jnp.float32) * SCALE
-            term = jnp.dot(keys_t[:, rows], dscore, preferred_element_type=jnp.float32)
-            gq = term if gq is None else gq + term
-        gq = (gq * SCALE).T.astype(jnp.bfloat16)
-        for b in range(QUAD // 2):
-            gq_ref[(pair * (QUAD // 2) + b) ^ mine] = gq[b * BLOCK : (b + 1) * BLOCK]
+    q, g = queries[...], grads[...]
+    chunks = [(pl.ds(row, half), own if row else half) for row in reversed(range(0, 2 * own, half))]
+    lows = [prob_ref[0, rows, pl.ds(0, width)] for rows, width in chunks]
+    dprobs = [
+        lax.dot_general(values[rows, :], g[:width], NT, preferred_element_type=jnp.float32)
+        for rows, width in chunks
+    ]
+    sums = [
+        jnp.sum(low.astype(jnp.float32) * dprob, axis=0, keepdims=True)
+        for low, dprob in zip(lows, dprobs)
+    ]
+    delta = functools.reduce(jnp.add, sums[:-1])
+    delta = jnp.concatenate([delta[:, :half] + sums[-1], delta[:, half:]], axis=1)
+    terms = []
+    for (rows, width), low, dprob in zip(chunks, lows, dprobs):
+        dscore = (low.astype(jnp.float32) * (dprob - delta[:, :width])).astype(jnp.bfloat16)
+        dv_ref[rows, :] += jnp.dot(low, g[:width], preferred_element_type=jnp.float32)
+        dk_ref[rows, :] += jnp.dot(dscore, q[:width], preferred_element_type=jnp.float32) * SCALE
+        terms.append(jnp.dot(keys_t[:, rows], dscore, preferred_element_type=jnp.float32))
+    gq = functools.reduce(jnp.add, terms[:-1])
+    gq = jnp.concatenate([gq[:, :half] + terms[-1], gq[:, half:]], axis=1)
+    gq = (gq * SCALE).T.astype(jnp.bfloat16)
+    for b in range(QUAD):
+        gq_ref[b ^ mine] = gq[b * BLOCK : (b + 1) * BLOCK]
 
 
 def attend(place, prob, queries, keyval, prefix, partials, base, heads, head_bits, before=()):

time: 212 us -> 212 us (level)
  no operation moved by 1% of the time
where the time goes in v4:
time: 212 us; the launch traced here: 211 us
  waiting for transfers between devices  73.7 us (35%)
  starting transfers between devices  61 us (29%)
  Pallas kernels  44.4 us (21%)
  local copies, waits for them, and re-layouts  15.3 us (7%)
  other arithmetic  14.3 us (7%)
  between operations  2.31 us (1%)
    ppermute x6, waiting for transfers between devices, flip(): return lax.ppermute(x, 'head', [(s, s ^ bits) for s in range(sides)])  29.7 us
    ppermute x27, starting transfers between devices, swap(): return lax.ppermute(x, 'ctx', [(c, c ^ bits) for c in range(places)])  28.3 us
    ppermute x27, waiting for transfers between devices, swap(): return lax.ppermute(x, 'ctx', [(c, c ^ bits) for c in range(places)])  22.3 us
    pallas_call x8, Pallas kernels, project(): pl.pallas_call(project_kernel, grid_spec=pltpu.PrefetchScalarGridSpec(num...  18.5 us
    pallas_call x2, Pallas kernels, attend(): pl.pallas_call(functools.partial(attend_kernel, head_bits, len(partials))...  16.7 us
    ppermute x6, starting transfers between devices, hop(): lax.ppermute(x, 'ctx', [(s * QUAD + i, t * QUAD + i) for s, t in pairs fo...  13.6 us
    ppermute x6, waiting for transfers between devices, hop(): lax.ppermute(x, 'ctx', [(s * QUAD + i, t * QUAD + i) for s, t in pairs fo...  11.4 us
    ppermute x7, waiting for transfers between devices, rotate(): lax.ppermute(x, 'ctx', [(c, (c + shift) % places) for c in range(places)])  10.3 us
  transfers between devices with their start and end apart: 50, of which 19 were waited for; matrix products, arithmetic and copies ran while one was open for 8% of the time, Pallas kernels for 21%

profile of v4, /device:TPU:9, one launch (start us, length us, event | category | flops | bytes accessed | tf_op | source)
XLA Modules:
  0.0 211.0 jit_solution(3277764597435752972)
XLA Ops:
  0.7 3.1 %dynamic-slice_bitcast_fusion = (bf16[1,512,512]{2,1,0:T(8,128)(2,1)}, bf16[1,512,512]{2,1,0:T(8,128)(2,1)S(1)}, bf16[1,512,512]{2,1,0:T(8,128)(2,1)}, bf16[1,51...) fusion(bf16[4096,512]{1,0:T(8,128)(2,1)} %refs_0_.15, s32[]{:T(128)S(6)} %select_n.306, ...), kind=kLoop, calls=%fused_computation.16 | loop fusion | bytes 6291480 | tf_op jit(solution)/shard_map/stack | solution.py:378
  6.8 2.2 %constant_dynamic-slice_fusion.8 = (bf16[128,1024]{1,0:T(8,128)(2,1)}, bf16[128,1024]{1,0:T(8,128)(2,1)}, bf16[128,1024]{1,0:T(8,128)(2,1)}, bf16[128,1024]{1,0:T(8,128)(2,1)}) fusion(bf16[128,4096]{1,0:T(8,128)(2,1)} %param.6, s32[]{:T(128)S(6)} %select_n.309, s32[]{:T(128)S(6)} %select_n.281, s32[]{:T(128)S(6)} %select_n.282, s32[]{:T(128)S(6)} %select_n.283), kind=kLoop, calls=%fused_computation.83 | loop fusion | bytes 2097168 | tf_op jit(solution)/shard_map/dynamic_slice | solution.py:285
  9.8 3.1 %collective-permute-done = bf16[64,2048]{1,0:T(8,128)(2,1)S(1)} collective-permute-done((bf16[64,2048]{1,0:T(8,128)(2,1)S(1)}, bf16[64,2048]{1,0:T(8,128)(2,1)S(1)}, u32[]{:S(2)}, u32[]{:S(2)}) %collective-permute-start) | collective-permute-done | bytes 262176 | tf_op jit(solution)/shard_map/ppermute | solution.py:273
  15.0 2.1 %pad_maximum_fusion.3 = bf16[2,512,512]{2,1,0:T(8,128)(2,1)} fusion(bf16[1,512,512]{2,1,0:T(8,128)(2,1)S(1)} %slice.48, bf16[1,512,512]{2,1,0:T(8,128)(2,1)} %get-tuple-element.102), kind=kLoop, calls=%fused_computation.3 | loop fusion | flops 524288 | bytes 2097152 | tf_op jit(solution)/shard_map/stack | solution.py:378
  24.3 2.1 pad_maximum_fusion.8
  26.7 7.8 %collective-permute-done.3 = bf16[64,2048]{1,0:T(8,128)(2,1)} collective-permute-done((bf16[64,2048]{1,0:T(8,128)(2,1)S(1)}, bf16[64,2048]{1,0:T(8,128)(2,1)}, u32[]{:S(2)}, u32[]{:S(2)}) %collective-permute-start.3) | collective-permute-done | bytes 262176 | tf_op jit(solution)/shard_map/ppermute | solution.py:277
  34.5 5.8 %collective-permute-done.6.refs_2_.refs_3_ = bf16[2,512,512]{2,1,0:T(8,128)(2,1)S(1)} collective-permute-done((bf16[2,512,512]{2,1,0:T(8,128)(2,1)}, bf16[2,512,512]{2,1,0:T(8,128)(2,1)S(1)}, u32[]{:S(2)}, u32[]{:S(2)}) %collective-permute-start.6) | collective-permute-done | bytes 1048608 | tf_op jit(solution)/shard_map/ppermute | solution.py:270
  45.5 2.6 %collective-permute-start.14 = (bf16[128,256]{1,0:T(8,128)(2,1)}, bf16[128,256]{1,0:T(8,128)(2,1)S(1)}, u32[]{:S(2)}, u32[]{:S(2)}) collective-permute-start(bf16[128,256]{1,0:T(8,128)(2,1)} %pad_maximum_fusion.16), channel_id=1, source_target_pairs={{0,6},{2,4},{4,2},{6,0},{8,14},{10,12},{12,10},{14,8},{16,22},{18,... | collective-permute-start | bytes 196616 | tf_op jit(solution)/shard_map/ppermute | solution.py:270
  49.8 8.8 %collective-permute-done.9 = bf16[128,2048]{1,0:T(8,128)(2,1)S(1)} collective-permute-done((bf16[128,2048]{1,0:T(8,128)(2,1)S(1)}, bf16[128,2048]{1,0:T(8,128)(2,1)S(1)}, u32[]{:S(2)}, u32[]{:S(2)}) %collective-permute-start.9) | collective-permute-done | bytes 524320 | tf_op jit(solution)/shard_map/ppermute | solution.py:273
  58.6 4.3 %collective-permute-start.12 = (bf16[128,256]{1,0:T(8,128)(2,1)S(1)}, bf16[128,256]{1,0:T(8,128)(2,1)S(1)}, u32[]{:S(2)}, u32[]{:S(2)}) collective-permute-start(bf16[128,256]{1,0:T(8,128)(2,1)S(1)} %copy-done.35), channel_id=1, source_target_pairs={{0,2},{2,0},{4,6},{6,4},{8,10},{10,8},{12,14},{14,12},{16,18},{18,... | collective-permute-start | bytes 196616 | tf_op jit(solution)/shard_map/ppermute | solution.py:270
  66.9 7.8 %collective-permute-done.15 = bf16[4,128,256]{2,1,0:T(8,128)(2,1)S(1)} collective-permute-done((bf16[4,128,256]{2,1,0:T(8,128)(2,1)S(1)}, bf16[4,128,256]{2,1,0:T(8,128)(2,1)S(1)}, u32[]{:S(2)}, u32[]{:S(2)}) %collective-permute-start.15) | collective-permute-done | bytes 262176 | tf_op jit(solution)/shard_map/ppermute | solution.py:280
  80.1 3.7 %collective-permute-done.19 = bf16[64,2048]{1,0:T(8,128)(2,1)S(1)} collective-permute-done((bf16[64,2048]{1,0:T(8,128)(2,1)S(1)}, bf16[64,2048]{1,0:T(8,128)(2,1)S(1)}, u32[]{:S(2)}, u32[]{:S(2)}) %collective-permute-start.19) | collective-permute-done | bytes 262176 | tf_op jit(solution)/shard_map/ppermute | solution.py:270
  85.0 7.6 %collective-permute-done.17 = bf16[128,2048]{1,0:T(8,128)(2,1)S(1)} collective-permute-done((bf16[128,2048]{1,0:T(8,128)(2,1)S(1)}, bf16[128,2048]{1,0:T(8,128)(2,1)S(1)}, u32[]{:S(2)}, u32[]{:S(2)}) %collective-permute-start.17) | collective-permute-done | bytes 524320 | tf_op jit(solution)/shard_map/ppermute | solution.py:273
  99.3 9.6 %collective-permute-done.22 = bf16[128,2048]{1,0:T(8,128)(2,1)S(1)} collective-permute-done((bf16[128,2048]{1,0:T(8,128)(2,1)S(1)}, bf16[128,2048]{1,0:T(8,128)(2,1)S(1)}, u32[]{:S(2)}, u32[]{:S(2)}) %collective-permute-start.22) | collective-permute-done | bytes 524320 | tf_op jit(solution)/shard_map/ppermute | solution.py:273
  108.9 3.3 %collective-permute-start.26 = (bf16[4,128,256]{2,1,0:T(8,128)(2,1)S(1)}, bf16[4,128,256]{2,1,0:T(8,128)(2,1)S(1)}, u32[]{:S(2)}, u32[]{:S(2)}) collective-permute-start(bf16[4,128,256]{2,1,0:T(8,128)(2,1)S(1)} %broadcast_select_fusion.2), channel_id=1, source_target_pairs={{8,0},{10,2},{12,4},{14,6},{24,16},{26,18},{28,20},{30,22},{9,1},{... | collective-permute-start | bytes 786440 | tf_op jit(solution)/shard_map/ppermute | solution.py:280
  114.5 2.8 %shard_map.86 = bf16[512,512]{1,0:T(8,128)(2,1)} custom-call(s32[3]{0:T(128)S(1)} %pad_add_fusion.place_ref, bf16[512,2048]{1,0:T(8,128)(2,1)S(1)} %constant_dynamic-update-slice_fusion.6.x_ref, bf16[4096,512]{1,0:T(8,128)(2,1)S(1)} %copy-done, bf16[2,512,512]{2,1,0:T(8,128)(2,1)S(1)} %collective-permute-done.5.refs_1_, ...), custom_call_target="tpu_custom_call" | custom-call | flops 1073741824 | bytes 4718592 | tf_op jit(solution)/shard_map/pallas_call | solution.py:51
  117.9 2.1 shard_map.88
  120.0 2.1 shard_map.89
  128.2 4.2 %collective-permute-done.28.refs_2_ = bf16[128,1024]{1,0:T(8,128)(2,1)} collective-permute-done((bf16[128,1024]{1,0:T(8,128)(2,1)}, bf16[128,1024]{1,0:T(8,128)(2,1)}, u32[]{:S(2)}, u32[]{:S(2)}) %collective-permute-start.28) | collective-permute-done | bytes 262176 | tf_op jit(solution)/shard_map/ppermute | solution.py:270
  132.5 4.4 %collective-permute-start.38 = (bf16[512,512]{1,0:T(8,128)(2,1)}, bf16[512,512]{1,0:T(8,128)(2,1)S(1)}, u32[]{:S(2)}, u32[]{:S(2)}) collective-permute-start(bf16[512,512]{1,0:T(8,128)(2,1)} %copy-done.10), channel_id=1, source_target_pairs={{8,0},{10,2},{12,4},{14,6},{16,8},{18,10},{20,12},{22,14},{24,16},... | collective-permute-start | bytes 1572872 | tf_op jit(solution)/shard_map/ppermute | solution.py:280
  140.9 2.2 %copy-done.1 = bf16[4096,512]{1,0:T(8,128)(2,1)S(1)} copy-done((bf16[4096,512]{1,0:T(8,128)(2,1)S(1)}, bf16[4096,512]{1,0:T(8,128)(2,1)}, u32[]{:S(2)}) %copy-start.1) | copy-done | bytes 4194328
  145.9 3.0 %shard_map.90 = bf16[512,512]{1,0:T(8,128)(2,1)S(1)} custom-call(s32[3]{0:T(128)S(1)} %pad_add_fusion.place_ref, bf16[512,2048]{1,0:T(8,128)(2,1)S(1)} %copy-done.7, bf16[4096,512]{1,0:T(8,128)(2,1)S(1)} %copy-done.1, bf16[2,512,512]{2,1,0:T(8,128)(2,1)S(1)} %copy-done.4, bf16[2,512,512]{2,1,0:T(8,128)(2,1)S(1)} %collective-permute-done.31.refs_2_.refs_3_, ...), custom_call_target="tpu_custom_call" | custom-call | flops 1073741824 | bytes 4718592 | tf_op jit(solution)/shard_map/pallas_call | solution.py:51
  149.0 2.3 %collective-permute-start.37 = (bf16[512,512]{1,0:T(8,128)(2,1)S(1)}, bf16[512,512]{1,0:T(8,128)(2,1)S(1)}, u32[]{:S(2)}, u32[]{:S(2)}) collective-permute-start(bf16[512,512]{1,0:T(8,128)(2,1)S(1)} %shard_map.90), channel_id=1, source_target_pairs={{0,16},{2,18},{4,20},{6,22},{8,24},{10,26},{12,28},{14,30},{16,0},... | collective-permute-start | bytes 1572872 | tf_op jit(solution)/shard_map/ppermute | solution.py:277
  152.8 2.1 %shard_map.92 = f32[512,512]{1,0:T(8,128)S(1)} custom-call(s32[3]{0:T(128)S(1)} %pad_add_fusion.place_ref, bf16[512,2048]{1,0:T(8,128)(2,1)S(1)} %pad_maximum_fusion.1.x_ref, bf16[4096,512]{1,0:T(8,128)(2,1)S(1)} %copy-done.2, bf16[2,512,512]{2,1,0:T(8,128)(2,1)S(1)} %collective-permute-done.5.refs_1_, ...), custom_call_target="tpu_custom_call" | custom-call | flops 1073741824 | bytes 4718592 | tf_op jit(solution)/shard_map/pallas_call | solution.py:51
  154.9 9.2 %shard_map.91.prob_ref = bf16[8,1024,512]{2,1,0:T(8,128)(2,1)S(1)} custom-call(s32[3]{0:T(128)S(1)} %pad_add_fusion.place_ref, bf16[4,128,256]{2,1,0:T(8,128)(2,1)S(1)} %pad_maximum_fusion.13.k_ref.v_ref, bf16[4,128,256]{2,1,0:T(8,128)(2,1)S(1)} %broadcast_select_fusion.1.kp_ref.vp_ref, bf16[128,1024]{1,0:T(8,128)(2,1)S(1)} %copy-done.8, ...), custom_call_target="tpu_custom_call" | custom-call | flops 1073741824 | bytes 8388608 | tf_op jit(solution)/shard_map/pallas_call | solution.py:115
  164.2 8.4 %shard_map.93 = (bf16[4,128,512]{2,1,0:T(8,128)(2,1)S(1)}, f32[1024,128]{1,0:T(8,128)S(1)}, f32[1024,128]{1,0:T(8,128)S(1)}) custom-call(s32[3]{0:T(128)S(1)} %pad_add_fusion.place_ref, bf16[8,1024,512]{2,1,0:T(8,128)(2,1)S(1)} %shard_map.91.prob_ref, bf16[4,128,256]{2,1,0:T(8,128)(2,1)S(1)} %pad_maximum_fusion.13.k_ref.v_ref, ...), custom_call_target="tpu_custom_call" | custom-call | flops 2147483648 | bytes 4194304 | tf_op jit(solution)/shard_map/pallas_call | solution.py:214
  174.9 2.1 %shard_map.94 = f32[512,512]{1,0:T(8,128)S(1)} custom-call(s32[3]{0:T(128)S(1)} %pad_add_fusion.place_ref, bf16[512,2048]{1,0:T(8,128)(2,1)S(1)} %pad_maximum_fusion.1.x_ref, bf16[4096,512]{1,0:T(8,128)(2,1)S(1)} %copy-done.2, bf16[2,512,512]{2,1,0:T(8,128)(2,1)S(1)} %copy-done.5, bf16[2,512,512]{2,1,0:T(8,128)(2,1)S(1)} %collective-permute-done.31.refs_2_.refs_3_, ...), custom_call_target="tpu_custom_call" | custom-call | flops 1073741824 | bytes 4718592 | tf_op jit(solution)/shard_map/pallas_call | solution.py:51
  177.6 8.3 %shard_map.95 = (bf16[4,128,512]{2,1,0:T(8,128)(2,1)S(1)}, f32[1024,128]{1,0:T(8,128)S(1)}, f32[1024,128]{1,0:T(8,128)S(1)}) custom-call(s32[3]{0:T(128)S(1)} %pad_add_fusion.place_ref, bf16[8,1024,512]{2,1,0:T(8,128)(2,1)S(1)} %shard_map.91.prob_ref, bf16[4,128,256]{2,1,0:T(8,128)(2,1)S(1)} %pad_maximum_fusion.13.k_ref.v_ref, ...), custom_call_target="tpu_custom_call" | custom-call | flops 2147483648 | bytes 4194304 | tf_op jit(solution)/shard_map/pallas_call | solution.py:214
  189.8 2.5 %collective-permute-done.40 = bf16[128,512]{1,0:T(8,128)(2,1)S(1)} collective-permute-done((bf16[128,512]{1,0:T(8,128)(2,1)S(1)}, bf16[128,512]{1,0:T(8,128)(2,1)S(1)}, u32[]{:S(2)}, u32[]{:S(2)}) %collective-permute-start.40) | collective-permute-done | bytes 131104 | tf_op jit(solution)/shard_map/ppermute | solution.py:270
  192.3 3.6 %collective-permute-done.42 = bf16[512,256]{1,0:T(8,128)(2,1)S(1)} collective-permute-done((bf16[512,256]{1,0:T(8,128)(2,1)S(1)}, bf16[512,256]{1,0:T(8,128)(2,1)S(1)}, u32[]{:S(2)}, u32[]{:S(2)}) %collective-permute-start.42) | collective-permute-done | bytes 262176 | tf_op jit(solution)/shard_map/ppermute | solution.py:280
  196.0 2.4 %collective-permute-start.43 = (bf16[128,256]{1,0:T(8,128)(2,1)S(1)}, bf16[128,256]{1,0:T(8,128)(2,1)S(1)}, u32[]{:S(2)}, u32[]{:S(2)}) collective-permute-start(bf16[128,256]{1,0:T(8,128)(2,1)S(1)} %get-tuple-element.124), channel_id=1, source_target_pairs={{8,24},{10,26},{12,28},{14,30},{9,25},{11,27},{13,29},{15,31}} | collective-permute-start | bytes 196616 | tf_op jit(solution)/shard_map/ppermute | solution.py:557
  198.5 2.2 %collective-permute-start.45 = (bf16[128,256]{1,0:T(8,128)(2,1)S(1)}, bf16[128,256]{1,0:T(8,128)(2,1)S(1)}, u32[]{:S(2)}, u32[]{:S(2)}) collective-permute-start(bf16[128,256]{1,0:T(8,128)(2,1)S(1)} %get-tuple-element.123), channel_id=1, source_target_pairs={{8,26},{10,24},{12,30},{14,28},{9,27},{11,25},{13,31},{15,29}} | collective-permute-start | bytes 196616 | tf_op jit(solution)/shard_map/ppermute | solution.py:557
  (222 shorter events, 70.8 us)
Async XLA Ops:
  4.8 10.1 %collective-permute-start.5 = (bf16[2,512,512]{2,1,0:T(8,128)(2,1)}, bf16[2,512,512]{2,1,0:T(8,128)(2,1)S(1)}, u32[]{:S(2)}, u32[]{:S(2)}) collective-permute-start(bf16[2,512,512]{2,1,0:T(8,128)(2,1)} %pad_maximum_fusion.2), channel_id=1, source_target_pairs={{0,2},{2,0},{4,6},{6,4},{8,10},{10,8},{12,14},{14,12},{16,18},{18,... | collective-permute-start | bytes 3145736 | tf_op jit(solution)/shard_map/ppermute | solution.py:270
  9.0 115.5 %collective-permute-start.27 = (bf16[128,1024]{1,0:T(8,128)(2,1)}, bf16[128,1024]{1,0:T(8,128)(2,1)}, u32[]{:S(2)}, u32[]{:S(2)}) collective-permute-start(bf16[128,1024]{1,0:T(8,128)(2,1)} %get-tuple-element.111), channel_id=1, source_target_pairs={{0,2},{2,0},{4,6},{6,4},{8,10},{10,8},{12,14},{14,12},{16,18},{18,... | collective-permute-start | bytes 786440 | tf_op jit(solution)/shard_map/ppermute | solution.py:270
  17.1 23.2 %collective-permute-start.6 = (bf16[2,512,512]{2,1,0:T(8,128)(2,1)}, bf16[2,512,512]{2,1,0:T(8,128)(2,1)S(1)}, u32[]{:S(2)}, u32[]{:S(2)}) collective-permute-start(bf16[2,512,512]{2,1,0:T(8,128)(2,1)} %pad_maximum_fusion.3), channel_id=1, source_target_pairs={{0,4},{2,6},{4,0},{6,2},{8,12},{10,14},{12,8},{14,10},{16,20},{18,... | collective-permute-start | bytes 3145736 | tf_op jit(solution)/shard_map/ppermute | solution.py:270
  21.6 13.0 %collective-permute-start.3 = (bf16[64,2048]{1,0:T(8,128)(2,1)S(1)}, bf16[64,2048]{1,0:T(8,128)(2,1)}, u32[]{:S(2)}, u32[]{:S(2)}) collective-permute-start(bf16[64,2048]{1,0:T(8,128)(2,1)S(1)} %get-tuple-element.107), channel_id=1, source_target_pairs={{0,8},{2,10},{4,12},{6,14},{8,16},{10,18},{12,20},{14,22},{16,24},... | collective-permute-start | bytes 786440 | tf_op jit(solution)/shard_map/ppermute | solution.py:277
  34.5 10.9 %collective-permute-start.4 = (bf16[64,2048]{1,0:T(8,128)(2,1)}, bf16[64,2048]{1,0:T(8,128)(2,1)S(1)}, u32[]{:S(2)}, u32[]{:S(2)}) collective-permute-start(bf16[64,2048]{1,0:T(8,128)(2,1)} %get-tuple-element.50), channel_id=1, source_target_pairs={{0,16},{2,18},{4,20},{6,22},{8,24},{10,26},{12,28},{14,30},{16,0},... | collective-permute-start | bytes 786440 | tf_op jit(solution)/shard_map/ppermute | solution.py:277
  41.6 21.3 %collective-permute-start.13 = (bf16[128,256]{1,0:T(8,128)(2,1)}, bf16[128,256]{1,0:T(8,128)(2,1)S(1)}, u32[]{:S(2)}, u32[]{:S(2)}) collective-permute-start(bf16[128,256]{1,0:T(8,128)(2,1)} %pad_maximum_fusion.15), channel_id=1, source_target_pairs={{0,4},{2,6},{4,0},{6,2},{8,12},{10,14},{12,8},{14,10},{16,20},{18,... | collective-permute-start | bytes 196616 | tf_op jit(solution)/shard_map/ppermute | solution.py:270
  45.5 17.6 %collective-permute-start.14 = (bf16[128,256]{1,0:T(8,128)(2,1)}, bf16[128,256]{1,0:T(8,128)(2,1)S(1)}, u32[]{:S(2)}, u32[]{:S(2)}) collective-permute-start(bf16[128,256]{1,0:T(8,128)(2,1)} %pad_maximum_fusion.16), channel_id=1, source_target_pairs={{0,6},{2,4},{4,2},{6,0},{8,14},{10,12},{12,10},{14,8},{16,22},{18,... | collective-permute-start | bytes 196616 | tf_op jit(solution)/shard_map/ppermute | solution.py:270
  48.2 10.4 %collective-permute-start.9 = (bf16[128,2048]{1,0:T(8,128)(2,1)S(1)}, bf16[128,2048]{1,0:T(8,128)(2,1)S(1)}, u32[]{:S(2)}, u32[]{:S(2)}) collective-permute-start(bf16[128,2048]{1,0:T(8,128)(2,1)S(1)} %pad_maximum_fusion.10), channel_id=1, source_target_pairs={{0,1},{1,0},{2,3},{3,2},{4,5},{5,4},{6,7},{7,6},{8,9},{9,8},{10,11... | collective-permute-start | bytes 1572872 | tf_op jit(solution)/shard_map/ppermute | solution.py:273
  49.5 14.3 %collective-permute-start.10 = (bf16[128,2048]{1,0:T(8,128)(2,1)S(1)}, bf16[128,2048]{1,0:T(8,128)(2,1)S(1)}, u32[]{:S(2)}, u32[]{:S(2)}) collective-permute-start(bf16[128,2048]{1,0:T(8,128)(2,1)S(1)} %constant_dynamic-update-slice_fusion), channel_id=1, source_target_pairs={{0,4},{2,6},{4,0},{6,2},{8,12},{10,14},{12,8},{14,10},{16,20},{18,... | collective-permute-start | bytes 1572872 | tf_op jit(solution)/shard_map/ppermute | solution.py:270
  63.0 16.8 %collective-permute-start.30 = (bf16[2,512,512]{2,1,0:T(8,128)(2,1)S(1)}, bf16[2,512,512]{2,1,0:T(8,128)(2,1)S(1)}, u32[]{:S(2)}, u32[]{:S(2)}) collective-permute-start(bf16[2,512,512]{2,1,0:T(8,128)(2,1)S(1)} %copy-done.27), channel_id=1, source_target_pairs={{0,2},{2,0},{4,6},{6,4},{8,10},{10,8},{12,14},{14,12},{16,18},{18,... | collective-permute-start | bytes 3145736 | tf_op jit(solution)/shard_map/ppermute | solution.py:270
  63.8 13.3 %collective-permute-start.16 = (bf16[256,2048]{1,0:T(8,128)(2,1)S(1)}, bf16[256,2048]{1,0:T(8,128)(2,1)S(1)}, u32[]{:S(2)}, u32[]{:S(2)}) collective-permute-start(bf16[256,2048]{1,0:T(8,128)(2,1)S(1)} %pad_maximum_fusion.4), channel_id=1, source_target_pairs={{0,2},{2,0},{4,6},{6,4},{8,10},{10,8},{12,14},{14,12},{16,18},{18,... | collective-permute-start | bytes 3145736 | tf_op jit(solution)/shard_map/ppermute | solution.py:270
  64.2 10.6 %collective-permute-start.15 = (bf16[4,128,256]{2,1,0:T(8,128)(2,1)S(1)}, bf16[4,128,256]{2,1,0:T(8,128)(2,1)S(1)}, u32[]{:S(2)}, u32[]{:S(2)}) collective-permute-start(bf16[4,128,256]{2,1,0:T(8,128)(2,1)S(1)} %pad_maximum_fusion.13.k_ref.v_ref), channel_id=1, source_target_pairs={{24,8},{26,10},{28,12},{30,14},{25,9},{27,11},{29,13},{31,15}} | collective-permute-start | bytes 786440 | tf_op jit(solution)/shard_map/ppermute | solution.py:280
  65.5 10.3 %collective-permute-start.11 = (bf16[64,2048]{1,0:T(8,128)(2,1)S(1)}, bf16[64,2048]{1,0:T(8,128)(2,1)S(1)}, u32[]{:S(2)}, u32[]{:S(2)}) collective-permute-start(bf16[64,2048]{1,0:T(8,128)(2,1)S(1)} %collective-permute-done.4), channel_id=1, source_target_pairs={{0,4},{2,6},{4,0},{6,2},{8,12},{10,14},{12,8},{14,10},{16,20},{18,... | collective-permute-start | bytes 786440 | tf_op jit(solution)/shard_map/ppermute | solution.py:270
  74.7 20.3 %collective-permute-start.23 = (bf16[256,2048]{1,0:T(8,128)(2,1)S(1)}, bf16[256,2048]{1,0:T(8,128)(2,1)S(1)}, u32[]{:S(2)}, u32[]{:S(2)}) collective-permute-start(bf16[256,2048]{1,0:T(8,128)(2,1)S(1)} %bitcast.59), channel_id=1, source_target_pairs={{0,2},{2,0},{4,6},{6,4},{8,10},{10,8},{12,14},{14,12},{16,18},{18,... | collective-permute-start | bytes 3145736 | tf_op jit(solution)/shard_map/ppermute | solution.py:270
  79.4 13.3 %collective-permute-start.17 = (bf16[128,2048]{1,0:T(8,128)(2,1)S(1)}, bf16[128,2048]{1,0:T(8,128)(2,1)S(1)}, u32[]{:S(2)}, u32[]{:S(2)}) collective-permute-start(bf16[128,2048]{1,0:T(8,128)(2,1)S(1)} %pad_maximum_fusion.11), channel_id=1, source_target_pairs={{0,1},{1,0},{2,3},{3,2},{4,5},{5,4},{6,7},{7,6},{8,9},{9,8},{10,11... | collective-permute-start | bytes 1572872 | tf_op jit(solution)/shard_map/ppermute | solution.py:273
  79.9 13.0 %collective-permute-start.18 = (bf16[512,512]{1,0:T(8,128)(2,1)S(1)}, bf16[512,512]{1,0:T(8,128)(2,1)S(1)}, u32[]{:S(2)}, u32[]{:S(2)}) collective-permute-start(bf16[512,512]{1,0:T(8,128)(2,1)S(1)} %shard_map.85), channel_id=1, source_target_pairs={{0,8},{2,10},{4,12},{6,14},{8,16},{10,18},{12,20},{14,22},{16,24},... | collective-permute-start | bytes 1572872 | tf_op jit(solution)/shard_map/ppermute | solution.py:277
  83.7 34.2 %collective-permute-start.31 = (bf16[2,512,512]{2,1,0:T(8,128)(2,1)S(1)}, bf16[2,512,512]{2,1,0:T(8,128)(2,1)S(1)}, u32[]{:S(2)}, u32[]{:S(2)}) collective-permute-start(bf16[2,512,512]{2,1,0:T(8,128)(2,1)S(1)} %pad_maximum_fusion.9), channel_id=1, source_target_pairs={{0,4},{2,6},{4,0},{6,2},{8,12},{10,14},{12,8},{14,10},{16,20},{18,... | collective-permute-start | bytes 3145736 | tf_op jit(solution)/shard_map/ppermute | solution.py:270
  93.6 20.8 %collective-permute-start.20 = (bf16[256,2048]{1,0:T(8,128)(2,1)S(1)}, bf16[256,2048]{1,0:T(8,128)(2,1)S(1)}, u32[]{:S(2)}, u32[]{:S(2)}) collective-permute-start(bf16[256,2048]{1,0:T(8,128)(2,1)S(1)} %pad_maximum_fusion.5), channel_id=1, source_target_pairs={{0,2},{2,0},{4,6},{6,4},{8,10},{10,8},{12,14},{14,12},{16,18},{18,... | collective-permute-start | bytes 3145736 | tf_op jit(solution)/shard_map/ppermute | solution.py:270
  95.3 13.6 %collective-permute-start.22 = (bf16[128,2048]{1,0:T(8,128)(2,1)S(1)}, bf16[128,2048]{1,0:T(8,128)(2,1)S(1)}, u32[]{:S(2)}, u32[]{:S(2)}) collective-permute-start(bf16[128,2048]{1,0:T(8,128)(2,1)S(1)} %pad_maximum_fusion.12), channel_id=1, source_target_pairs={{0,1},{1,0},{2,3},{3,2},{4,5},{5,4},{6,7},{7,6},{8,9},{9,8},{10,11... | collective-permute-start | bytes 1572872 | tf_op jit(solution)/shard_map/ppermute | solution.py:273
  98.6 14.8 %collective-permute-start.24 = (bf16[512,512]{1,0:T(8,128)(2,1)S(1)}, bf16[512,512]{1,0:T(8,128)(2,1)S(1)}, u32[]{:S(2)}, u32[]{:S(2)}) collective-permute-start(bf16[512,512]{1,0:T(8,128)(2,1)S(1)} %shard_map.87), channel_id=1, source_target_pairs={{0,24},{2,26},{4,28},{6,30},{8,0},{10,2},{12,4},{14,6},{16,8},{18,... | collective-permute-start | bytes 1572872 | tf_op jit(solution)/shard_map/ppermute | solution.py:277
  108.9 16.3 %collective-permute-start.26 = (bf16[4,128,256]{2,1,0:T(8,128)(2,1)S(1)}, bf16[4,128,256]{2,1,0:T(8,128)(2,1)S(1)}, u32[]{:S(2)}, u32[]{:S(2)}) collective-permute-start(bf16[4,128,256]{2,1,0:T(8,128)(2,1)S(1)} %broadcast_select_fusion.2), channel_id=1, source_target_pairs={{8,0},{10,2},{12,4},{14,6},{24,16},{26,18},{28,20},{30,22},{9,1},{... | collective-permute-start | bytes 786440 | tf_op jit(solution)/shard_map/ppermute | solution.py:280
  113.3 27.5 %collective-permute-start.25 = (bf16[256,2048]{1,0:T(8,128)(2,1)}, bf16[256,2048]{1,0:T(8,128)(2,1)}, u32[]{:S(2)}, u32[]{:S(2)}) collective-permute-start(bf16[256,2048]{1,0:T(8,128)(2,1)} %pad_maximum_fusion.6), channel_id=1, source_target_pairs={{0,2},{2,0},{4,6},{6,4},{8,10},{10,8},{12,14},{14,12},{16,18},{18,... | collective-permute-start | bytes 3145736 | tf_op jit(solution)/shard_map/ppermute | solution.py:270
  117.4 23.5 %collective-permute-start.21 = (bf16[512,512]{1,0:T(8,128)(2,1)}, bf16[512,512]{1,0:T(8,128)(2,1)}, u32[]{:S(2)}, u32[]{:S(2)}) collective-permute-start(bf16[512,512]{1,0:T(8,128)(2,1)} %shard_map.86), channel_id=1, source_target_pairs={{0,16},{2,18},{4,20},{6,22},{8,24},{10,26},{12,28},{14,30},{16,0},... | collective-permute-start | bytes 1572872 | tf_op jit(solution)/shard_map/ppermute | solution.py:277
  123.2 17.7 %collective-permute-start.32 = (bf16[512,512]{1,0:T(8,128)(2,1)}, bf16[512,512]{1,0:T(8,128)(2,1)}, u32[]{:S(2)}, u32[]{:S(2)}) collective-permute-start(bf16[512,512]{1,0:T(8,128)(2,1)} %broadcast_select_fusion), channel_id=1, source_target_pairs={{0,8},{2,10},{4,12},{6,14},{24,16},{26,18},{28,20},{30,22},{1,9},{... | collective-permute-start | bytes 1572872 | tf_op jit(solution)/shard_map/ppermute | solution.py:280
  126.0 12.8 %collective-permute-start.29 = (bf16[128,1024]{1,0:T(8,128)(2,1)}, bf16[128,1024]{1,0:T(8,128)(2,1)}, u32[]{:S(2)}, u32[]{:S(2)}) collective-permute-start(bf16[128,1024]{1,0:T(8,128)(2,1)} %get-tuple-element.112), channel_id=1, source_target_pairs={{0,6},{2,4},{4,2},{6,0},{8,14},{10,12},{12,10},{14,8},{16,22},{18,... | collective-permute-start | bytes 786440 | tf_op jit(solution)/shard_map/ppermute | solution.py:270
  132.5 44.6 %collective-permute-start.38 = (bf16[512,512]{1,0:T(8,128)(2,1)}, bf16[512,512]{1,0:T(8,128)(2,1)S(1)}, u32[]{:S(2)}, u32[]{:S(2)}) collective-permute-start(bf16[512,512]{1,0:T(8,128)(2,1)} %copy-done.10), channel_id=1, source_target_pairs={{8,0},{10,2},{12,4},{14,6},{16,8},{18,10},{20,12},{22,14},{24,16},... | collective-permute-start | bytes 1572872 | tf_op jit(solution)/shard_map/ppermute | solution.py:280
  138.8 38.8 %collective-permute-start.36 = (bf16[512,512]{1,0:T(8,128)(2,1)}, bf16[512,512]{1,0:T(8,128)(2,1)S(1)}, u32[]{:S(2)}, u32[]{:S(2)}) collective-permute-start(bf16[512,512]{1,0:T(8,128)(2,1)} %copy-done.9), channel_id=1, source_target_pairs={{0,8},{2,10},{4,12},{6,14},{8,16},{10,18},{12,20},{14,22},{16,24},... | collective-permute-start | bytes 1572872 | tf_op jit(solution)/shard_map/ppermute | solution.py:280
  149.0 28.6 %collective-permute-start.37 = (bf16[512,512]{1,0:T(8,128)(2,1)S(1)}, bf16[512,512]{1,0:T(8,128)(2,1)S(1)}, u32[]{:S(2)}, u32[]{:S(2)}) collective-permute-start(bf16[512,512]{1,0:T(8,128)(2,1)S(1)} %shard_map.90), channel_id=1, source_target_pairs={{0,16},{2,18},{4,20},{6,22},{8,24},{10,26},{12,28},{14,30},{16,0},... | collective-permute-start | bytes 1572872 | tf_op jit(solution)/shard_map/ppermute | solution.py:277
  172.6 14.6 %collective-permute-start.33 = (bf16[128,512]{1,0:T(8,128)(2,1)S(1)}, bf16[128,512]{1,0:T(8,128)(2,1)S(1)}, u32[]{:S(2)}, u32[]{:S(2)}) collective-permute-start(bf16[128,512]{1,0:T(8,128)(2,1)S(1)} %get-tuple-element.119), channel_id=1, source_target_pairs={{0,2},{2,0},{4,6},{6,4},{8,10},{10,8},{12,14},{14,12},{16,18},{18,... | collective-permute-start | bytes 393224 | tf_op jit(solution)/shard_map/ppermute | solution.py:270
  173.7 13.6 %collective-permute-start.34 = (bf16[128,512]{1,0:T(8,128)(2,1)S(1)}, bf16[128,512]{1,0:T(8,128)(2,1)S(1)}, u32[]{:S(2)}, u32[]{:S(2)}) collective-permute-start(bf16[128,512]{1,0:T(8,128)(2,1)S(1)} %get-tuple-element.118), channel_id=1, source_target_pairs={{0,4},{2,6},{4,0},{6,2},{8,12},{10,14},{12,8},{14,10},{16,20},{18,... | collective-permute-start | bytes 393224 | tf_op jit(solution)/shard_map/ppermute | solution.py:270
  177.1 10.2 %collective-permute-start.35 = (bf16[128,512]{1,0:T(8,128)(2,1)S(1)}, bf16[128,512]{1,0:T(8,128)(2,1)S(1)}, u32[]{:S(2)}, u32[]{:S(2)}) collective-permute-start(bf16[128,512]{1,0:T(8,128)(2,1)S(1)} %get-tuple-element.117), channel_id=1, source_target_pairs={{0,6},{2,4},{4,2},{6,0},{8,14},{10,12},{12,10},{14,8},{16,22},{18,... | collective-permute-start | bytes 393224 | tf_op jit(solution)/shard_map/ppermute | solution.py:270
  188.8 15.5 %collective-permute-start.41 = (bf16[128,512]{1,0:T(8,128)(2,1)S(1)}, bf16[128,512]{1,0:T(8,128)(2,1)S(1)}, u32[]{:S(2)}, u32[]{:S(2)}) collective-permute-start(bf16[128,512]{1,0:T(8,128)(2,1)S(1)} %get-tuple-element.114), channel_id=1, source_target_pairs={{0,6},{2,4},{4,2},{6,0},{8,14},{10,12},{12,10},{14,8},{16,22},{18,... | collective-permute-start | bytes 393224 | tf_op jit(solution)/shard_map/ppermute | solution.py:270
  (55 other events, 527.4 us)
